TPU v7x, 128 devices: a whole 4x4x4 slice. The times are simulated.
128 devices in a mesh: lon: 16 (over x, y), lat: 8 (over z, core).
Axes of the slice: x: 4, y: 4, z: 4, core: 2. Of those that a mesh axis runs over, the one named last changes fastest.
Arguments:
- lam_tracer: float32 [2, 50, 256, 2048], P(None, None, 'lat', 'lon'), may hold values from -6 to 6
- tracer: float32 [2, 50, 256, 2048], P(None, None, 'lat', 'lon'), may hold values from -6 to 6
- velocity: float32 [2, 50, 256, 2048], P(None, None, 'lat', 'lon'), may hold values from -4 to 4
- diffusivity: float32 [50, 256, 2048], P(None, 'lat', 'lon'), may hold values from 0.5 to 20
- lam_surface: float32 [256, 2048], P('lat', 'lon'), may hold values from -6 to 6
- sea_depth: float32 [256, 2048], P('lat', 'lon'), may hold values from 0.2 to 5
- levels: int32 [256, 2048], P('lat', 'lon'), may hold values from 0 to 50, as said below
Outputs:
- adjoint_tracer: float32 [2, 50, 256, 2048], P(None, None, 'lat', 'lon')
- adjoint_velocity: float32 [2, 50, 256, 2048], P(None, None, 'lat', 'lon')
- solution: float32 [256, 2048], P('lat', 'lon')
Inputs may be any that keep to these rules, and one draw needn't show every extreme that they name: A sea column is wet in its top levels; land columns are 0. Land comes in whole rows of a tile of 128 columns, far more often in some longitude bands than in others.
All inputs are finite; a program needn't handle non-finite values.
Results may differ from a plain program's by a relative error of at most 0.0001.
Values sent between devices are 32-bit elements; how exact they have to be, the bound alone decides.
No kernel may reach another device: no remote copies, remote signals or barrier semaphores. Data moves between devices by JAX's collectives and lax.ppermute only.
A program may use at most 64 MiB of HBM per device.

v0:
```python
import math

import jax
import jax.numpy as jnp
from jax import lax
from jax.sharding import PartitionSpec as P

LEVELS = 50
ITERS = 4


SURFACE_DAMPING = 0.05
COURANT = 0.25
GAIN_HEAT = 0.7
GAIN_SALT = -0.5


def with_halo(block, sides, width, periodic):
    for axis, dim in sides:
        count = lax.axis_size(axis)
        forward = [(i, i + 1) for i in range(count - 1)]
        if periodic:
            forward.append((count - 1, 0))
        backward = [(target, source) for source, target in forward]
        low = lax.ppermute(
            lax.slice_in_dim(block, block.shape[dim] - width, None, axis=dim), axis, forward
        )
        high = lax.ppermute(lax.slice_in_dim(block, 0, width, axis=dim), axis, backward)
        block = jnp.concatenate([low, block, high], axis=dim)
    return block


def column_solve(right_side, coupling):
    level_count = coupling.shape[0]
    ratios = []
    values = []
    ratio_prev = jnp.zeros_like(coupling[0])
    value_prev = jnp.zeros_like(right_side[:, 0])
    for level_idx in range(level_count):
        above_coef = coupling[level_idx]
        if level_idx > 0:
            below_coef = coupling[level_idx - 1]
        else:
            below_coef = jnp.zeros_like(above_coef)
        denominator = 1.0 + below_coef + above_coef + below_coef * ratio_prev
        ratio_prev = -above_coef / denominator
        value_prev = (right_side[:, level_idx] + below_coef * value_prev) / denominator
        ratios.append(ratio_prev)
        values.append(value_prev)
    results = [None] * level_count
    following = jnp.zeros_like(value_prev)
    for level_idx in range(level_count - 1, -1, -1):
        following = values[level_idx] - ratios[level_idx] * following
        results[level_idx] = following
    return jnp.stack(results, axis=1)


def surface_operator(
    field,
    sea_surface,
    face_east,
    face_west,
    face_north,
    face_south,
    east_field,
    west_field,
    north_field,
    south_field,
):
    return (
        field * (1.0 - sea_surface)
        + SURFACE_DAMPING * sea_surface * field
        + face_east * (field - east_field)
        + face_west * (field - west_field)
        + face_north * (field - north_field)
        + face_south * (field - south_field)
    )


def solve_blocks(pieces):
    packed, level_pack = pieces
    level_count = packed.shape[1]

    def one_block(block):
        block_fields, block_levels = block
        level_ids = jnp.arange(level_count, dtype=jnp.int32)[:, None, None]
        wet_cells = (level_ids < block_levels[0]).astype(jnp.float32)
        wet_below = jnp.concatenate([wet_cells[1:], jnp.zeros_like(wet_cells[:1])], axis=0)
        coupling = block_fields[2] * wet_below
        right_side = block_fields[:2]

        def solve_now(operands):
            return column_solve(operands[0], operands[1])

        def skip_block(operands):
            return jnp.zeros_like(operands[0])

        return lax.cond(jnp.max(block_levels) > 0, solve_now, skip_block, (right_side, coupling))

    solved = lax.map(one_block, (jnp.moveaxis(packed, 2, 0), jnp.moveaxis(level_pack, 2, 0)))
    return jnp.moveaxis(solved, 0, 2)


def residual_norm(residual):
    return lax.psum(jnp.sum(residual * residual), ("lon", "lat"))


def per_device(lam_tracer, tracer, velocity, diffusivity, lam_surface, sea_depth, levels):
    tile_rows, tile_cols = levels.shape
    level_ids = jnp.arange(LEVELS, dtype=jnp.int32)[:, None, None]
    wet_cells = (level_ids < levels[None]).astype(jnp.float32)
    sea_surface = (levels > 0).astype(jnp.float32)
    state_pack = jnp.concatenate([tracer, jnp.stack([sea_depth, sea_surface])[:, None]], axis=1)
    padded = with_halo(state_pack, (("lon", 3), ("lat", 2)), 1, True)
    row_ids = jnp.arange(tile_rows + 2, dtype=jnp.int32)
    lat_index = lax.axis_index("lat")
    last_index = lax.axis_size("lat") - 1
    pole_rows = (row_ids == 0) & (lat_index == 0) | (row_ids == tile_rows + 1) & (
        lat_index == last_index
    )
    pole_keep = jnp.where(pole_rows, 0.0, 1.0).astype(jnp.float32)
    padded = padded * pole_keep[:, None]
    group_count = lax.axis_size("lon")
    piece_rows = tile_rows // group_count
    right_side = wet_cells[None] * lam_tracer
    packed = jnp.concatenate([right_side, diffusivity[None]], axis=0).reshape(
        3, LEVELS, group_count, piece_rows, tile_cols
    )
    level_pack = levels.reshape(1, 1, group_count, piece_rows, tile_cols)
    solved = solve_blocks((packed, level_pack))
    mixed = solved.reshape(2, LEVELS, tile_rows, tile_cols)
    forcing = sea_surface * (
        lam_surface
        + (GAIN_HEAT * jnp.sum(mixed[0], axis=0) + GAIN_SALT * jnp.sum(mixed[1], axis=0))
        / math.sqrt(LEVELS)
    )
    height = padded[0, LEVELS]
    sea_pad = padded[1, LEVELS]
    face_east = 0.5 * (sea_depth + height[1:-1, 2:]) * sea_surface * sea_pad[1:-1, 2:]
    face_west = 0.5 * (sea_depth + height[1:-1, :-2]) * sea_surface * sea_pad[1:-1, :-2]
    face_north = 0.5 * (sea_depth + height[2:, 1:-1]) * sea_surface * sea_pad[2:, 1:-1]
    face_south = 0.5 * (sea_depth + height[:-2, 1:-1]) * sea_surface * sea_pad[:-2, 1:-1]
    solution = jnp.zeros_like(forcing)
    residual = forcing
    direction = forcing
    norm_now = residual_norm(residual)
    for step_idx in range(ITERS):
        operate_extended = with_halo(direction, (("lon", 1), ("lat", 0)), 1, True)
        image_field = surface_operator(
            direction,
            sea_surface,
            face_east,
            face_west,
            face_north,
            face_south,
            operate_extended[1:-1, 2:],
            operate_extended[1:-1, :-2],
            operate_extended[2:, 1:-1],
            operate_extended[:-2, 1:-1],
        )
        step_size = norm_now / lax.psum(jnp.sum(direction * image_field), ("lon", "lat"))
        solution = solution + step_size * direction
        residual = residual - step_size * image_field
        norm_next = residual_norm(residual)
        direction = residual + norm_next / norm_now * direction
        norm_now = norm_next
    tracer_gains = jnp.array([GAIN_HEAT, GAIN_SALT], dtype=jnp.float32)[:, None, None, None]
    adjoint = mixed + tracer_gains * wet_cells[None] * solution[None, None]
    zonal = velocity[0]
    meridional = velocity[1]

    def zonal_sweep(field):
        flux_field = zonal * field
        extended = with_halo(flux_field, (("lon", 3),), 1, True)
        return field + COURANT * wet_cells * (extended[..., 2:] - extended[..., :-2])

    adjoint = zonal_sweep(adjoint)

    def meridional_sweep(field):
        flux_field = meridional * field
        extended = with_halo(flux_field, (("lat", 2),), 1, False)
        return field + COURANT * wet_cells * (extended[:, :, 2:] - extended[:, :, :-2])

    adjoint = meridional_sweep(adjoint)
    adjoint = meridional_sweep(adjoint)
    adjoint = zonal_sweep(adjoint)
    tracer_pad = padded[:, :LEVELS]
    lam_zonal = (
        -COURANT
        * wet_cells
        * (
            adjoint[0] * (tracer_pad[0, :, 1:-1, 2:] - tracer_pad[0, :, 1:-1, :-2])
            + adjoint[1] * (tracer_pad[1, :, 1:-1, 2:] - tracer_pad[1, :, 1:-1, :-2])
        )
    )
    lam_meridional = (
        -COURANT
        * wet_cells
        * (
            adjoint[0] * (tracer_pad[0, :, 2:, 1:-1] - tracer_pad[0, :, :-2, 1:-1])
            + adjoint[1] * (tracer_pad[1, :, 2:, 1:-1] - tracer_pad[1, :, :-2, 1:-1])
        )
    )
    return (adjoint, jnp.stack([lam_zonal, lam_meridional]), solution)


def solution(mesh):
    in_specs = (
        P(None, None, "lat", "lon"),
        P(None, None, "lat", "lon"),
        P(None, None, "lat", "lon"),
        P(None, "lat", "lon"),
        P("lat", "lon"),
        P("lat", "lon"),
        P("lat", "lon"),
    )
    out_specs = (P(None, None, "lat", "lon"), P(None, None, "lat", "lon"), P("lat", "lon"))
    return jax.shard_map(
        per_device, mesh=mesh, in_specs=in_specs, out_specs=out_specs, check_vma=False
    )
```

profile of v0, /device:TPU:1, one launch (start us, length us, event | category | flops | bytes accessed | tf_op | source)
XLA Modules:
  0.0 1166.9 jit_solution(5560915899400672378)
XLA Ops:
  1.5 2.0 broadcast_multiply_fusion.3
  3.5 2.6 copy_bitcast_fusion
  6.1 110.6 %while.10 = (s32[]{:T(128)}, f32[16,2,50,2,128]{4,3,1,2,0:T(2,128)S(1)}, s32[16,1,1,2,128]{4,3,2,1,0:T(2,128)S(1)}, f32[16,3,50,2,128]{4,3,2,1,0:T(2,128)}, s32[]{:T(128)}, /*index=5*/s32[]{:T(128)}) while((s32[]{:T(128)}, f32[16,2,50,2,128]{4,3,1,2,0:T(2,128)S(1)}, s32[16,1,1,2,128]{4,3,2,1,0:T(2,128)S(1)}, f32[16,3,50,2,128]{4,3,2,1,0:T(2,128)}, ...), condition=%wide.region_4.5_spmd, body=%wide.region_0.4_spmd.sunk | while | flops 417795 | bytes 1998999 | solution.py:100
  22.1 32.5 %conditional.2 = (f32[1,2,50,2,128]{4,3,1,2,0:T(2,128)}) conditional(s32[]{:T(128)} %convert_element_type.38, () %tuple.282, (f32[16,3,50,2,128]{4,3,2,1,0:T(2,128)}, s32[]{:T(128)}, f32[50,2,128]{2,1,0:T(2,128)S(1)}) %tuple.283), branch_computations={%region_2.2_spmd, %region_3.3_spmd} | conditional | flops 391936 | bytes 1739800 | solution.py:98
  83.3 32.5 %conditional.2 = (f32[1,2,50,2,128]{4,3,1,2,0:T(2,128)}) conditional(s32[]{:T(128)} %convert_element_type.38, () %tuple.282, (f32[16,3,50,2,128]{4,3,2,1,0:T(2,128)}, s32[]{:T(128)}, f32[50,2,128]{2,1,0:T(2,128)S(1)}) %tuple.283), branch_computations={%region_2.2_spmd, %region_3.3_spmd} | conditional | flops 391936 | bytes 1739800 | solution.py:98
  118.2 65.8 %collective-permute-start.5 = (f32[32,1]{1,0:T(8,128)}, f32[32,1]{1,0:T(8,128)S(1)}, u32[]{:S(2)}, u32[]{:S(2)}) collective-permute-start(f32[32,1]{1,0:T(8,128)} %get-tuple-element.350), channel_id=1, source_target_pairs={{0,8},{8,16},{16,24},{24,32},{32,40},{40,48},{48,56},{56,64},{64,7... | collective-permute-start | bytes 392 | tf_op jit(solution)/shard_map/ppermute | solution.py:25
  184.0 385.8 %collective-permute-start.4 = (f32[32,1]{1,0:T(8,128)S(1)}, f32[32,1]{1,0:T(8,128)S(1)}, u32[]{:S(2)}, u32[]{:S(2)}) collective-permute-start(f32[32,1]{1,0:T(8,128)S(1)} %get-tuple-element.351), channel_id=1, source_target_pairs={{8,0},{16,8},{24,16},{32,24},{40,32},{48,40},{56,48},{64,56},{72,6... | collective-permute-start | bytes 392 | tf_op jit(solution)/shard_map/ppermute | solution.py:28
  570.4 1.2 copy.48
  571.6 1.5 collective-permute-start.1
  573.1 1.2 copy.47
  574.5 6.1 collective-permute-done
  580.5 1.6 copy.49
  582.1 1.6 copy.50
  583.7 2.0 pad_maximum_fusion.14
  585.7 4.2 collective-permute-start.2
  590.0 1.4 collective-permute-start.6
  591.7 2.3 collective-permute-done.3
  594.0 2.6 maximum_multiply_fusion
  596.6 1.9 copy-done
  599.3 63.9 %all-reduce.1 = (f32[]{:T(128)}, f32[]{:T(128)}) all-reduce(f32[]{:T(128)} %get-tuple-element.68, f32[]{:T(128)} %get-tuple-element.67), channel_id=1, replica_groups=mesh['lon'=16,'lat'=8] {'lon','lat'}, use_global_device_ids=true, to_apply=%region_8.9 | all-reduce | flops 2 | bytes 16 | tf_op jit(solution)/shard_map/psum | solution.py:105
  665.0 63.1 %psum.58 = f32[]{:T(128)} all-reduce(f32[]{:T(128)} %multiply_reduce_fusion.4), channel_id=1, replica_groups=mesh['lon'=16,'lat'=8] {'lon','lat'}, use_global_device_ids=true, to_apply=%region_12.13 | all-reduce | flops 1 | bytes 8 | tf_op jit(solution)/shard_map/psum | solution.py:105
  729.5 4.8 collective-permute-start.8
  734.3 1.1 collective-permute-done.9
  735.5 1.8 collective-permute-start.10
  737.3 1.2 collective-permute-done.10
  739.2 67.0 %psum.59 = f32[]{:T(128)} all-reduce(f32[]{:T(128)} %get-tuple-element.256), channel_id=1, replica_groups=mesh['lon'=16,'lat'=8] {'lon','lat'}, use_global_device_ids=true, to_apply=%region_14.15 | all-reduce | flops 1 | bytes 8 | tf_op jit(solution)/shard_map/psum | solution.py:161
  808.0 62.5 %psum.60 = f32[]{:T(128)} all-reduce(f32[]{:T(128)} %get-tuple-element.254), channel_id=1, replica_groups=mesh['lon'=16,'lat'=8] {'lon','lat'}, use_global_device_ids=true, to_apply=%region_16.17 | all-reduce | flops 1 | bytes 8 | tf_op jit(solution)/shard_map/psum | solution.py:105
  872.7 4.0 collective-permute-start.12
  876.7 1.1 collective-permute-done.13
  877.9 1.7 collective-permute-start.14
  880.6 1.2 collective-permute-done.14
  882.5 66.6 %psum.61 = f32[]{:T(128)} all-reduce(f32[]{:T(128)} %get-tuple-element.252), channel_id=1, replica_groups=mesh['lon'=16,'lat'=8] {'lon','lat'}, use_global_device_ids=true, to_apply=%region_18.19 | all-reduce | flops 1 | bytes 8 | tf_op jit(solution)/shard_map/psum | solution.py:161
  951.0 62.6 %psum.62 = f32[]{:T(128)} all-reduce(f32[]{:T(128)} %multiply_reduce_fusion), channel_id=1, replica_groups=mesh['lon'=16,'lat'=8] {'lon','lat'}, use_global_device_ids=true, to_apply=%region_20.21 | all-reduce | flops 1 | bytes 8 | tf_op jit(solution)/shard_map/psum | solution.py:105
  1015.6 4.1 collective-permute-start.16
  1019.7 1.1 collective-permute-done.17
  1020.9 1.7 collective-permute-start.18
  1022.6 1.1 collective-permute-start.19
  1023.7 2.4 slice_bitcast_fusion.50
  1026.9 2.1 copy.45
  1029.0 66.1 %psum.63 = f32[]{:T(128)} all-reduce(f32[]{:T(128)} %fusion.81), channel_id=1, replica_groups=mesh['lon'=16,'lat'=8] {'lon','lat'}, use_global_device_ids=true, to_apply=%region_22.23 | all-reduce | flops 1 | bytes 8 | tf_op jit(solution)/shard_map/psum | solution.py:161
  1096.5 1.9 fusion.67
  1098.4 2.3 fusion.149
  1100.7 2.4 copy.51
  1103.1 2.4 copy.53
  1105.5 4.8 collective-permute-start.20
  1111.3 2.5 copy.52
  1113.8 2.5 copy.54
  1116.3 4.4 broadcast_multiply_fusion.1
  1120.7 3.7 collective-permute-start.22
  1124.4 2.6 collective-permute-start.23
  1128.9 1.9 collective-permute-start.24
  1130.8 4.2 collective-permute-start.25
  1135.1 1.2 collective-permute-done.25
  1136.2 2.4 broadcast_multiply_fusion.2
  1138.6 2.3 fusion.146
  1140.9 2.4 copy.55
  1143.3 5.4 collective-permute-start.26
  1148.7 2.4 copy.57
  1151.1 2.5 copy.56
  1153.6 3.5 collective-permute-done.27
  1157.2 2.5 copy.58
  1159.7 4.1 fusion.57
  1163.8 1.3 select_multiply_fusion.1
  1165.1 1.3 pad_maximum_fusion.10
  (293 shorter events, 123.2 us)
Async XLA Ops:
  1.5 2.0 copy-start.4
  1.5 2.0 copy-start.12
  3.5 2.6 copy-start.13
  116.7 453.1 %copy-start.10 = (f32[16,2,50,2,128]{4,3,1,2,0:T(2,128)}, f32[16,2,50,2,128]{4,3,1,2,0:T(2,128)S(1)}, u32[]{:S(2)}) copy-start(f32[16,2,50,2,128]{4,3,1,2,0:T(2,128)S(1)} %get-tuple-element.61) | copy-start | bytes 4915204
  116.7 0.7 copy-start.16
  116.7 453.0 %copy-start.15 = (f32[32,128]{1,0:T(8,128)S(1)}, f32[32,128]{1,0:T(8,128)}, u32[]{:S(2)}) copy-start(f32[32,128]{1,0:T(8,128)} %param.17) | copy-start | bytes 49156
  116.8 453.0 %copy-start.2 = (f32[2,50,32,128]{3,2,1,0:T(8,128)S(1)}, f32[2,50,32,128]{3,2,1,0:T(8,128)}, u32[]{:S(2)}) copy-start(f32[2,50,32,128]{3,2,1,0:T(8,128)} %param.13) | copy-start | bytes 4915204
  118.2 471.7 %collective-permute-start.5 = (f32[32,1]{1,0:T(8,128)}, f32[32,1]{1,0:T(8,128)S(1)}, u32[]{:S(2)}, u32[]{:S(2)}) collective-permute-start(f32[32,1]{1,0:T(8,128)} %get-tuple-element.350), channel_id=1, source_target_pairs={{0,8},{8,16},{16,24},{24,32},{32,40},{40,48},{48,56},{56,64},{64,7... | collective-permute-start | bytes 392 | tf_op jit(solution)/shard_map/ppermute | solution.py:25
  184.0 405.9 %collective-permute-start.4 = (f32[32,1]{1,0:T(8,128)S(1)}, f32[32,1]{1,0:T(8,128)S(1)}, u32[]{:S(2)}, u32[]{:S(2)}) collective-permute-start(f32[32,1]{1,0:T(8,128)S(1)} %get-tuple-element.351), channel_id=1, source_target_pairs={{8,0},{16,8},{24,16},{32,24},{40,32},{48,40},{56,48},{64,56},{72,6... | collective-permute-start | bytes 392 | tf_op jit(solution)/shard_map/ppermute | solution.py:28
  571.6 10.5 collective-permute-start.1
  574.2 6.3 collective-permute-start
  583.7 10.3 copy-start.3
  585.7 6.0 collective-permute-start.2
  589.9 4.1 collective-permute-start.3
  590.0 8.6 collective-permute-start.6
  591.4 7.2 collective-permute-start.7
  596.6 1.9 copy-start
  729.5 5.9 collective-permute-start.9
  729.5 5.9 collective-permute-start.8
  735.5 3.0 collective-permute-start.10
  737.3 1.2 collective-permute-start.11
  871.9 5.9 collective-permute-start.13
  872.7 5.1 collective-permute-start.12
  877.9 4.0 collective-permute-start.14
  879.6 2.2 collective-permute-start.15
  1014.9 5.9 collective-permute-start.17
  1015.6 5.2 collective-permute-start.16
  1020.9 5.2 collective-permute-start.18
  1022.6 4.3 copy-start.11
  1022.6 3.5 collective-permute-start.19
  1026.1 70.3 %copy-start.6 = (f32[50,32,128]{2,1,0:T(8,128)}, f32[50,32,128]{2,1,0:T(8,128)S(1)}, u32[]{:S(2)}) copy-start(f32[50,32,128]{2,1,0:T(8,128)S(1)} %get-tuple-element.335) | copy-start | bytes 2457604
  1026.9 69.5 %copy-start.5 = (f32[50,32,128]{2,1,0:T(8,128)S(1)}, f32[50,32,128]{2,1,0:T(8,128)}, u32[]{:S(2)}) copy-start(f32[50,32,128]{2,1,0:T(8,128)} %copy-done.4) | copy-start | bytes 2457604
  1026.9 69.5 %copy-start.17 = (f32[2]{0:T(128)S(1)}, f32[2]{0:T(128)}, u32[]{:S(2)}) copy-start(f32[2]{0:T(128)} %constant.73.clone) | copy-start | bytes 28
  1096.4 19.9 %copy-start.14 = (f32[32,128]{1,0:T(8,128)}, f32[32,128]{1,0:T(8,128)S(1)}, u32[]{:S(2)}) copy-start(f32[32,128]{1,0:T(8,128)S(1)} %multiply_add_fusion.50) | copy-start | bytes 49156
  1105.4 8.4 collective-permute-start.21
  1105.5 5.8 collective-permute-start.20
  1116.3 11.7 %copy-start.8 = (f32[50,32,128]{2,1,0:T(8,128)S(1)}, f32[50,32,128]{2,1,0:T(8,128)}, u32[]{:S(2)}) copy-start(f32[50,32,128]{2,1,0:T(8,128)} %get-tuple-element.334) | copy-start | bytes 2457604
  1120.7 6.3 collective-permute-start.22
  1124.4 3.5 collective-permute-start.23
  1128.0 8.3 copy-start.7
  1128.9 6.2 collective-permute-start.24
  1130.8 5.4 collective-permute-start.25
  1143.3 7.8 collective-permute-start.26
  1151.0 6.1 collective-permute-start.27
  1159.7 4.1 copy-start.1
  1163.8 1.4 copy-start.9
where the time goes:
time: 1180 us; the launch traced here: 1170 us
  starting transfers between devices  504 us (43%)
  blocking collectives  452 us (38%)
  local copies, waits for them, and re-layouts  91.1 us (8%)
  other arithmetic  78.1 us (7%)
  waiting for transfers between devices  20.7 us (2%)
    ppermute x14, starting transfers between devices, with_halo(): lax.ppermute(lax.slice_in_dim(block, 0, width, axis=dim), axis, backward)  423 us
    psum x4, blocking collectives, residual_norm(): return lax.psum(jnp.sum(residual * residual), ('lon', 'lat'))  252 us
    psum x3, blocking collectives, per_device(): lax.psum(jnp.sum(direction * image_field), ('lon', 'lat'))  200 us
    ppermute x14, starting transfers between devices, with_halo(): lax.ppermute(lax.slice_in_dim(block, block.shape[dim] - width, None, axis...  81.2 us
    cond x52, other arithmetic  31 us
    cond x46, local copies, waits for them, and re-layouts  26.6 us
  transfers between devices with their start and end apart: 28, of which 11 were waited for; matrix products, arithmetic and copies ran while one was open for 2% of the time, Pallas kernels for 0%

commit v1 on v0

v1 whole, which is shorter than its diff:
```python
import math

import jax
import jax.numpy as jnp
from jax import lax
from jax.experimental import pallas as pl
from jax.experimental.pallas import tpu as pltpu
from jax.sharding import PartitionSpec as P

LEVELS = 50
SURFACE_DAMPING = 0.05
COURANT = 0.25
GAINS = (0.7, -0.5)
ROWS = 32
COLS = 128
HALF = LEVELS // 2
SLOTS = 32
FIELDS = 6
GROUPS = -(-LEVELS // 4)
VMEM_LIMIT = 56 * 1024 * 1024
F32 = jnp.float32
VMEM = pltpu.VMEM

PAIRS = tuple((i, j) for i in range(4) for j in range(i, 5))


def iota(shape, dim):
    return lax.broadcasted_iota(jnp.int32, shape, dim)


def pick(parity, even, odd):
    return jnp.where(jnp.broadcast_to(parity, even.shape) == 0, even, odd)


def roll(x, shift, axis):
    return pltpu.roll(x, shift, axis)


def two_sum(a, b):
    s = a + b
    bb = s - a
    return s, (a - (s - bb)) + (b - bb)


def quick_sum(a, b):
    s = a + b
    return s, b - (s - a)


def split(a):
    t = 4097.0 * a
    hi = t - (t - a)
    return hi, a - hi


def two_prod(a, b, sa=None, sb=None):
    ah, al = sa or split(a)
    bh, bl = sb or split(b)
    p = a * b
    return p, ((ah * bh - p) + ah * bl + al * bh) + al * bl


def dd_add(a, b):
    s, e = two_sum(a[0], b[0])
    return quick_sum(s, e + (a[1] + b[1]))


def dd_mul(a, b):
    p, e = two_prod(a[0], b[0])
    return quick_sum(p, e + (a[0] * b[1] + a[1] * b[0]))


def dd_neg(a):
    return -a[0], -a[1]


def dd_inv(a):
    r = 1.0 / a[0]
    p, e = two_prod(a[0], r)
    rest = ((1.0 - p) - e) - a[1] * r
    return quick_sum(r, r * rest)


def solve_kernel(
    lam_h, vel_h, tr_h, dif_h, lams_ref, depth_ref, lev_ref,
    mixed_ref, f_ref, osm_ref, big1_ref, big2_ref, slots_ref, g1_ref, g2_ref,
    lam, vel, tr, dif, w_s, z_s, col_sem, rest_sem,
):
    lon_par = lax.rem(lax.axis_index("lon"), 2)
    lat_par = lax.rem(lax.axis_index("lat"), 2)
    step = 5
    copies = []
    for i in range(HALF // step):
        top, low = i * step, LEVELS - (i + 1) * step
        part = []
        for n, at in enumerate((top, low)):
            part.append(pltpu.make_async_copy(dif_h.at[pl.ds(at, step)], dif.at[pl.ds(at, step)], col_sem.at[i, 2 * n]))
            part.append(pltpu.make_async_copy(lam_h.at[:, pl.ds(at, step)], lam.at[:, pl.ds(at, step)], col_sem.at[i, 2 * n + 1]))
        copies.append(part)
    for part in copies:
        for c in part:
            c.start()
    rest = [
        pltpu.make_async_copy(vel_h, vel, rest_sem.at[0]),
        pltpu.make_async_copy(tr_h, tr, rest_sem.at[1]),
    ]
    for c in rest:
        c.start()

    lev = lev_ref[...]
    zero = jnp.zeros((ROWS, COLS), F32)

    def coef(k):
        return jnp.where(lev > k + 1, dif[k], 0.0)

    def right(n, k):
        return jnp.where(lev > k, lam[n, k], 0.0)

    e = jnp.ones((ROWS, COLS), F32)
    y = [zero, zero]
    w = zero
    eb = e
    yb = [zero, zero]
    wb = zero
    cb = zero
    waited = 0
    for k in range(HALF):
        need = min((k + 1) // step, HALF // step - 1)
        while waited <= need:
            for c in copies[waited]:
                c.wait()
            waited += 1
        c_k = coef(k)
        y = [right(n, k) + w * y[n] for n in range(2)]
        inv = 1.0 / (e + c_k)
        w = c_k * inv
        w_s[k] = w
        for n in range(2):
            z_s[n, k] = y[n] * inv
        e = 1.0 + e * w
        if k < HALF - 1:
            m = LEVELS - 1 - k
            c_m = coef(m - 1)
            yb = [right(n, m) + wb * yb[n] for n in range(2)]
            invb = 1.0 / (eb + c_m)
            wb = c_m * invb
            w_s[m] = wb
            for n in range(2):
                z_s[n, m] = yb[n] * invb
            eb = 1.0 + eb * wb
    inv = 1.0 / (e + eb - 1.0)
    below = [(right(n, HALF) + wb * yb[n] + w * y[n]) * inv for n in range(2)]
    total = list(below)
    for n in range(2):
        mixed_ref[n, HALF] = below[n]
    above = list(below)
    for i in range(1, HALF + 1):
        k = HALF - i
        for n in range(2):
            above[n] = z_s[n, k] + w_s[k] * above[n]
            mixed_ref[n, k] = above[n]
            total[n] = total[n] + above[n]
        m = HALF + i
        if m < LEVELS:
            for n in range(2):
                below[n] = z_s[n, m] + w_s[m] * below[n]
                mixed_ref[n, m] = below[n]
                total[n] = total[n] + below[n]
    f = jnp.where(lev > 0, lams_ref[...] + (GAINS[0] * total[0] + GAINS[1] * total[1]) / math.sqrt(LEVELS), 0.0)
    f_ref[...] = f
    lane = iota((ROWS, COLS), 1)
    osm = jnp.where(
        lane < 16, roll(f, 8, 1), jnp.where(lane < 32, roll(depth_ref[...], 24, 1), roll(lev.astype(F32), 40, 1))
    )
    osm_ref[...] = osm

    for c in rest:
        c.wait()

    sources = (
        lambda k: mixed_ref[0, k], lambda k: mixed_ref[1, k], lambda k: vel[0, k],
        lambda k: vel[1, k], lambda k: tr[0, k], lambda k: tr[1, k],
    )
    slot = lane // 4
    for tile in range(2):
        count = min(SLOTS, LEVELS - tile * SLOTS)

        def gather(s, acc, tile=tile):
            here = slot == s
            return tuple(jnp.where(here, roll(src(s + tile * SLOTS), 4 * s + 2, 1), a) for src, a in zip(sources, acc))

        got = lax.fori_loop(0, count, gather, (zero,) * FIELDS)
        for i in range(FIELDS):
            slots_ref[i, tile] = got[i]
    near = lane % 4 < 2
    for i in range(FIELDS):
        a, b = slots_ref[i, 0], slots_ref[i, 1]
        east_edge = jnp.where(near, a, roll(b, 2, 1))
        west_edge = jnp.where(near, roll(a, COLS - 2, 1), b)
        big1_ref[i] = pick(lon_par, east_edge, west_edge)
        big2_ref[i] = pick(lon_par, west_edge, east_edge)

    pair = iota((8, COLS), 0) // 2
    for i, src in enumerate(sources):
        for g in range(GROUPS):
            first = jnp.zeros((8, COLS), F32)
            last = first
            for q in range(min(4, LEVELS - 4 * g)):
                tile = src(4 * g + q)
                first = jnp.where(pair == q, roll(tile[:8], 2 * q, 0) if q else tile[:8], first)
                last = jnp.where(pair == (q + 3) % 4, roll(tile[ROWS - 8 :], 2 * q, 0) if q else tile[ROWS - 8 :], last)
            g1_ref[i * GROUPS + g] = pick(lat_par, last, first)
            g2_ref[i * GROUPS + g] = pick(lat_par, first, last)


CORNERS = 4


def lon_kernel(
    f_ref, depth_ref, lev_ref, o1_ref, o2_ref, slots_ref, b1_ref, b2_ref, g1_ref, g2_ref,
    ext_ref, s1_ref, s2_ref, side_ref, h1_ref, h2_ref,
):
    lon_par = lax.rem(lax.axis_index("lon"), 2)
    lat_par = lax.rem(lax.axis_index("lat"), 2)
    lane = iota((ROWS, COLS), 1)
    o1, o2 = o1_ref[...], o2_ref[...]
    from_east, from_west = pick(lon_par, o1, o2), pick(lon_par, o2, o1)
    for i, own in enumerate((f_ref[...], depth_ref[...], lev_ref[...].astype(F32))):
        edge = jnp.where(lane < 16 * i + 8, from_west, from_east)
        edge = roll(edge, COLS - 8 - 16 * i, 1)
        edge = jnp.where((lane < 8) | (lane >= COLS - 8), edge, 0.0)
        ext_ref[i, :, :COLS] = own
        ext_ref[i, :, COLS:] = edge
        for at, here in ((0, own), (COLS, edge)):
            first, last = here[:8], here[ROWS - 8 :]
            s1_ref[i, :, at : at + COLS] = pick(lat_par, last, first)
            s2_ref[i, :, at : at + COLS] = pick(lat_par, first, last)
    near = lane % 4 < 2
    for i in range(FIELDS):
        b1, b2 = b1_ref[i], b2_ref[i]
        east, west = pick(lon_par, b1, b2), pick(lon_par, b2, b1)
        own_a, own_b = slots_ref[i, 0], slots_ref[i, 1]
        side_ref[0, i, 0] = jnp.where(near, west, own_a)
        side_ref[0, i, 1] = jnp.where(near, roll(west, COLS - 2, 1), own_b)
        side_ref[1, i, 0] = jnp.where(near, own_a, roll(east, 2, 1))
        side_ref[1, i, 1] = jnp.where(near, own_b, east)
    h1_ref[: FIELDS * GROUPS] = g1_ref[...]
    h2_ref[: FIELDS * GROUPS] = g2_ref[...]
    pair = iota((8, COLS), 0) // 2
    for c in range(CORNERS):
        first = jnp.zeros((8, COLS), F32)
        last = first
        for q in range(4):
            side, field, tile = corner_of(4 * c + q)
            x = side_ref[side, field, tile]
            first = jnp.where(pair == q, roll(x[:8], 2 * q, 0) if q else x[:8], first)
            last = jnp.where(pair == (q + 3) % 4, roll(x[ROWS - 8 :], 2 * q, 0) if q else x[ROWS - 8 :], last)
        h1_ref[FIELDS * GROUPS + c] = pick(lat_par, last, first)
        h2_ref[FIELDS * GROUPS + c] = pick(lat_par, first, last)


def corner_of(index):
    return index // 8, index // 2 % 4, index % 2


def krylov_kernel(ext_ref, s1_ref, s2_ref, vec_ref, lev_ref, gram_ref):
    lat_par = lax.rem(lax.axis_index("lat"), 2)
    rows, cols = ROWS + 16, 2 * COLS
    whole = []
    for i in range(3):
        s1, s2 = s1_ref[i], s2_ref[i]
        whole.append(jnp.concatenate([ext_ref[i], pick(lat_par, s1, s2), pick(lat_par, s2, s1)], axis=0))
    f, depth, lev = whole

    def east(x):
        return roll(x, cols - 1, 1)

    def west(x):
        return roll(x, 1, 1)

    def north(x):
        return roll(x, rows - 1, 0)

    def south(x):
        return roll(x, 1, 0)

    sea = jnp.where(lev > 0.0, 1.0, 0.0)
    face_east = 0.5 * (depth + east(depth)) * sea * east(sea)
    face_north = 0.5 * (depth + north(depth)) * sea * north(sea)
    base = (1.0 - sea) + SURFACE_DAMPING * sea
    sub = iota((8, cols), 0)

    def trim(x):
        return jnp.concatenate([x[:ROWS], jnp.where(sub < 4, x[ROWS : ROWS + 8], x[ROWS + 8 :])], axis=0)

    lev_ref[...] = trim(lev)
    vectors = [f]
    vec_ref[0] = trim(f)
    for i in range(1, 5):
        p = vectors[-1]
        flow_east = face_east * (p - east(p))
        flow_north = face_north * (p - north(p))
        p = base * p + (flow_east - west(flow_east)) + (flow_north - south(flow_north))
        vectors.append(p)
        if i < 4:
            vec_ref[i] = trim(p)
    own = [v[:ROWS, :COLS] for v in vectors]
    parts = [split(v) for v in own]
    row = iota((16, COLS), 0)
    hi = jnp.zeros((16, COLS), F32)
    lo = hi
    for at, (i, j) in enumerate(PAIRS):
        p, e = two_prod(own[i], own[j], parts[i], parts[j])
        quarters = [(p[8 * r : 8 * r + 8], e[8 * r : 8 * r + 8]) for r in range(ROWS // 8)]
        total = dd_add(dd_add(quarters[0], quarters[1]), dd_add(quarters[2], quarters[3]))
        for s in (4, 2, 1):
            total = dd_add(total, (roll(total[0], s, 0), roll(total[1], s, 0)))
        hi = jnp.where(row == at, jnp.concatenate([total[0]] * 2, axis=0), hi)
        lo = jnp.where(row == at, jnp.concatenate([total[1]] * 2, axis=0), lo)
    total = (hi, lo)
    for s in (64, 32, 16, 8, 4, 2, 1):
        total = dd_add(total, (roll(total[0], s, 1), roll(total[1], s, 1)))
    lane = iota((16, COLS), 1)
    line = jnp.where(lane == row, total[0], jnp.where(lane == row + 16, total[1], 0.0))
    line = line[:8] + line[8:]
    for s in (4, 2, 1):
        line = line + roll(line, s, 0)
    gram_ref[...] = jnp.concatenate([line] * (gram_ref.shape[0] // 8), axis=0)


def galerkin(gram):
    rows = gram.shape[0]
    parts = [(gram[8 * r : 8 * r + 8], roll(gram[8 * r : 8 * r + 8], COLS - 16, 1)) for r in range(rows // 8)]
    while len(parts) > 1:
        parts = [dd_add(parts[i], parts[i + 1]) for i in range(0, len(parts) - 1, 2)] + parts[len(parts) // 2 * 2 :]
    total = parts[0]
    for s in (4, 2, 1):
        total = dd_add(total, (roll(total[0], s, 0), roll(total[1], s, 0)))
    entry = {}
    for at, (i, j) in enumerate(PAIRS):
        entry[i, j] = entry[j, i] = tuple(jnp.broadcast_to(t[:, at : at + 1], (8, COLS)) for t in total)
    mat = [[entry[i, j + 1] for j in range(4)] for i in range(4)]
    rhs = [entry[i, 0] for i in range(4)]
    size = [jnp.abs(mat[i][i][0]) for i in range(4)]
    for k in range(4):
        fine = mat[k][k][0] > 1e-12 * size[k]
        inv = dd_inv((jnp.where(fine, mat[k][k][0], 1.0), jnp.where(fine, mat[k][k][1], 0.0)))
        inv = tuple(jnp.where(fine, t, 0.0) for t in inv)
        for j in range(k + 1, 4):
            mat[k][j] = dd_mul(mat[k][j], inv)
        rhs[k] = dd_mul(rhs[k], inv)
        for i in range(k + 1, 4):
            less = dd_neg(mat[i][k])
            for j in range(k + 1, 4):
                mat[i][j] = dd_add(mat[i][j], dd_mul(less, mat[k][j]))
            rhs[i] = dd_add(rhs[i], dd_mul(less, rhs[k]))
    for k in range(2, -1, -1):
        for j in range(k + 1, 4):
            rhs[k] = dd_add(rhs[k], dd_neg(dd_mul(mat[k][j], rhs[j])))
    return [r[0] for r in rhs]


CHUNK = 12
CHUNKS = tuple((c * CHUNK, CHUNK if c < 3 else LEVELS - 3 * CHUNK) for c in range(4))


def final_kernel(
    gram_ref, vec_ref, lev_ref, side_ref, h1_ref, h2_ref, mixed_h, vel_h, tr_h,
    adj_h, avel_h, sol_ref,
    mixed, vel, tr, adj, avel, sol_s, edge1, edge2, edge3, in_sem, out_sem,
):
    lat_par = lax.rem(lax.axis_index("lat"), 2)
    reads = []
    for c, (at, count) in enumerate(CHUNKS):
        part = [
            pltpu.make_async_copy(src.at[:, pl.ds(at, count)], dst.at[:, pl.ds(at, count)], in_sem.at[c, i])
            for i, (src, dst) in enumerate(((mixed_h, mixed), (vel_h, vel), (tr_h, tr)))
        ]
        for r in part:
            r.start()
        reads.append(part)

    coefs = galerkin(gram_ref[...])
    tall = ROWS + 8
    for half in range(2):
        at = half * COLS
        total = 0.0
        for i in range(4):
            wide = jnp.concatenate([coefs[i]] * (tall // 8), axis=0)
            total = total + wide * vec_ref[i, :, at : at + COLS]
        sol_s[:, at : at + COLS] = total
    sol_ref[...] = sol_s[:ROWS, :COLS]

    lane = iota((tall, COLS), 1)
    pair = iota((8, COLS), 0) // 2
    even = jnp.broadcast_to(lat_par, (8, COLS)) == 0
    masks = [(pair == q) == even for q in range(4)]

    def edge_rows(index, q):
        x = jnp.where(masks[q], h1_ref[index], h2_ref[index])
        return roll(x, 8 - 2 * q, 0) if q else x

    flux1, flux2 = [], []
    for side in range(2):
        def around(ref):
            own, edge = roll(ref[:, :COLS], 2, 1), roll(ref[:, COLS:], 2, 1)
            x = jnp.where(lane < 2, own, edge) if side else jnp.where(lane < 2, edge, own)
            for s in (4, 8, 16, 32, 64):
                x = jnp.where(lane < s, x, roll(x, s, 1))
            return x

        levels, pressure = around(lev_ref), around(sol_s)
        for tile in range(2):
            def column(field):
                index = side * 8 + field * 2 + tile
                return jnp.concatenate(
                    [side_ref[side, field, tile], edge_rows(FIELDS * GROUPS + index // 4, index % 4)], axis=0
                )

            wet = jnp.where((lane // 4 + tile * SLOTS).astype(F32) < levels, 1.0, 0.0)
            move = COURANT * wet
            u, v = column(2), column(3)
            for n in range(2):
                x = column(n) + GAINS[n] * wet * pressure
                flux = u * x
                flux1.append(flux)
                x = x + move * (roll(flux, COLS - 1, 1) - roll(flux, 1, 1))
                for _ in range(2):
                    flux = v * x
                    x = x + move * (roll(flux, tall - 1, 0) - roll(flux, 1, 0))
                flux2.append(u * x)
    own_rows = iota((ROWS, COLS), 1) % 4 == 2
    for tile in range(2):
        for n in range(2):
            west, east = tile * 2 + n, 4 + tile * 2 + n
            edge1[n, tile] = jnp.where(lane % 4 == 2, flux1[east], roll(flux1[west], 2, 1))
            edge2[n, tile] = jnp.where(lane % 4 == 2, flux2[east], roll(flux2[west], 2, 1))[:ROWS]
            edge3[n, tile] = jnp.where(own_rows, side_ref[1, 4 + n, tile], roll(side_ref[0, 4 + n, tile], 2, 1))

    def zonal(x, edge, shift):
        width = x.shape[0]
        at = lane[:width]
        around = roll(edge, shift, 1)
        high = jnp.where(at == COLS - 1, around, roll(x, COLS - 1, 1))
        low = jnp.where(at == 0, around, roll(x, 1, 1))
        return high - low

    def meridional(x):
        return roll(x, tall - 1, 0) - roll(x, 1, 0)

    def one_level(g, q):
        k = 4 * g + q
        tile, slot = k // SLOTS, lax.rem(k, SLOTS)
        shift = COLS - 3 - 4 * slot
        wet = jnp.where(k.astype(F32) < lev_ref[:, :COLS], 1.0, 0.0)
        move = COURANT * wet
        wet_sol = wet * sol_s[:, :COLS]

        def tall_field(ref, n, field):
            return jnp.concatenate([ref[n, k], edge_rows(field * GROUPS + g, q)], axis=0)

        u, v = tall_field(vel, 0, 2), tall_field(vel, 1, 3)
        east_sum, north_sum = 0.0, 0.0
        for n in range(2):
            x = tall_field(mixed, n, n) + GAINS[n] * wet_sol
            x = x + move * zonal(u * x, edge1[n, tile], shift)
            x = x + move * meridional(v * x)
            x = (x + move * meridional(v * x))[:ROWS]
            x = x + move[:ROWS] * zonal(u[:ROWS] * x, edge2[n, tile], shift)
            adj[n, k] = x
            t = tall_field(tr, n, 4 + n)
            east_sum = east_sum + x * zonal(t[:ROWS], edge3[n, tile], shift)
            north_sum = north_sum + x * meridional(t)[:ROWS]
        avel[0, k] = -move[:ROWS] * east_sum
        avel[1, k] = -move[:ROWS] * north_sum

    writes = []
    for c, (at, count) in enumerate(CHUNKS):
        for r in reads[c]:
            r.wait()

        def group(g, carry):
            for q in range(4):
                one_level(g, q)
            return carry

        lax.fori_loop(at // 4, (at + count) // 4, group, 0)
        for q in range(count % 4):
            one_level(jnp.int32(GROUPS - 1), q)
        for i, (src, dst) in enumerate(((adj, adj_h), (avel, avel_h))):
            copy = pltpu.make_async_copy(src.at[:, pl.ds(at, count)], dst.at[:, pl.ds(at, count)], out_sem.at[c, i])
            copy.start()
            writes.append(copy)
    for copy in writes:
        copy.wait()


def swaps(size, first, periodic):
    out = []
    for i in range(first, size, 2):
        if i + 1 < size or periodic:
            out += [(i, (i + 1) % size), ((i + 1) % size, i)]
    return out


def shape(*dims):
    return jax.ShapeDtypeStruct(dims, F32)


def call(kernel, name, outs, in_any, out_any, scratch, args):
    here, there = pl.BlockSpec(memory_space=VMEM), pl.BlockSpec(memory_space=pl.ANY)
    return pl.pallas_call(
        kernel,
        name=name,
        out_shape=outs,
        in_specs=[there if i in in_any else here for i in range(len(args))],
        out_specs=tuple(there if i in out_any else here for i in range(len(outs))),
        scratch_shapes=scratch,
        compiler_params=pltpu.CompilerParams(vmem_limit_bytes=VMEM_LIMIT),
    )(*args)


def per_device(lam_tracer, tracer, velocity, diffusivity, lam_surface, sea_depth, levels):
    lon, lat = lax.axis_size("lon"), lax.axis_size("lat")
    tile = (ROWS, COLS)
    deep = (2, LEVELS) + tile
    mixed, f, osm, big1, big2, slots, g1, g2 = call(
        solve_kernel, "column_solve",
        (shape(*deep), shape(*tile), shape(*tile), shape(FIELDS, *tile), shape(FIELDS, *tile),
         shape(FIELDS, 2, *tile), shape(FIELDS * GROUPS, 8, COLS), shape(FIELDS * GROUPS, 8, COLS)),
        (0, 1, 2, 3), (),
        [VMEM(deep, F32), VMEM(deep, F32), VMEM(deep, F32), VMEM((LEVELS,) + tile, F32), VMEM((LEVELS,) + tile, F32),
         VMEM(deep, F32), pltpu.SemaphoreType.DMA((HALF // 5, 4)), pltpu.SemaphoreType.DMA((2,))],
        (lam_tracer, velocity, tracer, diffusivity, lam_surface, sea_depth, levels),
    )
    even_lon, odd_lon = swaps(lon, 0, True), swaps(lon, 1, True)
    even_lat, odd_lat = swaps(lat, 0, False), swaps(lat, 1, False)
    o1, b1 = lax.ppermute(osm, "lon", even_lon), lax.ppermute(big1, "lon", even_lon)
    o2, b2 = lax.ppermute(osm, "lon", odd_lon), lax.ppermute(big2, "lon", odd_lon)
    height = FIELDS * GROUPS + CORNERS
    ext, s1, s2, side, h1, h2 = call(
        lon_kernel, "after_lon",
        (shape(3, ROWS, 2 * COLS), shape(3, 8, 2 * COLS), shape(3, 8, 2 * COLS), shape(2, FIELDS, 2, *tile),
         shape(height, 8, COLS), shape(height, 8, COLS)),
        (), (), [],
        (f, sea_depth, levels, o1, o2, slots, b1, b2, g1, g2),
    )
    s1, h1 = lax.ppermute(s1, "lat", even_lat), lax.ppermute(h1, "lat", even_lat)
    s2, h2 = lax.ppermute(s2, "lat", odd_lat), lax.ppermute(h2, "lat", odd_lat)
    vec, lev, gram = call(
        krylov_kernel, "krylov",
        (shape(4, ROWS + 8, 2 * COLS), shape(ROWS + 8, 2 * COLS), shape(lon * lat, COLS)),
        (), (), [],
        (ext, s1, s2),
    )
    gram = lax.all_to_all(gram, ("lon", "lat"), 0, 0, tiled=True)
    adjoint, adjoint_velocity, pressure = call(
        final_kernel, "sweeps",
        (shape(*deep), shape(*deep), shape(*tile)),
        (6, 7, 8), (0, 1),
        [VMEM(deep, F32)] * 5
        + [VMEM((ROWS + 8, 2 * COLS), F32), VMEM((2, 2, ROWS + 8, COLS), F32), VMEM((2, 2) + tile, F32), VMEM((2, 2) + tile, F32),
           pltpu.SemaphoreType.DMA((4, 3)), pltpu.SemaphoreType.DMA((4, 2))],
        (gram, vec, lev, side, h1, h2, mixed, velocity, tracer),
    )
    return adjoint, adjoint_velocity, pressure


def solution(mesh):
    deep, flat = P(None, None, "lat", "lon"), P("lat", "lon")
    return jax.shard_map(
        per_device,
        mesh=mesh,
        in_specs=(deep, deep, deep, P(None, "lat", "lon"), flat, flat, flat),
        out_specs=(deep, deep, flat),
        check_vma=False,
    )
```

time: 1180 us -> 73.8 us (0.06); the launches traced: 1170 us -> 73.5 us
  starting transfers between devices: 504 us -> 16.8 us
  blocking collectives: 452 us -> 16 us
  local copies, waits for them, and re-layouts: 91.1 us -> 2.11 us
  other arithmetic: 78.1 us -> 0 us
  Pallas kernels: 0 us -> 30.6 us
  waiting for transfers between devices: 20.7 us -> 7.13 us
    ppermute x28 -> x8, starting transfers between devices: 504 us -> 16.8 us  [the longest x1 4.1 us: per_device(): lax.ppermute(big2, 'lon', odd_lon)]
    psum x7 -> x0, blocking collectives: 452 us -> none  [the longest x4 252 us: residual_norm(): return lax.psum(jnp.sum(residual * residual), ('lon', 'lat'))]
    cond x52 -> x0, other arithmetic: 31 us -> none
    pallas_call x0 -> x4, Pallas kernels: none -> 30.6 us  [call(): pl.pallas_call(kernel, name=name, out_shape=outs, in_specs=[there if i in...]
    cond x46 -> x0, local copies, waits for them, and re-layouts: 26.6 us -> none
    slice x18 -> x0, local copies, waits for them, and re-layouts: 19.3 us -> none  [the longest x7 10.6 us: with_halo(): lax.slice_in_dim(block, 0, width, axis=dim)]
    mul x17 -> x0, other arithmetic: 18.9 us -> none  [the longest x2 5.17 us: meridional_sweep(): flux_field = meridional * field]
    all_to_all x0 -> x1, blocking collectives: none -> 16 us  [per_device(): gram = lax.all_to_all(gram, ('lon', 'lat'), 0, 0, tiled=True)]
  transfers between devices with their start and end apart: 28 -> 8, of which waited for: 11 -> 2; matrix products, arithmetic and copies ran while one was open for 2% -> 0% of each run, Pallas kernels for 0% -> 4%
where the time goes in v1:
time: 73.8 us; the launch traced here: 73.5 us
  Pallas kernels  30.6 us (41%)
  starting transfers between devices  16.8 us (23%)
  blocking collectives  16 us (22%)
  waiting for transfers between devices  7.13 us (10%)
  local copies, waits for them, and re-layouts  2.11 us (3%)
    pallas_call x4, Pallas kernels, call(): pl.pallas_call(kernel, name=name, out_shape=outs, in_specs=[there if i in...  30.6 us
    all_to_all x1, blocking collectives, per_device(): gram = lax.all_to_all(gram, ('lon', 'lat'), 0, 0, tiled=True)  16 us
    ppermute x1, waiting for transfers between devices, per_device(): lax.ppermute(osm, 'lon', odd_lon)  5.43 us
    ppermute x1, starting transfers between devices, per_device(): lax.ppermute(big2, 'lon', odd_lon)  4.1 us
    ppermute x1, starting transfers between devices, per_device(): lax.ppermute(s2, 'lat', odd_lat)  3.92 us
    ppermute x1, starting transfers between devices, per_device(): lax.ppermute(h2, 'lat', odd_lat)  3.44 us
    ppermute x1, starting transfers between devices, per_device(): lax.ppermute(h1, 'lat', even_lat)  2.38 us
    ppermute x1, starting transfers between devices, per_device(): lax.ppermute(big1, 'lon', even_lon)  2.21 us
  transfers between devices with their start and end apart: 8, of which 2 were waited for; matrix products, arithmetic and copies ran while one was open for 0% of the time, Pallas kernels for 4%

profile of v1, /device:TPU:1, one launch (start us, length us, event | category | flops | bytes accessed | tf_op | source)
XLA Modules:
  0.0 73.5 jit_solution(1925793150254354162)
XLA Ops:
  0.6 9.9 %column_solve.1 = (f32[2,50,32,128]{3,2,1,0:T(8,128)}, f32[32,128]{1,0:T(8,128)}, f32[32,128]{1,0:T(8,128)}, f32[6,32,128]{2,1,0:T(8,128)}, f32[6,32,128]{2,1,0:...) custom-call(f32[2,50,32,128]{3,2,1,0:T(8,128)} %lam_h.1, ...), custom_call_target="tpu_custom_call" | custom-call | tf_op jit(solution)/shard_map/column_solve/pallas_call | solution.py:512
  10.5 2.2 %collective-permute-start.2 = (f32[6,32,128]{2,1,0:T(8,128)}, f32[6,32,128]{2,1,0:T(8,128)S(1)}, u32[]{:S(2)}, u32[]{:S(2)}) collective-permute-start(f32[6,32,128]{2,1,0:T(8,128)} %get-tuple-element.23), channel_id=1, source_target_pairs={{0,8},{8,0},{16,24},{24,16},{32,40},{40,32},{48,56},{56,48},{64,72... | collective-permute-start | bytes 294920 | tf_op jit(solution)/shard_map/ppermute | solution.py:538
  12.8 4.1 %collective-permute-start.3 = (f32[6,32,128]{2,1,0:T(8,128)}, f32[6,32,128]{2,1,0:T(8,128)S(1)}, u32[]{:S(2)}, u32[]{:S(2)}) collective-permute-start(f32[6,32,128]{2,1,0:T(8,128)} %get-tuple-element.24), channel_id=1, source_target_pairs={{8,16},{16,8},{24,32},{32,24},{40,48},{48,40},{56,64},{64,56},{72,... | collective-permute-start | bytes 294920 | tf_op jit(solution)/shard_map/ppermute | solution.py:539
  16.8 0.7 collective-permute-start.1
  17.5 0.0 collective-permute-start
  17.5 5.4 %collective-permute-done.1.o2_ref = f32[32,128]{1,0:T(8,128)S(1)} collective-permute-done((f32[32,128]{1,0:T(8,128)}, f32[32,128]{1,0:T(8,128)S(1)}, u32[]{:S(2)}, u32[]{:S(2)}) %collective-permute-start.1) | collective-permute-done | bytes 16416 | tf_op jit(solution)/shard_map/ppermute | solution.py:539
  23.0 0.0 copy-start.6
  23.0 0.0 collective-permute-done.o1_ref
  23.0 0.0 copy-start.7
  23.0 0.0 collective-permute-done.2.b1_ref
  23.0 0.0 copy-start.2
  23.0 0.0 collective-permute-done.3.b2_ref
  23.0 0.0 copy-start.3
  23.0 0.6 copy-done.6
  23.6 0.0 copy-done.7
  23.6 0.1 copy-done.2
  23.6 0.0 copy-done.3
  23.7 2.5 %after_lon.1 = (f32[3,32,256]{2,1,0:T(8,128)}, f32[3,8,256]{2,1,0:T(8,128)}, f32[3,8,256]{2,1,0:T(8,128)}, f32[2,6,2,32,128]{4,3,2,1,0:T(8,128)}, f32[82,8,128]{2,1,0:T(8,128)}, /*index=5*/f32[82,8,128]{2,1,0:T(8,128)}) custom-call(f32[32,128]{1,0:T(8,128)} %get-tuple-element.20.f_ref, f32[32,128]{1,0:T(8,128)} %depth_ref.3, s32[32,128]{1,0:T(8,128)} %lev_ref.3, ...), custom_call_target="tpu_custom_call" | custom-call | tf_op jit(solution)/shard_map/after_lon/pallas_call | solution.py:512
  26.1 2.4 %collective-permute-start.6 = (f32[82,8,128]{2,1,0:T(8,128)}, f32[82,8,128]{2,1,0:T(8,128)S(1)}, u32[]{:S(2)}, u32[]{:S(2)}) collective-permute-start(f32[82,8,128]{2,1,0:T(8,128)} %get-tuple-element.34), channel_id=1, source_target_pairs={{0,1},{1,0},{2,3},{3,2},{4,5},{5,4},{6,7},{7,6},{8,9},{9,8},{10,11... | collective-permute-start | bytes 1007624 | tf_op jit(solution)/shard_map/ppermute | solution.py:548
  28.5 3.4 %collective-permute-start.7 = (f32[82,8,128]{2,1,0:T(8,128)}, f32[82,8,128]{2,1,0:T(8,128)S(1)}, u32[]{:S(2)}, u32[]{:S(2)}) collective-permute-start(f32[82,8,128]{2,1,0:T(8,128)} %get-tuple-element.35), channel_id=1, source_target_pairs={{1,2},{2,1},{3,4},{4,3},{5,6},{6,5},{9,10},{10,9},{11,12},{12,11},... | collective-permute-start | bytes 1007624 | tf_op jit(solution)/shard_map/ppermute | solution.py:549
  32.0 0.1 collective-permute-start.4
  32.0 3.9 %collective-permute-start.5 = (f32[3,8,256]{2,1,0:T(8,128)}, f32[3,8,256]{2,1,0:T(8,128)S(1)}, u32[]{:S(2)}, u32[]{:S(2)}) collective-permute-start(f32[3,8,256]{2,1,0:T(8,128)} %get-tuple-element.29), channel_id=1, source_target_pairs={{1,2},{2,1},{3,4},{4,3},{5,6},{6,5},{9,10},{10,9},{11,12},{12,11},... | collective-permute-start | bytes 73736 | tf_op jit(solution)/shard_map/ppermute | solution.py:549
  36.0 0.0 collective-permute-done.4.s1_ref
  36.0 0.0 copy-start.4
  36.0 1.7 %collective-permute-done.5.s2_ref = f32[3,8,256]{2,1,0:T(8,128)S(1)} collective-permute-done((f32[3,8,256]{2,1,0:T(8,128)}, f32[3,8,256]{2,1,0:T(8,128)S(1)}, u32[]{:S(2)}, u32[]{:S(2)}) %collective-permute-start.5) | collective-permute-done | bytes 24608 | tf_op jit(solution)/shard_map/ppermute | solution.py:549
  37.7 0.0 copy-start.5
  37.7 0.0 copy-done.4
  37.7 0.6 copy-done.5
  38.3 2.8 %krylov.1 = (f32[4,40,256]{2,1,0:T(8,128)}, f32[40,256]{1,0:T(8,128)}, f32[128,128]{1,0:T(8,128)}) custom-call(f32[3,32,256]{2,1,0:T(8,128)} %get-tuple-element.27.ext_ref, f32[3,8,256]{2,1,0:T(8,128)} %copy-done.4, f32[3,8,256]{2,1,0:T(8,128)} %copy-done.5), custom_call_target="tpu_custom_call" | custom-call | tf_op jit(solution)/shard_map/krylov/pallas_call | solution.py:512
  41.1 16.0 %all_to_all.11 = f32[128,1,128]{2,1,0:T(1,128)} all-to-all(f32[128,1,128]{2,1,0:T(1,128)} %bitcast.5), channel_id=1, replica_groups=mesh['lon'=16,'lat'=8] {'lon','lat'}, dimensions={0} | all-to-all | bytes 131072 | tf_op jit(solution)/shard_map/all_to_all | solution.py:556
  57.1 0.0 collective-permute-done.6.h1_ref
  57.1 0.0 copy-start
  57.1 0.0 collective-permute-done.7.h2_ref
  57.1 0.0 copy-start.1
  57.1 0.7 copy-done
  57.8 0.1 copy-done.1
  57.9 15.5 %sweeps.1 = (f32[2,50,32,128]{3,2,1,0:T(8,128)}, f32[2,50,32,128]{3,2,1,0:T(8,128)}, f32[32,128]{1,0:T(8,128)}) custom-call(f32[128,128]{1,0:T(8,128)} %bitcast.4, f32[4,40,256]{2,1,0:T(8,128)} %get-tuple-element.31.vec_ref, f32[40,256]{1,0:T(8,128)} %get-tuple-element.32.lev_ref, f32[2,6,2,32,128]{4,3,2,1,0:T(8,128)} %get-tuple-element.33.side_ref, ...), custom_call_target="tpu_custom_call" | custom-call | tf_op jit(solution)/shard_map/sweeps/pallas_call | solution.py:512
Async XLA Ops:
  10.5 12.4 %collective-permute-start.2 = (f32[6,32,128]{2,1,0:T(8,128)}, f32[6,32,128]{2,1,0:T(8,128)S(1)}, u32[]{:S(2)}, u32[]{:S(2)}) collective-permute-start(f32[6,32,128]{2,1,0:T(8,128)} %get-tuple-element.23), channel_id=1, source_target_pairs={{0,8},{8,0},{16,24},{24,16},{32,40},{40,32},{48,56},{56,48},{64,72... | collective-permute-start | bytes 294920 | tf_op jit(solution)/shard_map/ppermute | solution.py:538
  12.8 10.2 %collective-permute-start.3 = (f32[6,32,128]{2,1,0:T(8,128)}, f32[6,32,128]{2,1,0:T(8,128)S(1)}, u32[]{:S(2)}, u32[]{:S(2)}) collective-permute-start(f32[6,32,128]{2,1,0:T(8,128)} %get-tuple-element.24), channel_id=1, source_target_pairs={{8,16},{16,8},{24,32},{32,24},{40,48},{48,40},{56,64},{64,56},{72,... | collective-permute-start | bytes 294920 | tf_op jit(solution)/shard_map/ppermute | solution.py:539
  16.8 6.1 %collective-permute-start.1 = (f32[32,128]{1,0:T(8,128)}, f32[32,128]{1,0:T(8,128)S(1)}, u32[]{:S(2)}, u32[]{:S(2)}) collective-permute-start(f32[32,128]{1,0:T(8,128)} %get-tuple-element.21), channel_id=1, source_target_pairs={{8,16},{16,8},{24,32},{32,24},{40,48},{48,40},{56,64},{64,56},{72,... | collective-permute-start | bytes 49160 | tf_op jit(solution)/shard_map/ppermute | solution.py:539
  17.5 5.4 %collective-permute-start = (f32[32,128]{1,0:T(8,128)}, f32[32,128]{1,0:T(8,128)S(1)}, u32[]{:S(2)}, u32[]{:S(2)}) collective-permute-start(f32[32,128]{1,0:T(8,128)} %get-tuple-element.21), channel_id=1, source_target_pairs={{0,8},{8,0},{16,24},{24,16},{32,40},{40,32},{48,56},{56,48},{64,72... | collective-permute-start | bytes 49160 | tf_op jit(solution)/shard_map/ppermute | solution.py:538
  23.0 0.6 copy-start.6
  23.0 0.6 copy-start.7
  23.0 0.7 copy-start.2
  23.0 0.7 copy-start.3
  26.1 31.0 %collective-permute-start.6 = (f32[82,8,128]{2,1,0:T(8,128)}, f32[82,8,128]{2,1,0:T(8,128)S(1)}, u32[]{:S(2)}, u32[]{:S(2)}) collective-permute-start(f32[82,8,128]{2,1,0:T(8,128)} %get-tuple-element.34), channel_id=1, source_target_pairs={{0,1},{1,0},{2,3},{3,2},{4,5},{5,4},{6,7},{7,6},{8,9},{9,8},{10,11... | collective-permute-start | bytes 1007624 | tf_op jit(solution)/shard_map/ppermute | solution.py:548
  28.5 28.6 %collective-permute-start.7 = (f32[82,8,128]{2,1,0:T(8,128)}, f32[82,8,128]{2,1,0:T(8,128)S(1)}, u32[]{:S(2)}, u32[]{:S(2)}) collective-permute-start(f32[82,8,128]{2,1,0:T(8,128)} %get-tuple-element.35), channel_id=1, source_target_pairs={{1,2},{2,1},{3,4},{4,3},{5,6},{6,5},{9,10},{10,9},{11,12},{12,11},... | collective-permute-start | bytes 1007624 | tf_op jit(solution)/shard_map/ppermute | solution.py:549
  32.0 4.0 %collective-permute-start.4 = (f32[3,8,256]{2,1,0:T(8,128)}, f32[3,8,256]{2,1,0:T(8,128)S(1)}, u32[]{:S(2)}, u32[]{:S(2)}) collective-permute-start(f32[3,8,256]{2,1,0:T(8,128)} %get-tuple-element.28), channel_id=1, source_target_pairs={{0,1},{1,0},{2,3},{3,2},{4,5},{5,4},{6,7},{7,6},{8,9},{9,8},{10,11... | collective-permute-start | bytes 73736 | tf_op jit(solution)/shard_map/ppermute | solution.py:548
  32.0 5.6 %collective-permute-start.5 = (f32[3,8,256]{2,1,0:T(8,128)}, f32[3,8,256]{2,1,0:T(8,128)S(1)}, u32[]{:S(2)}, u32[]{:S(2)}) collective-permute-start(f32[3,8,256]{2,1,0:T(8,128)} %get-tuple-element.29), channel_id=1, source_target_pairs={{1,2},{2,1},{3,4},{4,3},{5,6},{6,5},{9,10},{10,9},{11,12},{12,11},... | collective-permute-start | bytes 73736 | tf_op jit(solution)/shard_map/ppermute | solution.py:549
  36.0 1.7 %copy-start.4 = (f32[3,8,256]{2,1,0:T(8,128)}, f32[3,8,256]{2,1,0:T(8,128)S(1)}, u32[]{:S(2)}) copy-start(f32[3,8,256]{2,1,0:T(8,128)S(1)} %collective-permute-done.4.s1_ref) | copy-start | bytes 73732
  37.7 0.6 copy-start.5
  57.1 0.7 copy-start
  57.1 0.8 %copy-start.1 = (f32[82,8,128]{2,1,0:T(8,128)}, f32[82,8,128]{2,1,0:T(8,128)S(1)}, u32[]{:S(2)}) copy-start(f32[82,8,128]{2,1,0:T(8,128)S(1)} %collective-permute-done.7.h2_ref) | copy-start | bytes 1007620

commit v2 on v1

v2 whole, which is shorter than its diff:
```python
import math

import jax
import jax.numpy as jnp
from jax import lax
from jax.experimental import pallas as pl
from jax.experimental.pallas import tpu as pltpu
from jax.sharding import PartitionSpec as P

LEVELS = 50
SURFACE_DAMPING = 0.05
COURANT = 0.25
GAINS = (0.7, -0.5)
ROWS = 32
COLS = 128
HALF = LEVELS // 2
SLOTS = 32
FIELDS = 6
GROUPS = -(-LEVELS // 4)
VMEM_LIMIT = 56 * 1024 * 1024
F32 = jnp.float32
VMEM = pltpu.VMEM

PAIRS = tuple((i, j) for i in range(4) for j in range(i, 5))


def iota(shape, dim):
    return lax.broadcasted_iota(jnp.int32, shape, dim)


def pick(parity, even, odd):
    return jnp.where(jnp.broadcast_to(parity, even.shape) == 0, even, odd)


def roll(x, shift, axis):
    return pltpu.roll(x, shift, axis)


def two_sum(a, b):
    s = a + b
    bb = s - a
    return s, (a - (s - bb)) + (b - bb)


def quick_sum(a, b):
    s = a + b
    return s, b - (s - a)


def split(a):
    t = 4097.0 * a
    hi = t - (t - a)
    return hi, a - hi


def two_prod(a, b, sa=None, sb=None):
    ah, al = sa or split(a)
    bh, bl = sb or split(b)
    p = a * b
    return p, ((ah * bh - p) + ah * bl + al * bh) + al * bl


def dd_add(a, b):
    s, e = two_sum(a[0], b[0])
    return quick_sum(s, e + (a[1] + b[1]))


def dd_mul(a, b):
    p, e = two_prod(a[0], b[0])
    return quick_sum(p, e + (a[0] * b[1] + a[1] * b[0]))


def dd_neg(a):
    return -a[0], -a[1]


def dd_inv(a):
    r = 1.0 / a[0]
    p, e = two_prod(a[0], r)
    rest = ((1.0 - p) - e) - a[1] * r
    return quick_sum(r, r * rest)


def solve_kernel(
    lam_h, vel_h, tr_h, dif_h, lams_h, depth_h, lev_h,
    mixed_ref, vel, tr, base_ref, lon1_ref, lon2_ref, slots_ref, g1_ref, g2_ref,
    lam, dif, lams_s, lev_s, w_s, z_s, col_sem, rest_sem,
):
    lon_par = lax.rem(lax.axis_index("lon"), 2)
    lat_par = lax.rem(lax.axis_index("lat"), 2)
    step = 5
    flat = [
        pltpu.make_async_copy(lev_h, lev_s, rest_sem.at[0]),
        pltpu.make_async_copy(lams_h, lams_s, rest_sem.at[1]),
        pltpu.make_async_copy(depth_h, base_ref.at[1], rest_sem.at[2]),
    ]
    copies = []
    for i in range(HALF // step):
        top, low = i * step, LEVELS - (i + 1) * step
        part = []
        for n, at in enumerate((top, low)):
            part.append(pltpu.make_async_copy(dif_h.at[pl.ds(at, step)], dif.at[pl.ds(at, step)], col_sem.at[i, 2 * n]))
            part.append(pltpu.make_async_copy(lam_h.at[:, pl.ds(at, step)], lam.at[:, pl.ds(at, step)], col_sem.at[i, 2 * n + 1]))
        copies.append(part)
    rest = [
        pltpu.make_async_copy(vel_h, vel.at[:, pl.ds(0, LEVELS)], rest_sem.at[3]),
        pltpu.make_async_copy(tr_h, tr.at[:, pl.ds(0, LEVELS)], rest_sem.at[4]),
    ]
    for c in flat + sum(copies, []) + rest:
        c.start()
    for c in flat:
        c.wait()

    lev = lev_s[...]
    zero = jnp.zeros((ROWS, COLS), F32)

    def coef(k):
        return jnp.where(lev > k + 1, dif[k], 0.0)

    def right(n, k):
        return jnp.where(lev > k, lam[n, k], 0.0)

    e = jnp.ones((ROWS, COLS), F32)
    y = [zero, zero]
    w = zero
    eb = e
    yb = [zero, zero]
    wb = zero
    waited = 0
    for k in range(HALF):
        need = min((k + 1) // step, HALF // step - 1)
        while waited <= need:
            for c in copies[waited]:
                c.wait()
            waited += 1
        c_k = coef(k)
        y = [right(n, k) + w * y[n] for n in range(2)]
        inv = 1.0 / (e + c_k)
        w = c_k * inv
        w_s[k] = w
        for n in range(2):
            z_s[n, k] = y[n] * inv
        e = 1.0 + e * w
        if k < HALF - 1:
            m = LEVELS - 1 - k
            c_m = coef(m - 1)
            yb = [right(n, m) + wb * yb[n] for n in range(2)]
            invb = 1.0 / (eb + c_m)
            wb = c_m * invb
            w_s[m] = wb
            for n in range(2):
                z_s[n, m] = yb[n] * invb
            eb = 1.0 + eb * wb
    for c in rest:
        c.wait()

    lane = iota((ROWS, COLS), 1)
    slot = lane // 4
    begun = set()

    def gather(k, fields):
        tile, s = divmod(k, SLOTS)
        here = slot == s
        for i, x in enumerate(fields):
            before = slots_ref[i, tile] if (i, tile) in begun else zero
            begun.add((i, tile))
            slots_ref[i, tile] = jnp.where(here, roll(x, 4 * s + 2, 1), before)

    def level_done(k, solved):
        for n in range(2):
            mixed_ref[n, k] = solved[n]
        gather(k, (solved[0], solved[1], vel[0, k], vel[1, k], tr[0, k], tr[1, k]))

    inv = 1.0 / (e + eb - 1.0)
    below = [(right(n, HALF) + wb * yb[n] + w * y[n]) * inv for n in range(2)]
    total = list(below)
    level_done(HALF, below)
    above = list(below)
    for i in range(1, HALF + 1):
        k = HALF - i
        for n in range(2):
            above[n] = z_s[n, k] + w_s[k] * above[n]
            total[n] = total[n] + above[n]
        level_done(k, above)
        m = HALF + i
        if m < LEVELS:
            for n in range(2):
                below[n] = z_s[n, m] + w_s[m] * below[n]
                total[n] = total[n] + below[n]
            level_done(m, below)
    f = jnp.where(lev > 0, lams_s[...] + (GAINS[0] * total[0] + GAINS[1] * total[1]) / math.sqrt(LEVELS), 0.0)
    levels = lev.astype(F32)
    base_ref[0] = f
    base_ref[2] = levels
    small = jnp.where(lane < 16, roll(f, 8, 1), jnp.where(lane < 32, roll(base_ref[1], 24, 1), roll(levels, 40, 1)))
    lon1_ref[FIELDS] = small
    lon2_ref[FIELDS] = small
    near = lane % 4 < 2
    for i in range(FIELDS):
        a, b = slots_ref[i, 0], slots_ref[i, 1]
        east_edge = jnp.where(near, a, roll(b, 2, 1))
        west_edge = jnp.where(near, roll(a, COLS - 2, 1), b)
        lon1_ref[i] = pick(lon_par, east_edge, west_edge)
        lon2_ref[i] = pick(lon_par, west_edge, east_edge)

    pair = iota((8, COLS), 0) // 2
    for i, src in enumerate((mixed_ref, mixed_ref, vel, vel, tr, tr)):
        for g in range(GROUPS):
            first = jnp.zeros((8, COLS), F32)
            last = first
            for q in range(min(4, LEVELS - 4 * g)):
                top, end = src[i % 2, 4 * g + q, :8], src[i % 2, 4 * g + q, ROWS - 8 :]
                first = jnp.where(pair == q, roll(top, 2 * q, 0) if q else top, first)
                last = jnp.where(pair == (q + 3) % 4, roll(end, 2 * q, 0) if q else end, last)
            g1_ref[i * GROUPS + g] = pick(lat_par, last, first)
            g2_ref[i * GROUPS + g] = pick(lat_par, first, last)


CORNERS = 4
EDGES = FIELDS * GROUPS + CORNERS


def corner_of(index):
    return index // 8, index // 2 % 4, index % 2


def lon_kernel(
    base_ref, o1_ref, o2_ref, slots_ref, g1_ref, g2_ref,
    ext_ref, lat1_ref, s2_ref, h2_ref, side_ref,
):
    lon_par = lax.rem(lax.axis_index("lon"), 2)
    lat_par = lax.rem(lax.axis_index("lat"), 2)
    lane = iota((ROWS, COLS), 1)
    o1, o2 = o1_ref[FIELDS], o2_ref[FIELDS]
    from_east, from_west = pick(lon_par, o1, o2), pick(lon_par, o2, o1)
    for i in range(3):
        own = base_ref[i]
        edge = jnp.where(lane < 16 * i + 8, from_west, from_east)
        edge = roll(edge, COLS - 8 - 16 * i, 1)
        edge = jnp.where((lane < 8) | (lane >= COLS - 8), edge, 0.0)
        ext_ref[i, :, :COLS] = own
        ext_ref[i, :, COLS:] = edge
        for half, here in enumerate((own, edge)):
            first, last = here[:8], here[ROWS - 8 :]
            lat1_ref[EDGES + 2 * i + half] = pick(lat_par, last, first)
            s2_ref[2 * i + half] = pick(lat_par, first, last)
    near = lane % 4 < 2
    for i in range(FIELDS):
        b1, b2 = o1_ref[i], o2_ref[i]
        east, west = pick(lon_par, b1, b2), pick(lon_par, b2, b1)
        own_a, own_b = slots_ref[i, 0], slots_ref[i, 1]
        side_ref[0, i, 0] = jnp.where(near, west, own_a)
        side_ref[0, i, 1] = jnp.where(near, roll(west, COLS - 2, 1), own_b)
        side_ref[1, i, 0] = jnp.where(near, own_a, roll(east, 2, 1))
        side_ref[1, i, 1] = jnp.where(near, own_b, east)
    lat1_ref[: FIELDS * GROUPS] = g1_ref[...]
    h2_ref[: FIELDS * GROUPS] = g2_ref[...]
    pair = iota((8, COLS), 0) // 2
    for c in range(CORNERS):
        first = jnp.zeros((8, COLS), F32)
        last = first
        for q in range(4):
            side, field, tile = corner_of(4 * c + q)
            x = side_ref[side, field, tile]
            first = jnp.where(pair == q, roll(x[:8], 2 * q, 0) if q else x[:8], first)
            last = jnp.where(pair == (q + 3) % 4, roll(x[ROWS - 8 :], 2 * q, 0) if q else x[ROWS - 8 :], last)
        lat1_ref[FIELDS * GROUPS + c] = pick(lat_par, last, first)
        h2_ref[FIELDS * GROUPS + c] = pick(lat_par, first, last)


def krylov_kernel(ext_ref, lat1_ref, s2_ref, vec_ref, lev_ref, gram_ref):
    lat_par = lax.rem(lax.axis_index("lat"), 2)
    rows, cols = ROWS + 16, 2 * COLS
    whole = []
    for i in range(3):
        s1 = jnp.concatenate([lat1_ref[EDGES + 2 * i], lat1_ref[EDGES + 2 * i + 1]], axis=1)
        s2 = jnp.concatenate([s2_ref[2 * i], s2_ref[2 * i + 1]], axis=1)
        whole.append(jnp.concatenate([ext_ref[i], pick(lat_par, s1, s2), pick(lat_par, s2, s1)], axis=0))
    f, depth, lev = whole

    def east(x):
        return roll(x, cols - 1, 1)

    def west(x):
        return roll(x, 1, 1)

    def north(x):
        return roll(x, rows - 1, 0)

    def south(x):
        return roll(x, 1, 0)

    sea = jnp.where(lev > 0.0, 1.0, 0.0)
    face_east = 0.5 * (depth + east(depth)) * sea * east(sea)
    face_north = 0.5 * (depth + north(depth)) * sea * north(sea)
    base = (1.0 - sea) + SURFACE_DAMPING * sea
    sub = iota((8, cols), 0)

    def trim(x):
        return jnp.concatenate([x[:ROWS], jnp.where(sub < 4, x[ROWS : ROWS + 8], x[ROWS + 8 :])], axis=0)

    lev_ref[...] = trim(lev)
    vectors = [f]
    vec_ref[0] = trim(f)
    for i in range(1, 5):
        p = vectors[-1]
        flow_east = face_east * (p - east(p))
        flow_north = face_north * (p - north(p))
        p = base * p + (flow_east - west(flow_east)) + (flow_north - south(flow_north))
        vectors.append(p)
        if i < 4:
            vec_ref[i] = trim(p)
    own = [v[:ROWS, :COLS] for v in vectors]
    parts = [split(v) for v in own]
    row = iota((16, COLS), 0)
    hi = jnp.zeros((16, COLS), F32)
    lo = hi
    for at, (i, j) in enumerate(PAIRS):
        p, e = two_prod(own[i], own[j], parts[i], parts[j])
        quarters = [(p[8 * r : 8 * r + 8], e[8 * r : 8 * r + 8]) for r in range(ROWS // 8)]
        total = dd_add(dd_add(quarters[0], quarters[1]), dd_add(quarters[2], quarters[3]))
        for s in (4, 2, 1):
            total = dd_add(total, (roll(total[0], s, 0), roll(total[1], s, 0)))
        hi = jnp.where(row == at, jnp.concatenate([total[0]] * 2, axis=0), hi)
        lo = jnp.where(row == at, jnp.concatenate([total[1]] * 2, axis=0), lo)
    total = (hi, lo)
    for s in (64, 32, 16, 8, 4, 2, 1):
        total = dd_add(total, (roll(total[0], s, 1), roll(total[1], s, 1)))
    lane = iota((16, COLS), 1)
    line = jnp.where(lane == row, total[0], jnp.where(lane == row + 16, total[1], 0.0))
    line = line[:8] + line[8:]
    for s in (4, 2, 1):
        line = line + roll(line, s, 0)
    gram_ref[...] = jnp.concatenate([line] * (gram_ref.shape[0] // 8), axis=0)


def galerkin(gram):
    rows = gram.shape[0]
    parts = [(gram[8 * r : 8 * r + 8], roll(gram[8 * r : 8 * r + 8], COLS - 16, 1)) for r in range(rows // 8)]
    while len(parts) > 1:
        parts = [dd_add(parts[i], parts[i + 1]) for i in range(0, len(parts) - 1, 2)] + parts[len(parts) // 2 * 2 :]
    total = parts[0]
    for s in (4, 2, 1):
        total = dd_add(total, (roll(total[0], s, 0), roll(total[1], s, 0)))
    entry = {}
    for at, (i, j) in enumerate(PAIRS):
        entry[i, j] = entry[j, i] = tuple(jnp.broadcast_to(t[:, at : at + 1], (8, COLS)) for t in total)
    mat = [[entry[i, j + 1] for j in range(4)] for i in range(4)]
    rhs = [entry[i, 0] for i in range(4)]
    size = [jnp.abs(mat[i][i][0]) for i in range(4)]
    for k in range(4):
        fine = mat[k][k][0] > 1e-12 * size[k]
        inv = dd_inv((jnp.where(fine, mat[k][k][0], 1.0), jnp.where(fine, mat[k][k][1], 0.0)))
        inv = tuple(jnp.where(fine, t, 0.0) for t in inv)
        for j in range(k + 1, 4):
            mat[k][j] = dd_mul(mat[k][j], inv)
        rhs[k] = dd_mul(rhs[k], inv)
        for i in range(k + 1, 4):
            less = dd_neg(mat[i][k])
            for j in range(k + 1, 4):
                mat[i][j] = dd_add(mat[i][j], dd_mul(less, mat[k][j]))
            rhs[i] = dd_add(rhs[i], dd_mul(less, rhs[k]))
    for k in range(2, -1, -1):
        for j in range(k + 1, 4):
            rhs[k] = dd_add(rhs[k], dd_neg(dd_mul(mat[k][j], rhs[j])))
    return [r[0] for r in rhs]


SPANS = ((0, 3), (3, 6), (6, 9), (9, GROUPS))
TALL = ROWS + 8
PADDED = 4 * GROUPS
SPAN_LEVELS = 16
BF16 = jnp.bfloat16


def final_kernel(
    gram_ref, vec_ref, lev_ref, side_ref, h1_ref, h2_ref, mixed, vel, tr,
    adj_h, avel_h, sol_ref,
    adj, avel, sol_s, edge1, edge2, edge3, start_s, lhs, diff, weights, out_sem,
):
    lat_par = lax.rem(lax.axis_index("lat"), 2)
    shape = (COLS, COLS)
    source, target = iota(shape, 0), iota(shape, 1)
    shift = jnp.where(source == target + 1, 1.0, jnp.where(source == target - 1, -1.0, 0.0)).astype(BF16)
    ends = jnp.where(
        (target == COLS - 1) & (source % 2 == 0), 1.0, jnp.where((target == 0) & (source % 2 == 1), -1.0, 0.0)
    ).astype(BF16)
    weights[:COLS] = shift
    weights[COLS : 2 * COLS] = shift
    weights[2 * COLS :] = ends

    coefs = galerkin(gram_ref[...])
    for half in range(2):
        at = half * COLS
        total = 0.0
        for i in range(4):
            wide = jnp.concatenate([coefs[i]] * (TALL // 8), axis=0)
            total = total + wide * vec_ref[i, :, at : at + COLS]
        sol_s[:, at : at + COLS] = total
    sol_ref[...] = sol_s[:ROWS, :COLS]

    lane = iota((TALL, COLS), 1)
    pair = iota((8, COLS), 0) // 2
    even = jnp.broadcast_to(lat_par, (8, COLS)) == 0
    masks = [(pair == q) == even for q in range(4)]

    def edge_rows(index, q):
        x = jnp.where(masks[q], h1_ref[index], h2_ref[index])
        return roll(x, 8 - 2 * q, 0) if q else x

    def parts(x):
        hi = x.astype(BF16)
        return hi, (x - hi.astype(F32)).astype(BF16)

    flux1, flux2 = [], []
    for side in range(2):
        def around(ref):
            own, edge = roll(ref[:, :COLS], 2, 1), roll(ref[:, COLS:], 2, 1)
            x = jnp.where(lane < 2, own, edge) if side else jnp.where(lane < 2, edge, own)
            for s in (4, 8, 16, 32, 64):
                x = jnp.where(lane < s, x, roll(x, s, 1))
            return x

        levels, pressure = around(lev_ref), around(sol_s)
        for tile in range(2):
            def column(field):
                index = side * 8 + field * 2 + tile
                return jnp.concatenate(
                    [side_ref[side, field, tile], edge_rows(FIELDS * GROUPS + index // 4, index % 4)], axis=0
                )

            wet = jnp.where((lane // 4 + tile * SLOTS).astype(F32) < levels, 1.0, 0.0)
            move = COURANT * wet
            u, v = column(2), column(3)
            for n in range(2):
                x = column(n) + GAINS[n] * wet * pressure
                flux = u * x
                flux1.append(flux)
                x = x + move * (roll(flux, COLS - 1, 1) - roll(flux, 1, 1))
                for _ in range(2):
                    flux = v * x
                    x = x + move * (roll(flux, TALL - 1, 0) - roll(flux, 1, 0))
                flux2.append((u * x)[:ROWS])

    def pack(west, east):
        at = iota(east.shape, 1) % 4
        both = jnp.where(at == 2, east, roll(west, 2, 1))
        hi, mid = (t.astype(F32) for t in parts(both))
        return jnp.where(at >= 2, hi, roll(mid, COLS - 2, 1))

    for tile in range(2):
        for n in range(2):
            west, east = tile * 2 + n, 4 + tile * 2 + n
            edge1[tile, n * TALL : (n + 1) * TALL] = pack(flux1[west], flux1[east])
            edge2[tile, n * ROWS : (n + 1) * ROWS] = pack(flux2[west], flux2[east])
            edge3[tile, n * ROWS : (n + 1) * ROWS] = pack(side_ref[0, 4 + n, tile], side_ref[1, 4 + n, tile])

    def meridional(x):
        return roll(x, TALL - 1, 0) - roll(x, 1, 0)

    def tall_field(ref, n, field, g, q):
        return jnp.concatenate([ref[n, 4 * g + q], edge_rows(field * GROUPS + g, q)], axis=0)

    def wet_of(k, rows):
        return jnp.where(k.astype(F32) < lev_ref[:rows, :COLS], 1.0, 0.0)

    def put(at, rows, x, edge, k):
        here = iota(x.shape, 1) // 4 == lax.rem(k, SLOTS)
        hi, mid = parts(x)
        lhs[pl.ds(at, rows), :COLS] = hi
        lhs[pl.ds(at, rows), COLS : 2 * COLS] = mid
        lhs[pl.ds(at, rows), 2 * COLS :] = jnp.where(here, edge[k // SLOTS], 0.0).astype(BF16)

    writes = []
    for lo, hi in SPANS:
        def zonal_first(g, carry, lo=lo):
            for q in range(4):
                k, j = 4 * g + q, 4 * (g - lo) + q
                wet_sol = wet_of(k, TALL) * sol_s[:, :COLS]
                u = tall_field(vel, 0, 2, g, q)
                xs = [tall_field(mixed, n, n, g, q) + GAINS[n] * wet_sol for n in range(2)]
                for n in range(2):
                    start_s[j, n] = xs[n]
                at = pl.multiple_of(j * 2 * TALL, 16)
                put(at, 2 * TALL, jnp.concatenate([u * x for x in xs], axis=0), edge1, k)
            return carry

        def middle(g, carry, lo=lo):
            for q in range(4):
                k, j = 4 * g + q, 4 * (g - lo) + q
                move = COURANT * wet_of(k, TALL)
                v = tall_field(vel, 1, 3, g, q)
                u = vel[0, k]
                fluxes = []
                for n in range(2):
                    x = start_s[j, n] + move * diff[pl.ds(pl.multiple_of(j * 2 * TALL + n * TALL, 8), TALL)]
                    x = x + move * meridional(v * x)
                    x = (x + move * meridional(v * x))[:ROWS]
                    adj[n, k] = x
                    fluxes.append(u * x)
                at = pl.multiple_of(j * 4 * ROWS, 16)
                put(at, 2 * ROWS, jnp.concatenate(fluxes, axis=0), edge2, k)
                put(at + 2 * ROWS, 2 * ROWS, jnp.concatenate([tr[0, k], tr[1, k]], axis=0), edge3, k)
            return carry

        def zonal_last(g, carry, lo=lo):
            for q in range(4):
                k, j = 4 * g + q, 4 * (g - lo) + q
                move = COURANT * wet_of(k, ROWS)
                east_sum, north_sum = 0.0, 0.0
                for n in range(2):
                    at = j * 4 * ROWS + n * ROWS
                    x = adj[n, k] + move * diff[pl.ds(pl.multiple_of(at, 8), ROWS)]
                    adj[n, k] = x
                    east_sum = east_sum + x * diff[pl.ds(pl.multiple_of(at + 2 * ROWS, 8), ROWS)]
                    north_sum = north_sum + x * meridional(tall_field(tr, n, 4 + n, g, q))[:ROWS]
                avel[0, k] = -move * east_sum
                avel[1, k] = -move * north_sum
            return carry

        levels = 4 * (hi - lo)
        lax.fori_loop(lo, hi, zonal_first, 0)
        rows = levels * 2 * TALL
        diff[:rows] = jnp.dot(lhs[:rows], weights[...], preferred_element_type=F32)
        lax.fori_loop(lo, hi, middle, 0)
        rows = levels * 4 * ROWS
        diff[:rows] = jnp.dot(lhs[:rows], weights[...], preferred_element_type=F32)
        lax.fori_loop(lo, hi, zonal_last, 0)
        at, count = 4 * lo, min(4 * hi, LEVELS) - 4 * lo
        for i, (src, dst) in enumerate(((adj, adj_h), (avel, avel_h))):
            copy = pltpu.make_async_copy(
                src.at[:, pl.ds(at, count)], dst.at[:, pl.ds(at, count)], out_sem.at[len(writes) // 2, i]
            )
            copy.start()
            writes.append(copy)
    for copy in writes:
        copy.wait()


def swaps(size, first, periodic):
    out = []
    for i in range(first, size, 2):
        if i + 1 < size or periodic:
            out += [(i, (i + 1) % size), ((i + 1) % size, i)]
    return out


def shape(*dims):
    return jax.ShapeDtypeStruct(dims, F32)


def call(kernel, name, ins, outs, scratch, args):
    here, there = pl.BlockSpec(memory_space=VMEM), pl.BlockSpec(memory_space=pl.ANY)
    args = [a if far else pltpu.with_memory_space_constraint(a, VMEM) for a, far in zip(args, ins)]
    return pl.pallas_call(
        kernel,
        name=name,
        out_shape=tuple(o for o, _ in outs),
        in_specs=[there if far else here for far in ins],
        out_specs=tuple(there if far else here for _, far in outs),
        scratch_shapes=scratch,
        compiler_params=pltpu.CompilerParams(vmem_limit_bytes=VMEM_LIMIT),
    )(*args)


def kept(*dims):
    return VMEM(dims, F32), False


def per_device(lam_tracer, tracer, velocity, diffusivity, lam_surface, sea_depth, levels):
    lon, lat = lax.axis_size("lon"), lax.axis_size("lat")
    tile = (ROWS, COLS)
    deep, padded = (2, LEVELS) + tile, (2, PADDED) + tile
    mixed, vel, tr, base, lon1, lon2, slots, g1, g2 = call(
        solve_kernel, "column_solve", (True,) * 7,
        (kept(*padded), kept(*padded), kept(*padded), kept(3, *tile), kept(FIELDS + 1, *tile), kept(FIELDS + 1, *tile),
         kept(FIELDS, 2, *tile), kept(FIELDS * GROUPS, 8, COLS), kept(FIELDS * GROUPS, 8, COLS)),
        [VMEM(deep, F32), VMEM((LEVELS,) + tile, F32), VMEM(tile, F32), VMEM(tile, jnp.int32),
         VMEM((LEVELS,) + tile, F32), VMEM(deep, F32),
         pltpu.SemaphoreType.DMA((HALF // 5, 4)), pltpu.SemaphoreType.DMA((5,))],
        (lam_tracer, velocity, tracer, diffusivity, lam_surface, sea_depth, levels),
    )
    o1 = lax.ppermute(lon1, "lon", swaps(lon, 0, True))
    o2 = lax.ppermute(lon2, "lon", swaps(lon, 1, True))
    ext, lat1, s2, h2, side = call(
        lon_kernel, "after_lon", (False,) * 6,
        (kept(3, ROWS, 2 * COLS), kept(EDGES + 6, 8, COLS), kept(6, 8, COLS), kept(EDGES, 8, COLS),
         kept(2, FIELDS, 2, *tile)),
        [],
        (base, o1, o2, slots, g1, g2),
    )
    odd_lat = swaps(lat, 1, False)
    lat1 = lax.ppermute(lat1, "lat", swaps(lat, 0, False))
    s2 = lax.ppermute(s2, "lat", odd_lat)
    s2, h2 = lax.optimization_barrier((s2, h2))
    h2 = lax.ppermute(h2, "lat", odd_lat)
    vec, lev, gram = call(
        krylov_kernel, "krylov", (False,) * 3,
        (kept(4, TALL, 2 * COLS), kept(TALL, 2 * COLS), kept(lon * lat, COLS)),
        [],
        (ext, lat1, s2),
    )
    gram = lax.all_to_all(gram, ("lon", "lat"), 0, 0, tiled=True)
    return call(
        final_kernel, "sweeps", (False,) * 9,
        ((shape(*deep), True), (shape(*deep), True), (shape(*tile), False)),
        [VMEM(padded, F32), VMEM(padded, F32), VMEM((TALL, 2 * COLS), F32), VMEM((2, 2 * TALL, COLS), F32),
         VMEM((2, 2 * ROWS, COLS), F32), VMEM((2, 2 * ROWS, COLS), F32), VMEM((SPAN_LEVELS, 2, TALL, COLS), F32),
         VMEM((SPAN_LEVELS * 4 * ROWS, 3 * COLS), BF16), VMEM((SPAN_LEVELS * 4 * ROWS, COLS), F32),
         VMEM((3 * COLS, COLS), BF16), pltpu.SemaphoreType.DMA((len(SPANS), 2))],
        (gram, vec, lev, side, lat1, h2, mixed, vel, tr),
    )


def solution(mesh):
    deep, flat = P(None, None, "lat", "lon"), P("lat", "lon")
    return jax.shard_map(
        per_device,
        mesh=mesh,
        in_specs=(deep, deep, deep, P(None, "lat", "lon"), flat, flat, flat),
        out_specs=(deep, deep, flat),
        check_vma=False,
    )
```

time: 73.8 us -> 64.7 us (0.88)
  blocking collectives: 16 us -> 0 us
  Pallas kernels: 30.6 us -> 19.3 us
  waiting for transfers between devices: 7.13 us -> 13.9 us
  starting transfers between devices: 16.8 us -> 23.5 us
  local copies, waits for them, and re-layouts: 2.11 us -> 7.01 us
    all_to_all x1 -> x0, blocking collectives: 16 us -> none  [per_device(): gram = lax.all_to_all(gram, ('lon', 'lat'), 0, 0, tiled=True)]
    pallas_call x4, Pallas kernels: 30.6 us -> 19.3 us  [call(): pl.pallas_call(kernel, name=name, out_shape=tuple((o for o, _ in outs)),...]
    all_to_all x0 -> x1, waiting for transfers between devices: none -> 9.34 us  [per_device(): gram = lax.all_to_all(gram, ('lon', 'lat'), 0, 0, tiled=True)]
    all_to_all x0 -> x1, starting transfers between devices: none -> 8.37 us  [per_device(): gram = lax.all_to_all(gram, ('lon', 'lat'), 0, 0, tiled=True)]
    unnamed x16 -> x12, local copies, waits for them, and re-layouts: 2.11 us -> 7.01 us
    ppermute x8 -> x5, waiting for transfers between devices: 7.13 us -> 4.57 us  [the longest x1 2.86 us: per_device(): o2 = lax.ppermute(lon2, 'lon', swaps(lon, 1, True))]
    ppermute x8 -> x5, starting transfers between devices: 16.8 us -> 15.2 us  [the longest x1 4.1 us: per_device(): o2 = lax.ppermute(lon2, 'lon', swaps(lon, 1, True))]
  transfers between devices with their start and end apart: 8 -> 6, of which waited for: 2 -> 3; matrix products, arithmetic and copies ran while one was open for 0% -> 0% of each run, Pallas kernels for 4% -> 3%
where the time goes in v2:
time: 64.7 us; the launch traced here: 64.4 us
  starting transfers between devices  23.5 us (36%)
  Pallas kernels  19.3 us (30%)
  waiting for transfers between devices  13.9 us (21%)
  local copies, waits for them, and re-layouts  7.01 us (11%)
  between operations  0.7 us (1%)
    pallas_call x4, Pallas kernels, call(): pl.pallas_call(kernel, name=name, out_shape=tuple((o for o, _ in outs)),...  19.3 us
    all_to_all x1, waiting for transfers between devices, per_device(): gram = lax.all_to_all(gram, ('lon', 'lat'), 0, 0, tiled=True)  9.34 us
    all_to_all x1, starting transfers between devices, per_device(): gram = lax.all_to_all(gram, ('lon', 'lat'), 0, 0, tiled=True)  8.37 us
    unnamed x12, local copies, waits for them, and re-layouts  7.01 us
    ppermute x1, starting transfers between devices, per_device(): o2 = lax.ppermute(lon2, 'lon', swaps(lon, 1, True))  4.1 us
    ppermute x1, starting transfers between devices, per_device(): h2 = lax.ppermute(h2, 'lat', odd_lat)  3.42 us
    ppermute x1, starting transfers between devices, per_device(): s2 = lax.ppermute(s2, 'lat', odd_lat)  3.42 us
    ppermute x1, waiting for transfers between devices, per_device(): o2 = lax.ppermute(lon2, 'lon', swaps(lon, 1, True))  2.86 us
  transfers between devices with their start and end apart: 6, of which 3 were waited for; matrix products, arithmetic and copies ran while one was open for 0% of the time, Pallas kernels for 3%

profile of v2, /device:TPU:1, one launch (start us, length us, event | category | flops | bytes accessed | tf_op | source)
XLA Modules:
  0.0 64.4 jit_solution(2055399623252963859)
XLA Ops:
  0.6 4.7 %column_solve.1 = (f32[2,52,32,128]{3,2,1,0:T(8,128)S(1)}, f32[2,52,32,128]{3,2,1,0:T(8,128)S(1)}, f32[2,52,32,128]{3,2,1,0:T(8,128)S(1)}, f32[3,32,128]{2,1,0:T...) custom-call(f32[2,50,32,128]{3,2,1,0:T(8,128)} %lam_h.1, ...), custom_call_target="tpu_custom_call" | custom-call | tf_op jit(solution)/shard_map/column_solve/pallas_call | solution.py:555
  5.3 0.0 copy-start
  5.3 1.2 %copy-done = f32[2,52,32,128]{3,2,1,0:T(8,128)} copy-done((f32[2,52,32,128]{3,2,1,0:T(8,128)}, f32[2,52,32,128]{3,2,1,0:T(8,128)S(1)}, u32[]{:S(2)}) %copy-start) | copy-done | bytes 1703960
  6.5 0.0 copy-start.2
  6.5 1.2 %copy-done.2 = f32[2,52,32,128]{3,2,1,0:T(8,128)} copy-done((f32[2,52,32,128]{3,2,1,0:T(8,128)}, f32[2,52,32,128]{3,2,1,0:T(8,128)S(1)}, u32[]{:S(2)}) %copy-start.2) | copy-done | bytes 1703960
  7.7 2.1 %collective-permute-start = (f32[7,32,128]{2,1,0:T(8,128)S(1)}, f32[7,32,128]{2,1,0:T(8,128)S(1)}, u32[]{:S(2)}, u32[]{:S(2)}) collective-permute-start(f32[7,32,128]{2,1,0:T(8,128)S(1)} %get-tuple-element.23), channel_id=1, source_target_pairs={{0,8},{8,0},{16,24},{24,16},{32,40},{40,32},{48,56},{56,48},{64,72... | collective-permute-start | bytes 344072 | tf_op jit(solution)/shard_map/ppermute | solution.py:583
  9.8 4.1 %collective-permute-start.1 = (f32[7,32,128]{2,1,0:T(8,128)S(1)}, f32[7,32,128]{2,1,0:T(8,128)S(1)}, u32[]{:S(2)}, u32[]{:S(2)}) collective-permute-start(f32[7,32,128]{2,1,0:T(8,128)S(1)} %get-tuple-element.24), channel_id=1, source_target_pairs={{8,16},{16,8},{24,32},{32,24},{40,48},{48,40},{56,64},{64,56},{72,... | collective-permute-start | bytes 344072 | tf_op jit(solution)/shard_map/ppermute | solution.py:584
  13.9 0.0 collective-permute-done.o1_ref
  13.9 2.9 %collective-permute-done.1.o2_ref = f32[7,32,128]{2,1,0:T(8,128)S(1)} collective-permute-done((f32[7,32,128]{2,1,0:T(8,128)S(1)}, f32[7,32,128]{2,1,0:T(8,128)S(1)}, u32[]{:S(2)}, u32[]{:S(2)}) %collective-permute-start.1) | collective-permute-done | bytes 114720 | tf_op jit(solution)/shard_map/ppermute | solution.py:584
  16.8 0.8 %after_lon.1 = (f32[3,32,256]{2,1,0:T(8,128)S(1)}, f32[88,8,128]{2,1,0:T(8,128)S(1)}, f32[6,8,128]{2,1,0:T(8,128)S(1)}, f32[82,8,128]{2,1,0:T(8,128)}, f32[2,6,2,32,128]{4,3,2,1,0:T(8,128)S(1)}) custom-call(f32[3,32,128]{2,1,0:T(8,128)S(1)} %get-tuple-element.22.base_ref, f32[7,32,128]{2,1,0:T(8,128)S(1)} %collective-permute-done.o1_ref, ...), custom_call_target="tpu_custom_call" | custom-call | tf_op jit(solution)/shard_map/after_lon/pallas_call | solution.py:555
  17.6 2.1 %collective-permute-start.2 = (f32[88,8,128]{2,1,0:T(8,128)S(1)}, f32[88,8,128]{2,1,0:T(8,128)S(1)}, u32[]{:S(2)}, u32[]{:S(2)}) collective-permute-start(f32[88,8,128]{2,1,0:T(8,128)S(1)} %get-tuple-element.29), channel_id=1, source_target_pairs={{0,1},{1,0},{2,3},{3,2},{4,5},{5,4},{6,7},{7,6},{8,9},{9,8},{10,11... | collective-permute-start | bytes 1081352 | tf_op jit(solution)/shard_map/ppermute | solution.py:593
  19.7 3.4 %collective-permute-start.3 = (f32[6,8,128]{2,1,0:T(8,128)S(1)}, f32[6,8,128]{2,1,0:T(8,128)S(1)}, u32[]{:S(2)}, u32[]{:S(2)}) collective-permute-start(f32[6,8,128]{2,1,0:T(8,128)S(1)} %get-tuple-element.30), channel_id=1, source_target_pairs={{1,2},{2,1},{3,4},{4,3},{5,6},{6,5},{9,10},{10,9},{11,12},{12,11},... | collective-permute-start | bytes 73736 | tf_op jit(solution)/shard_map/ppermute | solution.py:594
  23.2 1.7 %collective-permute-done.3.s2_ref = f32[6,8,128]{2,1,0:T(8,128)S(1)} collective-permute-done((f32[6,8,128]{2,1,0:T(8,128)S(1)}, f32[6,8,128]{2,1,0:T(8,128)S(1)}, u32[]{:S(2)}, u32[]{:S(2)}) %collective-permute-start.3) | collective-permute-done | bytes 24608 | tf_op jit(solution)/shard_map/ppermute | solution.py:594
  24.9 3.4 %collective-permute-start.4 = (f32[82,8,128]{2,1,0:T(8,128)}, f32[82,8,128]{2,1,0:T(8,128)S(1)}, u32[]{:S(2)}, u32[]{:S(2)}) collective-permute-start(f32[82,8,128]{2,1,0:T(8,128)} %get-tuple-element.37), channel_id=1, source_target_pairs={{1,2},{2,1},{3,4},{4,3},{5,6},{6,5},{9,10},{10,9},{11,12},{12,11},... | collective-permute-start | bytes 1007624 | tf_op jit(solution)/shard_map/ppermute | solution.py:596
  28.3 0.0 collective-permute-done.2.lat1_ref.h1_ref
  28.3 1.8 %krylov.1 = (f32[4,40,256]{2,1,0:T(8,128)S(1)}, f32[40,256]{1,0:T(8,128)S(1)}, f32[128,128]{1,0:T(8,128)}) custom-call(f32[3,32,256]{2,1,0:T(8,128)S(1)} %get-tuple-element.28.ext_ref, f32[88,8,128]{2,1,0:T(8,128)S(1)} %collective-permute-done.2.lat1_ref.h1_ref, f32[6,8,128]{2,1,0:T(8,128)S(1)} %collective-permute-done.3.s2_ref), custom_call_target="tpu_custom_call" | custom-call | tf_op jit(solution)/shard_map/krylov/pallas_call | solution.py:555
  30.1 0.0 copy-start.4
  30.1 0.7 %copy-done.4 = f32[88,8,128]{2,1,0:T(8,128)} copy-done((f32[88,8,128]{2,1,0:T(8,128)}, f32[88,8,128]{2,1,0:T(8,128)S(1)}, u32[]{:S(2)}) %copy-start.4) | copy-done | bytes 360472
  30.9 8.4 %all-to-all-start = ((f32[128,1,128]{2,1,0:T(1,128)}), f32[128,1,128]{2,1,0:T(1,128)S(1)}, u32[]{:S(2)}, u32[]{:S(2)}) async-start(f32[128,1,128]{2,1,0:T(1,128)} %bitcast.1), calls=%async_computation | async-start | bytes 131072 | tf_op jit(solution)/shard_map/all_to_all | solution.py:603
  39.3 0.0 collective-permute-done.4.h2_ref
  39.3 9.3 %all-to-all-done = f32[128,1,128]{2,1,0:T(1,128)S(1)} async-done(((f32[128,1,128]{2,1,0:T(1,128)}), f32[128,1,128]{2,1,0:T(1,128)S(1)}, u32[]{:S(2)}, u32[]{:S(2)}) %all-to-all-start) | async-done | bytes 65568 | tf_op jit(solution)/shard_map/all_to_all | solution.py:603
  48.6 0.0 copy-start.1
  48.6 1.5 %copy-done.1 = f32[2,52,32,128]{3,2,1,0:T(8,128)S(1)} copy-done((f32[2,52,32,128]{3,2,1,0:T(8,128)S(1)}, f32[2,52,32,128]{3,2,1,0:T(8,128)}, u32[]{:S(2)}) %copy-start.1) | copy-done | bytes 1703960
  50.1 0.0 copy-start.3
  50.1 1.5 %copy-done.3 = f32[2,52,32,128]{3,2,1,0:T(8,128)S(1)} copy-done((f32[2,52,32,128]{3,2,1,0:T(8,128)S(1)}, f32[2,52,32,128]{3,2,1,0:T(8,128)}, u32[]{:S(2)}) %copy-start.3) | copy-done | bytes 1703960
  51.5 0.0 copy-start.5
  51.5 1.0 %copy-done.5 = f32[88,8,128]{2,1,0:T(8,128)S(1)} copy-done((f32[88,8,128]{2,1,0:T(8,128)S(1)}, f32[88,8,128]{2,1,0:T(8,128)}, u32[]{:S(2)}) %copy-start.5) | copy-done | bytes 360472
  52.5 11.9 %sweeps.1 = (f32[2,50,32,128]{3,2,1,0:T(8,128)}, f32[2,50,32,128]{3,2,1,0:T(8,128)}, f32[32,128]{1,0:T(8,128)}) custom-call(f32[128,128]{1,0:T(8,128)S(1)} %bitcast.4, f32[4,40,256]{2,1,0:T(8,128)S(1)} %get-tuple-element.34.vec_ref, f32[40,256]{1,0:T(8,128)S(1)} %get-tuple-element.35.lev_ref, f32[2,6,2,32,128]{4,3,2,1,0:T(8,128)S(1)} %get-tuple-element.36.side_ref, ...), custom_call_target="tpu_custom_call" | custom-call | tf_op jit(solution)/shard_map/sweeps/pallas_call | solution.py:555
Async XLA Ops:
  5.3 1.2 %copy-start = (f32[2,52,32,128]{3,2,1,0:T(8,128)}, f32[2,52,32,128]{3,2,1,0:T(8,128)S(1)}, u32[]{:S(2)}) copy-start(f32[2,52,32,128]{3,2,1,0:T(8,128)S(1)} %get-tuple-element.39.vel) | copy-start | bytes 5111812
  6.5 1.2 %copy-start.2 = (f32[2,52,32,128]{3,2,1,0:T(8,128)}, f32[2,52,32,128]{3,2,1,0:T(8,128)S(1)}, u32[]{:S(2)}) copy-start(f32[2,52,32,128]{3,2,1,0:T(8,128)S(1)} %get-tuple-element.40.tr) | copy-start | bytes 5111812
  7.7 6.2 %collective-permute-start = (f32[7,32,128]{2,1,0:T(8,128)S(1)}, f32[7,32,128]{2,1,0:T(8,128)S(1)}, u32[]{:S(2)}, u32[]{:S(2)}) collective-permute-start(f32[7,32,128]{2,1,0:T(8,128)S(1)} %get-tuple-element.23), channel_id=1, source_target_pairs={{0,8},{8,0},{16,24},{24,16},{32,40},{40,32},{48,56},{56,48},{64,72... | collective-permute-start | bytes 344072 | tf_op jit(solution)/shard_map/ppermute | solution.py:583
  9.8 7.0 %collective-permute-start.1 = (f32[7,32,128]{2,1,0:T(8,128)S(1)}, f32[7,32,128]{2,1,0:T(8,128)S(1)}, u32[]{:S(2)}, u32[]{:S(2)}) collective-permute-start(f32[7,32,128]{2,1,0:T(8,128)S(1)} %get-tuple-element.24), channel_id=1, source_target_pairs={{8,16},{16,8},{24,32},{32,24},{40,48},{48,40},{56,64},{64,56},{72,... | collective-permute-start | bytes 344072 | tf_op jit(solution)/shard_map/ppermute | solution.py:584
  17.6 10.7 %collective-permute-start.2 = (f32[88,8,128]{2,1,0:T(8,128)S(1)}, f32[88,8,128]{2,1,0:T(8,128)S(1)}, u32[]{:S(2)}, u32[]{:S(2)}) collective-permute-start(f32[88,8,128]{2,1,0:T(8,128)S(1)} %get-tuple-element.29), channel_id=1, source_target_pairs={{0,1},{1,0},{2,3},{3,2},{4,5},{5,4},{6,7},{7,6},{8,9},{9,8},{10,11... | collective-permute-start | bytes 1081352 | tf_op jit(solution)/shard_map/ppermute | solution.py:593
  19.7 5.1 %collective-permute-start.3 = (f32[6,8,128]{2,1,0:T(8,128)S(1)}, f32[6,8,128]{2,1,0:T(8,128)S(1)}, u32[]{:S(2)}, u32[]{:S(2)}) collective-permute-start(f32[6,8,128]{2,1,0:T(8,128)S(1)} %get-tuple-element.30), channel_id=1, source_target_pairs={{1,2},{2,1},{3,4},{4,3},{5,6},{6,5},{9,10},{10,9},{11,12},{12,11},... | collective-permute-start | bytes 73736 | tf_op jit(solution)/shard_map/ppermute | solution.py:594
  24.9 14.4 %collective-permute-start.4 = (f32[82,8,128]{2,1,0:T(8,128)}, f32[82,8,128]{2,1,0:T(8,128)S(1)}, u32[]{:S(2)}, u32[]{:S(2)}) collective-permute-start(f32[82,8,128]{2,1,0:T(8,128)} %get-tuple-element.37), channel_id=1, source_target_pairs={{1,2},{2,1},{3,4},{4,3},{5,6},{6,5},{9,10},{10,9},{11,12},{12,11},... | collective-permute-start | bytes 1007624 | tf_op jit(solution)/shard_map/ppermute | solution.py:596
  30.1 0.7 %copy-start.4 = (f32[88,8,128]{2,1,0:T(8,128)}, f32[88,8,128]{2,1,0:T(8,128)S(1)}, u32[]{:S(2)}) copy-start(f32[88,8,128]{2,1,0:T(8,128)S(1)} %collective-permute-done.2.lat1_ref.h1_ref) | copy-start | bytes 1081348
  30.9 17.7 %all-to-all-start = ((f32[128,1,128]{2,1,0:T(1,128)}), f32[128,1,128]{2,1,0:T(1,128)S(1)}, u32[]{:S(2)}, u32[]{:S(2)}) async-start(f32[128,1,128]{2,1,0:T(1,128)} %bitcast.1), calls=%async_computation | async-start | bytes 131072 | tf_op jit(solution)/shard_map/all_to_all | solution.py:603
  48.6 1.5 %copy-start.1 = (f32[2,52,32,128]{3,2,1,0:T(8,128)S(1)}, f32[2,52,32,128]{3,2,1,0:T(8,128)}, u32[]{:S(2)}) copy-start(f32[2,52,32,128]{3,2,1,0:T(8,128)} %copy-done) | copy-start | bytes 5111812
  50.1 1.5 %copy-start.3 = (f32[2,52,32,128]{3,2,1,0:T(8,128)S(1)}, f32[2,52,32,128]{3,2,1,0:T(8,128)}, u32[]{:S(2)}) copy-start(f32[2,52,32,128]{3,2,1,0:T(8,128)} %copy-done.2) | copy-start | bytes 5111812
  51.5 1.0 %copy-start.5 = (f32[88,8,128]{2,1,0:T(8,128)S(1)}, f32[88,8,128]{2,1,0:T(8,128)}, u32[]{:S(2)}) copy-start(f32[88,8,128]{2,1,0:T(8,128)} %copy-done.4) | copy-start | bytes 1081348

commit v3 on v2

--- a/solution.py
+++ b/solution.py
@@ -17,7 +17,7 @@
 SLOTS = 32
 FIELDS = 6
 GROUPS = -(-LEVELS // 4)
-VMEM_LIMIT = 56 * 1024 * 1024
+VMEM_LIMIT = 12 * 1024 * 1024
 F32 = jnp.float32
 VMEM = pltpu.VMEM
 
@@ -103,8 +103,8 @@
             part.append(pltpu.make_async_copy(lam_h.at[:, pl.ds(at, step)], lam.at[:, pl.ds(at, step)], col_sem.at[i, 2 * n + 1]))
         copies.append(part)
     rest = [
-        pltpu.make_async_copy(vel_h, vel.at[:, pl.ds(0, LEVELS)], rest_sem.at[3]),
-        pltpu.make_async_copy(tr_h, tr.at[:, pl.ds(0, LEVELS)], rest_sem.at[4]),
+        pltpu.make_async_copy(vel_h, vel, rest_sem.at[3]),
+        pltpu.make_async_copy(tr_h, tr, rest_sem.at[4]),
     ]
     for c in flat + sum(copies, []) + rest:
         c.start()
@@ -224,10 +224,7 @@
     return index // 8, index // 2 % 4, index % 2
 
 
-def lon_kernel(
-    base_ref, o1_ref, o2_ref, slots_ref, g1_ref, g2_ref,
-    ext_ref, lat1_ref, s2_ref, h2_ref, side_ref,
-):
+def flat_kernel(base_ref, o1_ref, o2_ref, ext_ref, s1_ref, s2_ref):
     lon_par = lax.rem(lax.axis_index("lon"), 2)
     lat_par = lax.rem(lax.axis_index("lat"), 2)
     lane = iota((ROWS, COLS), 1)
@@ -242,9 +239,14 @@
         ext_ref[i, :, COLS:] = edge
         for half, here in enumerate((own, edge)):
             first, last = here[:8], here[ROWS - 8 :]
-            lat1_ref[EDGES + 2 * i + half] = pick(lat_par, last, first)
+            s1_ref[2 * i + half] = pick(lat_par, last, first)
             s2_ref[2 * i + half] = pick(lat_par, first, last)
-    near = lane % 4 < 2
+
+
+def deep_kernel(s1_ref, o1_ref, o2_ref, slots_ref, g1_ref, g2_ref, lat1_ref, h2_ref, side_ref):
+    lon_par = lax.rem(lax.axis_index("lon"), 2)
+    lat_par = lax.rem(lax.axis_index("lat"), 2)
+    near = iota((ROWS, COLS), 1) % 4 < 2
     for i in range(FIELDS):
         b1, b2 = o1_ref[i], o2_ref[i]
         east, west = pick(lon_par, b1, b2), pick(lon_par, b2, b1)
@@ -254,6 +256,7 @@
         side_ref[1, i, 0] = jnp.where(near, own_a, roll(east, 2, 1))
         side_ref[1, i, 1] = jnp.where(near, own_b, east)
     lat1_ref[: FIELDS * GROUPS] = g1_ref[...]
+    lat1_ref[EDGES:] = s1_ref[...]
     h2_ref[: FIELDS * GROUPS] = g2_ref[...]
     pair = iota((8, COLS), 0) // 2
     for c in range(CORNERS):
@@ -366,10 +369,9 @@
     return [r[0] for r in rhs]
 
 
-SPANS = ((0, 3), (3, 6), (6, 9), (9, GROUPS))
+SPANS = ((0, 12), (12, 25), (25, 38), (38, LEVELS))
 TALL = ROWS + 8
-PADDED = 4 * GROUPS
-SPAN_LEVELS = 16
+SPAN_LEVELS = 13
 BF16 = jnp.bfloat16
 
 
@@ -458,78 +460,71 @@
     def meridional(x):
         return roll(x, TALL - 1, 0) - roll(x, 1, 0)
 
-    def tall_field(ref, n, field, g, q):
-        return jnp.concatenate([ref[n, 4 * g + q], edge_rows(field * GROUPS + g, q)], axis=0)
+    def tall_field(ref, n, field, k):
+        return jnp.concatenate([ref[n, k], edge_rows(field * GROUPS + k // 4, k % 4)], axis=0)
 
     def wet_of(k, rows):
-        return jnp.where(k.astype(F32) < lev_ref[:rows, :COLS], 1.0, 0.0)
+        return jnp.where(float(k) < lev_ref[:rows, :COLS], 1.0, 0.0)
 
     def put(at, rows, x, edge, k):
-        here = iota(x.shape, 1) // 4 == lax.rem(k, SLOTS)
+        here = iota(x.shape, 1) // 4 == k % SLOTS
         hi, mid = parts(x)
         lhs[pl.ds(at, rows), :COLS] = hi
         lhs[pl.ds(at, rows), COLS : 2 * COLS] = mid
         lhs[pl.ds(at, rows), 2 * COLS :] = jnp.where(here, edge[k // SLOTS], 0.0).astype(BF16)
 
     writes = []
-    for lo, hi in SPANS:
-        def zonal_first(g, carry, lo=lo):
-            for q in range(4):
-                k, j = 4 * g + q, 4 * (g - lo) + q
-                wet_sol = wet_of(k, TALL) * sol_s[:, :COLS]
-                u = tall_field(vel, 0, 2, g, q)
-                xs = [tall_field(mixed, n, n, g, q) + GAINS[n] * wet_sol for n in range(2)]
-                for n in range(2):
-                    start_s[j, n] = xs[n]
-                at = pl.multiple_of(j * 2 * TALL, 16)
-                put(at, 2 * TALL, jnp.concatenate([u * x for x in xs], axis=0), edge1, k)
-            return carry
-
-        def middle(g, carry, lo=lo):
-            for q in range(4):
-                k, j = 4 * g + q, 4 * (g - lo) + q
-                move = COURANT * wet_of(k, TALL)
-                v = tall_field(vel, 1, 3, g, q)
-                u = vel[0, k]
-                fluxes = []
-                for n in range(2):
-                    x = start_s[j, n] + move * diff[pl.ds(pl.multiple_of(j * 2 * TALL + n * TALL, 8), TALL)]
-                    x = x + move * meridional(v * x)
-                    x = (x + move * meridional(v * x))[:ROWS]
-                    adj[n, k] = x
-                    fluxes.append(u * x)
-                at = pl.multiple_of(j * 4 * ROWS, 16)
-                put(at, 2 * ROWS, jnp.concatenate(fluxes, axis=0), edge2, k)
-                put(at + 2 * ROWS, 2 * ROWS, jnp.concatenate([tr[0, k], tr[1, k]], axis=0), edge3, k)
-            return carry
-
-        def zonal_last(g, carry, lo=lo):
-            for q in range(4):
-                k, j = 4 * g + q, 4 * (g - lo) + q
-                move = COURANT * wet_of(k, ROWS)
-                east_sum, north_sum = 0.0, 0.0
-                for n in range(2):
-                    at = j * 4 * ROWS + n * ROWS
-                    x = adj[n, k] + move * diff[pl.ds(pl.multiple_of(at, 8), ROWS)]
-                    adj[n, k] = x
-                    east_sum = east_sum + x * diff[pl.ds(pl.multiple_of(at + 2 * ROWS, 8), ROWS)]
-                    north_sum = north_sum + x * meridional(tall_field(tr, n, 4 + n, g, q))[:ROWS]
-                avel[0, k] = -move * east_sum
-                avel[1, k] = -move * north_sum
-            return carry
-
-        levels = 4 * (hi - lo)
-        lax.fori_loop(lo, hi, zonal_first, 0)
+    for first, last in SPANS:
+        def zonal_first(k, j):
+            wet_sol = wet_of(k, TALL) * sol_s[:, :COLS]
+            u = tall_field(vel, 0, 2, k)
+            xs = [tall_field(mixed, n, n, k) + GAINS[n] * wet_sol for n in range(2)]
+            for n in range(2):
+                start_s[j, n] = xs[n]
+            at = j * 2 * TALL
+            put(at, 2 * TALL, jnp.concatenate([u * x for x in xs], axis=0), edge1, k)
+
+        def middle(k, j):
+            move = COURANT * wet_of(k, TALL)
+            v = tall_field(vel, 1, 3, k)
+            u = vel[0, k]
+            fluxes = []
+            for n in range(2):
+                x = start_s[j, n] + move * diff[pl.ds((2 * j + n) * TALL, TALL)]
+                x = x + move * meridional(v * x)
+                x = (x + move * meridional(v * x))[:ROWS]
+                adj[n, k] = x
+                fluxes.append(u * x)
+            at = j * 4 * ROWS
+            put(at, 2 * ROWS, jnp.concatenate(fluxes, axis=0), edge2, k)
+            put(at + 2 * ROWS, 2 * ROWS, jnp.concatenate([tr[0, k], tr[1, k]], axis=0), edge3, k)
+
+        def zonal_last(k, j):
+            move = COURANT * wet_of(k, ROWS)
+            east_sum, north_sum = 0.0, 0.0
+            for n in range(2):
+                at = j * 4 * ROWS + n * ROWS
+                x = adj[n, k] + move * diff[pl.ds(at, ROWS)]
+                adj[n, k] = x
+                east_sum = east_sum + x * diff[pl.ds(at + 2 * ROWS, ROWS)]
+                north_sum = north_sum + x * meridional(tall_field(tr, n, 4 + n, k))[:ROWS]
+            avel[0, k] = -move * east_sum
+            avel[1, k] = -move * north_sum
+
+        levels = last - first
+        for k in range(first, last):
+            zonal_first(k, k - first)
         rows = levels * 2 * TALL
         diff[:rows] = jnp.dot(lhs[:rows], weights[...], preferred_element_type=F32)
-        lax.fori_loop(lo, hi, middle, 0)
+        for k in range(first, last):
+            middle(k, k - first)
         rows = levels * 4 * ROWS
         diff[:rows] = jnp.dot(lhs[:rows], weights[...], preferred_element_type=F32)
-        lax.fori_loop(lo, hi, zonal_last, 0)
-        at, count = 4 * lo, min(4 * hi, LEVELS) - 4 * lo
+        for k in range(first, last):
+            zonal_last(k, k - first)
         for i, (src, dst) in enumerate(((adj, adj_h), (avel, avel_h))):
             copy = pltpu.make_async_copy(
-                src.at[:, pl.ds(at, count)], dst.at[:, pl.ds(at, count)], out_sem.at[len(writes) // 2, i]
+                src.at[:, pl.ds(first, levels)], dst.at[:, pl.ds(first, levels)], out_sem.at[len(writes) // 2, i]
             )
             copy.start()
             writes.append(copy)
@@ -550,8 +545,8 @@
 
 
 def call(kernel, name, ins, outs, scratch, args):
-    here, there = pl.BlockSpec(memory_space=VMEM), pl.BlockSpec(memory_space=pl.ANY)
-    args = [a if far else pltpu.with_memory_space_constraint(a, VMEM) for a, far in zip(args, ins)]
+    here, there = pl.BlockSpec(memory_space=VMEM), pl.BlockSpec(memory_space=pltpu.HBM)
+    args = [pltpu.with_memory_space_constraint(a, pltpu.HBM if far else VMEM) for a, far in zip(args, ins)]
     return pl.pallas_call(
         kernel,
         name=name,
@@ -570,10 +565,10 @@
 def per_device(lam_tracer, tracer, velocity, diffusivity, lam_surface, sea_depth, levels):
     lon, lat = lax.axis_size("lon"), lax.axis_size("lat")
     tile = (ROWS, COLS)
-    deep, padded = (2, LEVELS) + tile, (2, PADDED) + tile
+    deep = (2, LEVELS) + tile
     mixed, vel, tr, base, lon1, lon2, slots, g1, g2 = call(
         solve_kernel, "column_solve", (True,) * 7,
-        (kept(*padded), kept(*padded), kept(*padded), kept(3, *tile), kept(FIELDS + 1, *tile), kept(FIELDS + 1, *tile),
+        (kept(*deep), kept(*deep), kept(*deep), kept(3, *tile), kept(FIELDS + 1, *tile), kept(FIELDS + 1, *tile),
          kept(FIELDS, 2, *tile), kept(FIELDS * GROUPS, 8, COLS), kept(FIELDS * GROUPS, 8, COLS)),
         [VMEM(deep, F32), VMEM((LEVELS,) + tile, F32), VMEM(tile, F32), VMEM(tile, jnp.int32),
          VMEM((LEVELS,) + tile, F32), VMEM(deep, F32),
@@ -582,17 +577,21 @@
     )
     o1 = lax.ppermute(lon1, "lon", swaps(lon, 0, True))
     o2 = lax.ppermute(lon2, "lon", swaps(lon, 1, True))
-    ext, lat1, s2, h2, side = call(
-        lon_kernel, "after_lon", (False,) * 6,
-        (kept(3, ROWS, 2 * COLS), kept(EDGES + 6, 8, COLS), kept(6, 8, COLS), kept(EDGES, 8, COLS),
-         kept(2, FIELDS, 2, *tile)),
+    ext, s1, s2 = call(
+        flat_kernel, "flat_edges", (False,) * 3,
+        (kept(3, ROWS, 2 * COLS), kept(6, 8, COLS), kept(6, 8, COLS)),
         [],
-        (base, o1, o2, slots, g1, g2),
+        (base, o1, o2),
+    )
+    lat1, h2, side = call(
+        deep_kernel, "deep_edges", (False,) * 6,
+        (kept(EDGES + 6, 8, COLS), kept(EDGES, 8, COLS), kept(2, FIELDS, 2, *tile)),
+        [],
+        (s1, o1, o2, slots, g1, g2),
     )
     odd_lat = swaps(lat, 1, False)
+    s2 = lax.ppermute(s2, "lat", odd_lat)
     lat1 = lax.ppermute(lat1, "lat", swaps(lat, 0, False))
-    s2 = lax.ppermute(s2, "lat", odd_lat)
-    s2, h2 = lax.optimization_barrier((s2, h2))
     h2 = lax.ppermute(h2, "lat", odd_lat)
     vec, lev, gram = call(
         krylov_kernel, "krylov", (False,) * 3,
@@ -604,7 +603,7 @@
     return call(
         final_kernel, "sweeps", (False,) * 9,
         ((shape(*deep), True), (shape(*deep), True), (shape(*tile), False)),
-        [VMEM(padded, F32), VMEM(padded, F32), VMEM((TALL, 2 * COLS), F32), VMEM((2, 2 * TALL, COLS), F32),
+        [VMEM(deep, F32), VMEM(deep, F32), VMEM((TALL, 2 * COLS), F32), VMEM((2, 2 * TALL, COLS), F32),
          VMEM((2, 2 * ROWS, COLS), F32), VMEM((2, 2 * ROWS, COLS), F32), VMEM((SPAN_LEVELS, 2, TALL, COLS), F32),
          VMEM((SPAN_LEVELS * 4 * ROWS, 3 * COLS), BF16), VMEM((SPAN_LEVELS * 4 * ROWS, COLS), F32),
          VMEM((3 * COLS, COLS), BF16), pltpu.SemaphoreType.DMA((len(SPANS), 2))],

time: 64.7 us -> 60.2 us (0.930)
  Pallas kernels: 19.3 us -> 15.1 us
  waiting for transfers between devices: 13.9 us -> 15.6 us
  local copies, waits for them, and re-layouts: 7.01 us -> 5.92 us
  starting transfers between devices: 23.5 us -> 22.6 us
    pallas_call x4 -> x5, Pallas kernels: 19.3 us -> 15.1 us  [call(): pl.pallas_call(kernel, name=name, out_shape=tuple((o for o, _ in outs)),...]
    ppermute x1, waiting for transfers between devices: 1.7 us -> 3.38 us  [per_device(): s2 = lax.ppermute(s2, 'lat', odd_lat)]
    ppermute x1, starting transfers between devices: 3.42 us -> 2.13 us  [per_device(): s2 = lax.ppermute(s2, 'lat', odd_lat)]
    unnamed x12 -> x14, local copies, waits for them, and re-layouts: 7.01 us -> 5.92 us
  transfers between devices with their start and end apart: 6 -> 6, of which waited for: 3 -> 3; matrix products, arithmetic and copies ran while one was open for 0% -> 0% of each run, Pallas kernels for 3% -> 2%
where the time goes in v3:
time: 60.2 us; the launch traced here: 59.9 us
  starting transfers between devices  22.6 us (38%)
  waiting for transfers between devices  15.6 us (26%)
  Pallas kernels  15.1 us (25%)
  local copies, waits for them, and re-layouts  5.92 us (10%)
  between operations  0.72 us (1%)
    pallas_call x5, Pallas kernels, call(): pl.pallas_call(kernel, name=name, out_shape=tuple((o for o, _ in outs)),...  15.1 us
    all_to_all x1, waiting for transfers between devices, per_device(): gram = lax.all_to_all(gram, ('lon', 'lat'), 0, 0, tiled=True)  9.34 us
    all_to_all x1, starting transfers between devices, per_device(): gram = lax.all_to_all(gram, ('lon', 'lat'), 0, 0, tiled=True)  8.72 us
    unnamed x14, local copies, waits for them, and re-layouts  5.92 us
    ppermute x1, starting transfers between devices, per_device(): o2 = lax.ppermute(lon2, 'lon', swaps(lon, 1, True))  4.1 us
    ppermute x1, starting transfers between devices, per_device(): h2 = lax.ppermute(h2, 'lat', odd_lat)  3.42 us
    ppermute x1, waiting for transfers between devices, per_device(): s2 = lax.ppermute(s2, 'lat', odd_lat)  3.38 us
    ppermute x1, waiting for transfers between devices, per_device(): o2 = lax.ppermute(lon2, 'lon', swaps(lon, 1, True))  2.86 us
  transfers between devices with their start and end apart: 6, of which 3 were waited for; matrix products, arithmetic and copies ran while one was open for 0% of the time, Pallas kernels for 2%

profile of v3, /device:TPU:1, one launch (start us, length us, event | category | flops | bytes accessed | tf_op | source)
XLA Modules:
  0.0 59.9 jit_solution(4956742926573753819)
XLA Ops:
  0.6 4.7 %column_solve.1 = (f32[2,50,32,128]{3,2,1,0:T(8,128)S(1)}, f32[2,50,32,128]{3,2,1,0:T(8,128)S(1)}, f32[2,50,32,128]{3,2,1,0:T(8,128)S(1)}, f32[3,32,128]{2,1,0:T...) custom-call(f32[2,50,32,128]{3,2,1,0:T(8,128)} %lam_h.1, ...), custom_call_target="tpu_custom_call" | custom-call | tf_op jit(solution)/shard_map/column_solve/pallas_call | solution.py:550
  5.3 0.0 copy-start
  5.3 1.2 %copy-done = f32[2,50,32,128]{3,2,1,0:T(8,128)} copy-done((f32[2,50,32,128]{3,2,1,0:T(8,128)}, f32[2,50,32,128]{3,2,1,0:T(8,128)S(1)}, u32[]{:S(2)}) %copy-start) | copy-done | bytes 1638424
  6.5 2.1 %collective-permute-start = (f32[7,32,128]{2,1,0:T(8,128)S(1)}, f32[7,32,128]{2,1,0:T(8,128)S(1)}, u32[]{:S(2)}, u32[]{:S(2)}) collective-permute-start(f32[7,32,128]{2,1,0:T(8,128)S(1)} %get-tuple-element.22), channel_id=1, source_target_pairs={{0,8},{8,0},{16,24},{24,16},{32,40},{40,32},{48,56},{56,48},{64,72... | collective-permute-start | bytes 344072 | tf_op jit(solution)/shard_map/ppermute | solution.py:578
  8.6 4.1 %collective-permute-start.1 = (f32[7,32,128]{2,1,0:T(8,128)S(1)}, f32[7,32,128]{2,1,0:T(8,128)S(1)}, u32[]{:S(2)}, u32[]{:S(2)}) collective-permute-start(f32[7,32,128]{2,1,0:T(8,128)S(1)} %get-tuple-element.23), channel_id=1, source_target_pairs={{8,16},{16,8},{24,32},{32,24},{40,48},{48,40},{56,64},{64,56},{72,... | collective-permute-start | bytes 344072 | tf_op jit(solution)/shard_map/ppermute | solution.py:579
  12.7 0.0 collective-permute-done.o1_ref
  12.7 2.9 %collective-permute-done.1.o2_ref = f32[7,32,128]{2,1,0:T(8,128)S(1)} collective-permute-done((f32[7,32,128]{2,1,0:T(8,128)S(1)}, f32[7,32,128]{2,1,0:T(8,128)S(1)}, u32[]{:S(2)}, u32[]{:S(2)}) %collective-permute-start.1) | collective-permute-done | bytes 114720 | tf_op jit(solution)/shard_map/ppermute | solution.py:579
  15.6 0.1 flat_edges.1
  15.6 0.9 %deep_edges.1 = (f32[88,8,128]{2,1,0:T(8,128)S(1)}, f32[82,8,128]{2,1,0:T(8,128)}, f32[2,6,2,32,128]{4,3,2,1,0:T(8,128)S(1)}) custom-call(f32[6,8,128]{2,1,0:T(8,128)S(1)} %get-tuple-element.25.s1_ref, f32[7,32,128]{2,1,0:T(8,128)S(1)} %collective-permute-done.o1_ref, f32[7,32,128]{2,1,0:T(8,128)S(1)} %collective-permute-done.1.o2_ref, ...), custom_call_target="tpu_custom_call" | custom-call | tf_op jit(solution)/shard_map/deep_edges/pallas_call | solution.py:550
  16.5 0.0 copy-start.4
  16.5 2.1 %collective-permute-start.2 = (f32[88,8,128]{2,1,0:T(8,128)S(1)}, f32[88,8,128]{2,1,0:T(8,128)S(1)}, u32[]{:S(2)}, u32[]{:S(2)}) collective-permute-start(f32[88,8,128]{2,1,0:T(8,128)S(1)} %get-tuple-element.29), channel_id=1, source_target_pairs={{0,1},{1,0},{2,3},{3,2},{4,5},{5,4},{6,7},{7,6},{8,9},{9,8},{10,11... | collective-permute-start | bytes 1081352 | tf_op jit(solution)/shard_map/ppermute | solution.py:594
  18.6 3.4 %collective-permute-start.4 = (f32[82,8,128]{2,1,0:T(8,128)}, f32[82,8,128]{2,1,0:T(8,128)}, u32[]{:S(2)}, u32[]{:S(2)}) collective-permute-start(f32[82,8,128]{2,1,0:T(8,128)} %get-tuple-element.35), channel_id=1, source_target_pairs={{1,2},{2,1},{3,4},{4,3},{5,6},{6,5},{9,10},{10,9},{11,12},{12,11},... | collective-permute-start | bytes 1007624 | tf_op jit(solution)/shard_map/ppermute | solution.py:595
  22.0 2.1 %collective-permute-start.3 = (f32[6,8,128]{2,1,0:T(8,128)S(1)}, f32[6,8,128]{2,1,0:T(8,128)S(1)}, u32[]{:S(2)}, u32[]{:S(2)}) collective-permute-start(f32[6,8,128]{2,1,0:T(8,128)S(1)} %get-tuple-element.30), channel_id=1, source_target_pairs={{1,2},{2,1},{3,4},{4,3},{5,6},{6,5},{9,10},{10,9},{11,12},{12,11},... | collective-permute-start | bytes 73736 | tf_op jit(solution)/shard_map/ppermute | solution.py:593
  24.2 3.4 %collective-permute-done.3.s2_ref = f32[6,8,128]{2,1,0:T(8,128)S(1)} collective-permute-done((f32[6,8,128]{2,1,0:T(8,128)S(1)}, f32[6,8,128]{2,1,0:T(8,128)S(1)}, u32[]{:S(2)}, u32[]{:S(2)}) %collective-permute-start.3) | collective-permute-done | bytes 24608 | tf_op jit(solution)/shard_map/ppermute | solution.py:593
  27.6 0.0 collective-permute-done.2.lat1_ref.h1_ref
  27.6 1.2 %krylov.1 = (f32[4,40,256]{2,1,0:T(8,128)S(1)}, f32[40,256]{1,0:T(8,128)S(1)}, f32[128,128]{1,0:T(8,128)S(1)}) custom-call(f32[3,32,256]{2,1,0:T(8,128)S(1)} %get-tuple-element.24.ext_ref, f32[88,8,128]{2,1,0:T(8,128)S(1)} %collective-permute-done.2.lat1_ref.h1_ref, f32[6,8,128]{2,1,0:T(8,128)S(1)} %collective-permute-done.3.s2_ref), custom_call_target="tpu_custom_call" | custom-call | tf_op jit(solution)/shard_map/krylov/pallas_call | solution.py:550
  28.8 0.0 copy-done.4
  28.8 0.0 copy-start.2
  28.8 0.7 %copy-done.2 = f32[88,8,128]{2,1,0:T(8,128)} copy-done((f32[88,8,128]{2,1,0:T(8,128)}, f32[88,8,128]{2,1,0:T(8,128)S(1)}, u32[]{:S(2)}) %copy-start.2) | copy-done | bytes 360472
  29.5 0.0 copy-start.6
  29.5 0.6 %copy-done.6 = f32[128,128]{1,0:T(8,128)} copy-done((f32[128,128]{1,0:T(8,128)}, f32[128,128]{1,0:T(8,128)S(1)}, u32[]{:S(2)}) %copy-start.6) | copy-done | bytes 65560
  30.2 8.7 %all-to-all-start = ((f32[128,1,128]{2,1,0:T(1,128)}), f32[128,1,128]{2,1,0:T(1,128)S(1)}, u32[]{:S(2)}, u32[]{:S(2)}) async-start(f32[128,1,128]{2,1,0:T(1,128)} %bitcast.5), calls=%async_computation | async-start | bytes 131072 | tf_op jit(solution)/shard_map/all_to_all | solution.py:602
  38.9 0.0 collective-permute-done.4.h2_ref
  38.9 9.3 %all-to-all-done = f32[128,1,128]{2,1,0:T(1,128)S(1)} async-done(((f32[128,1,128]{2,1,0:T(1,128)}), f32[128,1,128]{2,1,0:T(1,128)S(1)}, u32[]{:S(2)}, u32[]{:S(2)}) %all-to-all-start) | async-done | bytes 65568 | tf_op jit(solution)/shard_map/all_to_all | solution.py:602
  48.2 0.0 copy-start.1
  48.2 1.4 %copy-done.1 = f32[2,50,32,128]{3,2,1,0:T(8,128)S(1)} copy-done((f32[2,50,32,128]{3,2,1,0:T(8,128)S(1)}, f32[2,50,32,128]{3,2,1,0:T(8,128)}, u32[]{:S(2)}) %copy-start.1) | copy-done | bytes 1638424
  49.7 0.0 copy-start.3
  49.7 1.0 %copy-done.3 = f32[88,8,128]{2,1,0:T(8,128)S(1)} copy-done((f32[88,8,128]{2,1,0:T(8,128)S(1)}, f32[88,8,128]{2,1,0:T(8,128)}, u32[]{:S(2)}) %copy-start.3) | copy-done | bytes 360472
  50.6 0.0 copy-start.5
  50.6 1.0 %copy-done.5 = f32[2,6,2,32,128]{4,3,2,1,0:T(8,128)S(1)} copy-done((f32[2,6,2,32,128]{4,3,2,1,0:T(8,128)S(1)}, f32[2,6,2,32,128]{4,3,2,1,0:T(8,128)}, u32[]{:S(2)}) %copy-start.5) | copy-done | bytes 393240
  51.6 8.3 %sweeps.1 = (f32[2,50,32,128]{3,2,1,0:T(8,128)}, f32[2,50,32,128]{3,2,1,0:T(8,128)}, f32[32,128]{1,0:T(8,128)}) custom-call(f32[128,128]{1,0:T(8,128)S(1)} %bitcast.4, f32[4,40,256]{2,1,0:T(8,128)S(1)} %get-tuple-element.32.vec_ref, f32[40,256]{1,0:T(8,128)S(1)} %get-tuple-element.33.lev_ref, f32[2,6,2,32,128]{4,3,2,1,0:T(8,128)S(1)} %copy-done.5, ...), custom_call_target="tpu_custom_call" | custom-call | tf_op jit(solution)/shard_map/sweeps/pallas_call | solution.py:550
Async XLA Ops:
  5.3 1.2 %copy-start = (f32[2,50,32,128]{3,2,1,0:T(8,128)}, f32[2,50,32,128]{3,2,1,0:T(8,128)S(1)}, u32[]{:S(2)}) copy-start(f32[2,50,32,128]{3,2,1,0:T(8,128)S(1)} %get-tuple-element.38.tr) | copy-start | bytes 4915204
  6.5 6.2 %collective-permute-start = (f32[7,32,128]{2,1,0:T(8,128)S(1)}, f32[7,32,128]{2,1,0:T(8,128)S(1)}, u32[]{:S(2)}, u32[]{:S(2)}) collective-permute-start(f32[7,32,128]{2,1,0:T(8,128)S(1)} %get-tuple-element.22), channel_id=1, source_target_pairs={{0,8},{8,0},{16,24},{24,16},{32,40},{40,32},{48,56},{56,48},{64,72... | collective-permute-start | bytes 344072 | tf_op jit(solution)/shard_map/ppermute | solution.py:578
  8.6 7.0 %collective-permute-start.1 = (f32[7,32,128]{2,1,0:T(8,128)S(1)}, f32[7,32,128]{2,1,0:T(8,128)S(1)}, u32[]{:S(2)}, u32[]{:S(2)}) collective-permute-start(f32[7,32,128]{2,1,0:T(8,128)S(1)} %get-tuple-element.23), channel_id=1, source_target_pairs={{8,16},{16,8},{24,32},{32,24},{40,48},{48,40},{56,64},{64,56},{72,... | collective-permute-start | bytes 344072 | tf_op jit(solution)/shard_map/ppermute | solution.py:579
  16.5 12.3 %copy-start.4 = (f32[2,6,2,32,128]{4,3,2,1,0:T(8,128)}, f32[2,6,2,32,128]{4,3,2,1,0:T(8,128)S(1)}, u32[]{:S(2)}) copy-start(f32[2,6,2,32,128]{4,3,2,1,0:T(8,128)S(1)} %get-tuple-element.34.side_ref) | copy-start | bytes 1179652
  16.5 11.1 %collective-permute-start.2 = (f32[88,8,128]{2,1,0:T(8,128)S(1)}, f32[88,8,128]{2,1,0:T(8,128)S(1)}, u32[]{:S(2)}, u32[]{:S(2)}) collective-permute-start(f32[88,8,128]{2,1,0:T(8,128)S(1)} %get-tuple-element.29), channel_id=1, source_target_pairs={{0,1},{1,0},{2,3},{3,2},{4,5},{5,4},{6,7},{7,6},{8,9},{9,8},{10,11... | collective-permute-start | bytes 1081352 | tf_op jit(solution)/shard_map/ppermute | solution.py:594
  18.6 20.3 %collective-permute-start.4 = (f32[82,8,128]{2,1,0:T(8,128)}, f32[82,8,128]{2,1,0:T(8,128)}, u32[]{:S(2)}, u32[]{:S(2)}) collective-permute-start(f32[82,8,128]{2,1,0:T(8,128)} %get-tuple-element.35), channel_id=1, source_target_pairs={{1,2},{2,1},{3,4},{4,3},{5,6},{6,5},{9,10},{10,9},{11,12},{12,11},... | collective-permute-start | bytes 1007624 | tf_op jit(solution)/shard_map/ppermute | solution.py:595
  22.0 5.5 %collective-permute-start.3 = (f32[6,8,128]{2,1,0:T(8,128)S(1)}, f32[6,8,128]{2,1,0:T(8,128)S(1)}, u32[]{:S(2)}, u32[]{:S(2)}) collective-permute-start(f32[6,8,128]{2,1,0:T(8,128)S(1)} %get-tuple-element.30), channel_id=1, source_target_pairs={{1,2},{2,1},{3,4},{4,3},{5,6},{6,5},{9,10},{10,9},{11,12},{12,11},... | collective-permute-start | bytes 73736 | tf_op jit(solution)/shard_map/ppermute | solution.py:593
  28.8 0.7 %copy-start.2 = (f32[88,8,128]{2,1,0:T(8,128)}, f32[88,8,128]{2,1,0:T(8,128)S(1)}, u32[]{:S(2)}) copy-start(f32[88,8,128]{2,1,0:T(8,128)S(1)} %collective-permute-done.2.lat1_ref.h1_ref) | copy-start | bytes 1081348
  29.5 0.6 %copy-start.6 = (f32[128,128]{1,0:T(8,128)}, f32[128,128]{1,0:T(8,128)S(1)}, u32[]{:S(2)}) copy-start(f32[128,128]{1,0:T(8,128)S(1)} %get-tuple-element.31) | copy-start | bytes 196612
  30.2 18.1 %all-to-all-start = ((f32[128,1,128]{2,1,0:T(1,128)}), f32[128,1,128]{2,1,0:T(1,128)S(1)}, u32[]{:S(2)}, u32[]{:S(2)}) async-start(f32[128,1,128]{2,1,0:T(1,128)} %bitcast.5), calls=%async_computation | async-start | bytes 131072 | tf_op jit(solution)/shard_map/all_to_all | solution.py:602
  48.2 1.4 %copy-start.1 = (f32[2,50,32,128]{3,2,1,0:T(8,128)S(1)}, f32[2,50,32,128]{3,2,1,0:T(8,128)}, u32[]{:S(2)}) copy-start(f32[2,50,32,128]{3,2,1,0:T(8,128)} %copy-done) | copy-start | bytes 4915204
  49.7 1.0 %copy-start.3 = (f32[88,8,128]{2,1,0:T(8,128)S(1)}, f32[88,8,128]{2,1,0:T(8,128)}, u32[]{:S(2)}) copy-start(f32[88,8,128]{2,1,0:T(8,128)} %copy-done.2) | copy-start | bytes 1081348
  50.6 1.0 %copy-start.5 = (f32[2,6,2,32,128]{4,3,2,1,0:T(8,128)S(1)}, f32[2,6,2,32,128]{4,3,2,1,0:T(8,128)}, u32[]{:S(2)}) copy-start(f32[2,6,2,32,128]{4,3,2,1,0:T(8,128)} %copy-done.4) | copy-start | bytes 1179652

commit v4 on v3

--- a/solution.py
+++ b/solution.py
@@ -17,7 +17,7 @@
 SLOTS = 32
 FIELDS = 6
 GROUPS = -(-LEVELS // 4)
-VMEM_LIMIT = 12 * 1024 * 1024
+VMEM_LIMIT = 16 * 1024 * 1024
 F32 = jnp.float32
 VMEM = pltpu.VMEM
 
@@ -83,8 +83,8 @@
 
 def solve_kernel(
     lam_h, vel_h, tr_h, dif_h, lams_h, depth_h, lev_h,
-    mixed_ref, vel, tr, base_ref, lon1_ref, lon2_ref, slots_ref, g1_ref, g2_ref,
-    lam, dif, lams_s, lev_s, w_s, z_s, col_sem, rest_sem,
+    mixed_ref, base_ref, lon1_ref, lon2_ref, slots_ref, g1_ref, g2_ref,
+    lam, vel, tr, dif, lams_s, lev_s, w_s, z_s, col_sem, rest_sem,
 ):
     lon_par = lax.rem(lax.axis_index("lon"), 2)
     lat_par = lax.rem(lax.axis_index("lat"), 2)
@@ -217,14 +217,14 @@
 
 
 CORNERS = 4
-EDGES = FIELDS * GROUPS + CORNERS
+EDGES = FIELDS * GROUPS
 
 
 def corner_of(index):
     return index // 8, index // 2 % 4, index % 2
 
 
-def flat_kernel(base_ref, o1_ref, o2_ref, ext_ref, s1_ref, s2_ref):
+def lon_kernel(base_ref, o1_ref, o2_ref, slots_ref, g1_ref, ext_ref, lat1_ref, lat2_ref, side_ref):
     lon_par = lax.rem(lax.axis_index("lon"), 2)
     lat_par = lax.rem(lax.axis_index("lat"), 2)
     lane = iota((ROWS, COLS), 1)
@@ -239,14 +239,9 @@
         ext_ref[i, :, COLS:] = edge
         for half, here in enumerate((own, edge)):
             first, last = here[:8], here[ROWS - 8 :]
-            s1_ref[2 * i + half] = pick(lat_par, last, first)
-            s2_ref[2 * i + half] = pick(lat_par, first, last)
-
-
-def deep_kernel(s1_ref, o1_ref, o2_ref, slots_ref, g1_ref, g2_ref, lat1_ref, h2_ref, side_ref):
-    lon_par = lax.rem(lax.axis_index("lon"), 2)
-    lat_par = lax.rem(lax.axis_index("lat"), 2)
-    near = iota((ROWS, COLS), 1) % 4 < 2
+            lat1_ref[EDGES + CORNERS + 2 * i + half] = pick(lat_par, last, first)
+            lat2_ref[CORNERS + 2 * i + half] = pick(lat_par, first, last)
+    near = lane % 4 < 2
     for i in range(FIELDS):
         b1, b2 = o1_ref[i], o2_ref[i]
         east, west = pick(lon_par, b1, b2), pick(lon_par, b2, b1)
@@ -255,9 +250,7 @@
         side_ref[0, i, 1] = jnp.where(near, roll(west, COLS - 2, 1), own_b)
         side_ref[1, i, 0] = jnp.where(near, own_a, roll(east, 2, 1))
         side_ref[1, i, 1] = jnp.where(near, own_b, east)
-    lat1_ref[: FIELDS * GROUPS] = g1_ref[...]
-    lat1_ref[EDGES:] = s1_ref[...]
-    h2_ref[: FIELDS * GROUPS] = g2_ref[...]
+    lat1_ref[:EDGES] = g1_ref[...]
     pair = iota((8, COLS), 0) // 2
     for c in range(CORNERS):
         first = jnp.zeros((8, COLS), F32)
@@ -267,17 +260,17 @@
             x = side_ref[side, field, tile]
             first = jnp.where(pair == q, roll(x[:8], 2 * q, 0) if q else x[:8], first)
             last = jnp.where(pair == (q + 3) % 4, roll(x[ROWS - 8 :], 2 * q, 0) if q else x[ROWS - 8 :], last)
-        lat1_ref[FIELDS * GROUPS + c] = pick(lat_par, last, first)
-        h2_ref[FIELDS * GROUPS + c] = pick(lat_par, first, last)
-
-
-def krylov_kernel(ext_ref, lat1_ref, s2_ref, vec_ref, lev_ref, gram_ref):
+        lat1_ref[EDGES + c] = pick(lat_par, last, first)
+        lat2_ref[c] = pick(lat_par, first, last)
+
+
+def krylov_kernel(ext_ref, lat1_ref, lat2_ref, vec_ref, lev_ref, gram_ref):
     lat_par = lax.rem(lax.axis_index("lat"), 2)
     rows, cols = ROWS + 16, 2 * COLS
     whole = []
     for i in range(3):
-        s1 = jnp.concatenate([lat1_ref[EDGES + 2 * i], lat1_ref[EDGES + 2 * i + 1]], axis=1)
-        s2 = jnp.concatenate([s2_ref[2 * i], s2_ref[2 * i + 1]], axis=1)
+        s1 = jnp.concatenate([lat1_ref[EDGES + CORNERS + 2 * i + half] for half in range(2)], axis=1)
+        s2 = jnp.concatenate([lat2_ref[CORNERS + 2 * i + half] for half in range(2)], axis=1)
         whole.append(jnp.concatenate([ext_ref[i], pick(lat_par, s1, s2), pick(lat_par, s2, s1)], axis=0))
     f, depth, lev = whole
 
@@ -369,28 +362,165 @@
     return [r[0] for r in rhs]
 
 
-SPANS = ((0, 12), (12, 25), (25, 38), (38, LEVELS))
+SPANS = ((0, 12), (12, 26), (26, 38), (38, LEVELS))
+SPAN_LEVELS = 14
 TALL = ROWS + 8
-SPAN_LEVELS = 13
 BF16 = jnp.bfloat16
 
 
+class Sweeps:
+    def __init__(self, lev_ref, side_ref, h1_ref, h2_ref, c2_ref, lhs, weights):
+        self.lev_ref, self.side_ref, self.lhs = lev_ref, side_ref, lhs
+        self.h1_ref, self.h2_ref, self.c2_ref = h1_ref, h2_ref, c2_ref
+        shape = (COLS, COLS)
+        source, target = iota(shape, 0), iota(shape, 1)
+        shift = jnp.where(source == target + 1, 1.0, jnp.where(source == target - 1, -1.0, 0.0)).astype(BF16)
+        ends = jnp.where(
+            (target == COLS - 1) & (source % 2 == 0), 1.0, jnp.where((target == 0) & (source % 2 == 1), -1.0, 0.0)
+        ).astype(BF16)
+        weights[:COLS] = shift
+        weights[COLS : 2 * COLS] = shift
+        weights[2 * COLS :] = ends
+        self.lane = iota((TALL, COLS), 1)
+        pair = iota((8, COLS), 0) // 2
+        even = jnp.broadcast_to(lax.rem(lax.axis_index("lat"), 2), (8, COLS)) == 0
+        self.masks = [(pair == q) == even for q in range(4)]
+
+    def edge_rows(self, index, q):
+        other = self.h2_ref[index] if index < EDGES else self.c2_ref[index - EDGES]
+        x = jnp.where(self.masks[q], self.h1_ref[index], other)
+        return roll(x, 8 - 2 * q, 0) if q else x
+
+    def tall(self, ref, n, field, k):
+        return jnp.concatenate([ref[n, k], self.edge_rows(field * GROUPS + k // 4, k % 4)], axis=0)
+
+    def wet(self, k, rows):
+        return jnp.where(float(k) < self.lev_ref[:rows, :COLS], 1.0, 0.0)
+
+    def around(self, ref, side):
+        lane = self.lane
+        own, edge = roll(ref[:, :COLS], 2, 1), roll(ref[:, COLS:], 2, 1)
+        x = jnp.where(lane < 2, own, edge) if side else jnp.where(lane < 2, edge, own)
+        for s in (4, 8, 16, 32, 64):
+            x = jnp.where(lane < s, x, roll(x, s, 1))
+        return x
+
+    def columns(self, first_fields):
+        flux1, flux2 = [], []
+        for side in range(2):
+            levels = self.around(self.lev_ref, side)
+            flux1.append([])
+            flux2.append([])
+            for tile in range(2):
+                def column(field, side=side, tile=tile):
+                    index = side * 8 + field * 2 + tile
+                    return jnp.concatenate(
+                        [self.side_ref[side, field, tile], self.edge_rows(EDGES + index // 4, index % 4)], axis=0
+                    )
+
+                wet = jnp.where((self.lane // 4 + tile * SLOTS).astype(F32) < levels, 1.0, 0.0)
+                move = COURANT * wet
+                u, v = column(2), column(3)
+                flux1[-1].append([])
+                flux2[-1].append([])
+                for x in first_fields(side, tile, column, wet):
+                    flux = u * x
+                    flux1[-1][-1].append(flux)
+                    x = x + move * (roll(flux, COLS - 1, 1) - roll(flux, 1, 1))
+                    for _ in range(2):
+                        x = x + move * self.meridional(v * x)
+                    flux2[-1][-1].append((u * x)[:ROWS])
+        return flux1, flux2
+
+    @staticmethod
+    def meridional(x):
+        return roll(x, TALL - 1, 0) - roll(x, 1, 0)
+
+    @staticmethod
+    def parts(x):
+        hi = x.astype(BF16)
+        return hi, (x - hi.astype(F32)).astype(BF16)
+
+    def pack(self, west, east):
+        at = iota(east.shape, 1) % 4
+        both = jnp.where(at == 2, east, roll(west, 2, 1))
+        hi, mid = (t.astype(F32) for t in self.parts(both))
+        return jnp.where(at >= 2, hi, roll(mid, COLS - 2, 1))
+
+    def put(self, at, fields):
+        x = jnp.concatenate([f for f, _, _ in fields], axis=0)
+        edge = [
+            jnp.where(iota(e.shape, 1) // 4 == k % SLOTS, e, 0.0) for _, e, k in fields
+        ]
+        here = pl.ds(at, x.shape[0])
+        hi, mid = self.parts(x)
+        self.lhs[here, :COLS] = hi
+        self.lhs[here, COLS : 2 * COLS] = mid
+        self.lhs[here, 2 * COLS :] = jnp.concatenate(edge, axis=0).astype(BF16)
+
+
+def fetch(pairs, sem):
+    out = []
+    for c, (first, last) in enumerate(SPANS):
+        here = pl.ds(first, last - first)
+        out.append([pltpu.make_async_copy(a.at[:, here], b.at[:, here], sem.at[c, i]) for i, (a, b) in enumerate(pairs)])
+    return out
+
+
+def mixed_kernel(
+    lev_ref, side_ref, h1_ref, h2_ref, c2_ref, mixed, vel_h,
+    swept,
+    vel, edge1, edge2, lhs, diff, weights, in_sem,
+):
+    reads = fetch(((vel_h, vel),), in_sem)
+    for r in sum(reads, []):
+        r.start()
+    sw = Sweeps(lev_ref, side_ref, h1_ref, h2_ref, c2_ref, lhs, weights)
+    flux1, flux2 = sw.columns(lambda side, tile, column, wet: (column(0), column(1)))
+    for tile in range(2):
+        for n in range(2):
+            edge1[n, tile] = sw.pack(flux1[0][tile][n], flux1[1][tile][n])
+            edge2[n, tile] = sw.pack(flux2[0][tile][n], flux2[1][tile][n])
+    for (first, last), part in zip(SPANS, reads):
+        for r in part:
+            r.wait()
+        rows = 0
+        for k in range(first, last):
+            u, tile = sw.tall(vel, 0, 2, k), k // SLOTS
+            sw.put(rows, [(u * sw.tall(mixed, n, n, k), edge1[n, tile], k) for n in range(2)])
+            rows += 2 * TALL
+        diff[:rows] = jnp.dot(lhs[:rows], weights[...], preferred_element_type=F32)
+        rows = 0
+        for k in range(first, last):
+            move, tile = COURANT * sw.wet(k, TALL), k // SLOTS
+            u, v = vel[0, k], sw.tall(vel, 1, 3, k)
+            fields = []
+            for n in range(2):
+                at = (2 * (k - first) + n) * TALL
+                x = sw.tall(mixed, n, n, k) + move * diff[at : at + TALL]
+                x = x + move * sw.meridional(v * x)
+                x = (x + move * sw.meridional(v * x))[:ROWS]
+                swept[n, k] = x
+                fields.append((u * x, edge2[n, tile], k))
+            sw.put(rows, fields)
+            rows += 2 * ROWS
+        diff[:rows] = jnp.dot(lhs[:rows], weights[...], preferred_element_type=F32)
+        for k in range(first, last):
+            move = COURANT * sw.wet(k, ROWS)
+            for n in range(2):
+                at = (2 * (k - first) + n) * ROWS
+                swept[n, k] = swept[n, k] + move * diff[at : at + ROWS]
+
+
 def final_kernel(
-    gram_ref, vec_ref, lev_ref, side_ref, h1_ref, h2_ref, mixed, vel, tr,
+    gram_ref, vec_ref, lev_ref, side_ref, h1_ref, h2_ref, c2_ref, swept, vel_h, tr_h,
     adj_h, avel_h, sol_ref,
-    adj, avel, sol_s, edge1, edge2, edge3, start_s, lhs, diff, weights, out_sem,
+    vel, tr, adj, avel, sol_s, edge1, edge2, edge3, late, lhs, diff, weights, in_sem, out_sem,
 ):
-    lat_par = lax.rem(lax.axis_index("lat"), 2)
-    shape = (COLS, COLS)
-    source, target = iota(shape, 0), iota(shape, 1)
-    shift = jnp.where(source == target + 1, 1.0, jnp.where(source == target - 1, -1.0, 0.0)).astype(BF16)
-    ends = jnp.where(
-        (target == COLS - 1) & (source % 2 == 0), 1.0, jnp.where((target == 0) & (source % 2 == 1), -1.0, 0.0)
-    ).astype(BF16)
-    weights[:COLS] = shift
-    weights[COLS : 2 * COLS] = shift
-    weights[2 * COLS :] = ends
-
+    reads = fetch(((vel_h, vel), (tr_h, tr)), in_sem)
+    for r in sum(reads, []):
+        r.start()
+    sw = Sweeps(lev_ref, side_ref, h1_ref, h2_ref, c2_ref, lhs, weights)
     coefs = galerkin(gram_ref[...])
     for half in range(2):
         at = half * COLS
@@ -400,132 +530,54 @@
             total = total + wide * vec_ref[i, :, at : at + COLS]
         sol_s[:, at : at + COLS] = total
     sol_ref[...] = sol_s[:ROWS, :COLS]
-
-    lane = iota((TALL, COLS), 1)
-    pair = iota((8, COLS), 0) // 2
-    even = jnp.broadcast_to(lat_par, (8, COLS)) == 0
-    masks = [(pair == q) == even for q in range(4)]
-
-    def edge_rows(index, q):
-        x = jnp.where(masks[q], h1_ref[index], h2_ref[index])
-        return roll(x, 8 - 2 * q, 0) if q else x
-
-    def parts(x):
-        hi = x.astype(BF16)
-        return hi, (x - hi.astype(F32)).astype(BF16)
-
-    flux1, flux2 = [], []
-    for side in range(2):
-        def around(ref):
-            own, edge = roll(ref[:, :COLS], 2, 1), roll(ref[:, COLS:], 2, 1)
-            x = jnp.where(lane < 2, own, edge) if side else jnp.where(lane < 2, edge, own)
-            for s in (4, 8, 16, 32, 64):
-                x = jnp.where(lane < s, x, roll(x, s, 1))
-            return x
-
-        levels, pressure = around(lev_ref), around(sol_s)
-        for tile in range(2):
-            def column(field):
-                index = side * 8 + field * 2 + tile
-                return jnp.concatenate(
-                    [side_ref[side, field, tile], edge_rows(FIELDS * GROUPS + index // 4, index % 4)], axis=0
-                )
-
-            wet = jnp.where((lane // 4 + tile * SLOTS).astype(F32) < levels, 1.0, 0.0)
-            move = COURANT * wet
-            u, v = column(2), column(3)
-            for n in range(2):
-                x = column(n) + GAINS[n] * wet * pressure
-                flux = u * x
-                flux1.append(flux)
-                x = x + move * (roll(flux, COLS - 1, 1) - roll(flux, 1, 1))
-                for _ in range(2):
-                    flux = v * x
-                    x = x + move * (roll(flux, TALL - 1, 0) - roll(flux, 1, 0))
-                flux2.append((u * x)[:ROWS])
-
-    def pack(west, east):
-        at = iota(east.shape, 1) % 4
-        both = jnp.where(at == 2, east, roll(west, 2, 1))
-        hi, mid = (t.astype(F32) for t in parts(both))
-        return jnp.where(at >= 2, hi, roll(mid, COLS - 2, 1))
-
+    flux1, flux2 = sw.columns(lambda side, tile, column, wet: (wet * sw.around(sol_s, side),))
     for tile in range(2):
+        edge1[tile] = sw.pack(flux1[0][tile][0], flux1[1][tile][0])
+        edge2[tile] = sw.pack(flux2[0][tile][0], flux2[1][tile][0])
         for n in range(2):
-            west, east = tile * 2 + n, 4 + tile * 2 + n
-            edge1[tile, n * TALL : (n + 1) * TALL] = pack(flux1[west], flux1[east])
-            edge2[tile, n * ROWS : (n + 1) * ROWS] = pack(flux2[west], flux2[east])
-            edge3[tile, n * ROWS : (n + 1) * ROWS] = pack(side_ref[0, 4 + n, tile], side_ref[1, 4 + n, tile])
-
-    def meridional(x):
-        return roll(x, TALL - 1, 0) - roll(x, 1, 0)
-
-    def tall_field(ref, n, field, k):
-        return jnp.concatenate([ref[n, k], edge_rows(field * GROUPS + k // 4, k % 4)], axis=0)
-
-    def wet_of(k, rows):
-        return jnp.where(float(k) < lev_ref[:rows, :COLS], 1.0, 0.0)
-
-    def put(at, rows, x, edge, k):
-        here = iota(x.shape, 1) // 4 == k % SLOTS
-        hi, mid = parts(x)
-        lhs[pl.ds(at, rows), :COLS] = hi
-        lhs[pl.ds(at, rows), COLS : 2 * COLS] = mid
-        lhs[pl.ds(at, rows), 2 * COLS :] = jnp.where(here, edge[k // SLOTS], 0.0).astype(BF16)
-
+            edge3[n, tile] = sw.pack(side_ref[0, 4 + n, tile], side_ref[1, 4 + n, tile])
     writes = []
-    for first, last in SPANS:
-        def zonal_first(k, j):
-            wet_sol = wet_of(k, TALL) * sol_s[:, :COLS]
-            u = tall_field(vel, 0, 2, k)
-            xs = [tall_field(mixed, n, n, k) + GAINS[n] * wet_sol for n in range(2)]
-            for n in range(2):
-                start_s[j, n] = xs[n]
-            at = j * 2 * TALL
-            put(at, 2 * TALL, jnp.concatenate([u * x for x in xs], axis=0), edge1, k)
-
-        def middle(k, j):
-            move = COURANT * wet_of(k, TALL)
-            v = tall_field(vel, 1, 3, k)
-            u = vel[0, k]
-            fluxes = []
-            for n in range(2):
-                x = start_s[j, n] + move * diff[pl.ds((2 * j + n) * TALL, TALL)]
-                x = x + move * meridional(v * x)
-                x = (x + move * meridional(v * x))[:ROWS]
-                adj[n, k] = x
-                fluxes.append(u * x)
-            at = j * 4 * ROWS
-            put(at, 2 * ROWS, jnp.concatenate(fluxes, axis=0), edge2, k)
-            put(at + 2 * ROWS, 2 * ROWS, jnp.concatenate([tr[0, k], tr[1, k]], axis=0), edge3, k)
-
-        def zonal_last(k, j):
-            move = COURANT * wet_of(k, ROWS)
+    for (first, last), part in zip(SPANS, reads):
+        for r in part:
+            r.wait()
+        rows = 0
+        for k in range(first, last, 2):
+            fields = []
+            for m in (k, k + 1):
+                x = sw.wet(m, TALL) * sol_s[:, :COLS]
+                fields.append((sw.tall(vel, 0, 2, m) * x, edge1[m // SLOTS], m))
+            sw.put(rows, fields)
+            rows += 2 * TALL
+        diff[:rows] = jnp.dot(lhs[:rows], weights[...], preferred_element_type=F32)
+        rows = 0
+        for k in range(first, last):
+            wet = sw.wet(k, TALL)
+            move, at = COURANT * wet, (k - first) * TALL
+            v = sw.tall(vel, 1, 3, k)
+            x = wet * sol_s[:, :COLS] + move * diff[at : at + TALL]
+            x = x + move * sw.meridional(v * x)
+            x = (x + move * sw.meridional(v * x))[:ROWS]
+            late[k - first] = x
+            tile = k // SLOTS
+            sw.put(rows, [(vel[0, k] * x, edge2[tile], k)] + [(tr[n, k], edge3[n, tile], k) for n in range(2)])
+            rows += 3 * ROWS
+        diff[:rows] = jnp.dot(lhs[:rows], weights[...], preferred_element_type=F32)
+        for k in range(first, last):
+            at = 3 * (k - first) * ROWS
+            move = COURANT * sw.wet(k, ROWS)
+            x = late[k - first] + move * diff[at : at + ROWS]
             east_sum, north_sum = 0.0, 0.0
             for n in range(2):
-                at = j * 4 * ROWS + n * ROWS
-                x = adj[n, k] + move * diff[pl.ds(at, ROWS)]
-                adj[n, k] = x
-                east_sum = east_sum + x * diff[pl.ds(at + 2 * ROWS, ROWS)]
-                north_sum = north_sum + x * meridional(tall_field(tr, n, 4 + n, k))[:ROWS]
+                total = swept[n, k] + GAINS[n] * x
+                adj[n, k] = total
+                at += ROWS
+                east_sum = east_sum + total * diff[at : at + ROWS]
+                north_sum = north_sum + total * sw.meridional(sw.tall(tr, n, 4 + n, k))[:ROWS]
             avel[0, k] = -move * east_sum
             avel[1, k] = -move * north_sum
-
-        levels = last - first
-        for k in range(first, last):
-            zonal_first(k, k - first)
-        rows = levels * 2 * TALL
-        diff[:rows] = jnp.dot(lhs[:rows], weights[...], preferred_element_type=F32)
-        for k in range(first, last):
-            middle(k, k - first)
-        rows = levels * 4 * ROWS
-        diff[:rows] = jnp.dot(lhs[:rows], weights[...], preferred_element_type=F32)
-        for k in range(first, last):
-            zonal_last(k, k - first)
+        here = pl.ds(first, last - first)
         for i, (src, dst) in enumerate(((adj, adj_h), (avel, avel_h))):
-            copy = pltpu.make_async_copy(
-                src.at[:, pl.ds(first, levels)], dst.at[:, pl.ds(first, levels)], out_sem.at[len(writes) // 2, i]
-            )
+            copy = pltpu.make_async_copy(src.at[:, here], dst.at[:, here], out_sem.at[len(writes) // 2, i])
             copy.start()
             writes.append(copy)
     for copy in writes:
@@ -544,7 +596,7 @@
     return jax.ShapeDtypeStruct(dims, F32)
 
 
-def call(kernel, name, ins, outs, scratch, args):
+def call(kernel, name, ins, outs, scratch, args, aliases=None):
     here, there = pl.BlockSpec(memory_space=VMEM), pl.BlockSpec(memory_space=pltpu.HBM)
     args = [pltpu.with_memory_space_constraint(a, pltpu.HBM if far else VMEM) for a, far in zip(args, ins)]
     return pl.pallas_call(
@@ -554,6 +606,7 @@
         in_specs=[there if far else here for far in ins],
         out_specs=tuple(there if far else here for _, far in outs),
         scratch_shapes=scratch,
+        input_output_aliases=aliases or {},
         compiler_params=pltpu.CompilerParams(vmem_limit_bytes=VMEM_LIMIT),
     )(*args)
 
@@ -566,48 +619,52 @@
     lon, lat = lax.axis_size("lon"), lax.axis_size("lat")
     tile = (ROWS, COLS)
     deep = (2, LEVELS) + tile
-    mixed, vel, tr, base, lon1, lon2, slots, g1, g2 = call(
+    mixed, base, lon1, lon2, slots, g1, g2 = call(
         solve_kernel, "column_solve", (True,) * 7,
-        (kept(*deep), kept(*deep), kept(*deep), kept(3, *tile), kept(FIELDS + 1, *tile), kept(FIELDS + 1, *tile),
+        (kept(*deep), kept(3, *tile), kept(FIELDS + 1, *tile), kept(FIELDS + 1, *tile),
          kept(FIELDS, 2, *tile), kept(FIELDS * GROUPS, 8, COLS), kept(FIELDS * GROUPS, 8, COLS)),
-        [VMEM(deep, F32), VMEM((LEVELS,) + tile, F32), VMEM(tile, F32), VMEM(tile, jnp.int32),
+        [VMEM(deep, F32), VMEM(deep, F32), VMEM(deep, F32), VMEM((LEVELS,) + tile, F32), VMEM(tile, F32), VMEM(tile, jnp.int32),
          VMEM((LEVELS,) + tile, F32), VMEM(deep, F32),
          pltpu.SemaphoreType.DMA((HALF // 5, 4)), pltpu.SemaphoreType.DMA((5,))],
         (lam_tracer, velocity, tracer, diffusivity, lam_surface, sea_depth, levels),
     )
+    h2 = lax.ppermute(g2, "lat", swaps(lat, 1, False))
     o1 = lax.ppermute(lon1, "lon", swaps(lon, 0, True))
     o2 = lax.ppermute(lon2, "lon", swaps(lon, 1, True))
-    ext, s1, s2 = call(
-        flat_kernel, "flat_edges", (False,) * 3,
-        (kept(3, ROWS, 2 * COLS), kept(6, 8, COLS), kept(6, 8, COLS)),
+    o1, o2, h2 = lax.optimization_barrier((o1, o2, h2))
+    ext, lat1, lat2, side = call(
+        lon_kernel, "after_lon", (False,) * 5,
+        (kept(3, ROWS, 2 * COLS), kept(EDGES + CORNERS + 6, 8, COLS), kept(CORNERS + 6, 8, COLS), kept(2, FIELDS, 2, *tile)),
         [],
-        (base, o1, o2),
+        (base, o1, o2, slots, g1),
     )
-    lat1, h2, side = call(
-        deep_kernel, "deep_edges", (False,) * 6,
-        (kept(EDGES + 6, 8, COLS), kept(EDGES, 8, COLS), kept(2, FIELDS, 2, *tile)),
-        [],
-        (s1, o1, o2, slots, g1, g2),
-    )
-    odd_lat = swaps(lat, 1, False)
-    s2 = lax.ppermute(s2, "lat", odd_lat)
     lat1 = lax.ppermute(lat1, "lat", swaps(lat, 0, False))
-    h2 = lax.ppermute(h2, "lat", odd_lat)
+    lat2 = lax.ppermute(lat2, "lat", swaps(lat, 1, False))
     vec, lev, gram = call(
         krylov_kernel, "krylov", (False,) * 3,
         (kept(4, TALL, 2 * COLS), kept(TALL, 2 * COLS), kept(lon * lat, COLS)),
         [],
-        (ext, lat1, s2),
+        (ext, lat1, lat2),
     )
     gram = lax.all_to_all(gram, ("lon", "lat"), 0, 0, tiled=True)
+    rows = SPAN_LEVELS * 2 * TALL
+    (swept,) = call(
+        mixed_kernel, "mixed_sweeps", (False,) * 6 + (True,),
+        (kept(*deep),),
+        [VMEM(deep, F32), VMEM((2, 2, TALL, COLS), F32), VMEM((2, 2) + tile, F32),
+         VMEM((rows, 3 * COLS), BF16), VMEM((rows, COLS), F32), VMEM((3 * COLS, COLS), BF16),
+         pltpu.SemaphoreType.DMA((len(SPANS), 1))],
+        (lev, side, lat1, h2, lat2, mixed, velocity), {5: 0},
+    )
+    rows = SPAN_LEVELS * 3 * ROWS
     return call(
-        final_kernel, "sweeps", (False,) * 9,
+        final_kernel, "sweeps", (False,) * 8 + (True,) * 2,
         ((shape(*deep), True), (shape(*deep), True), (shape(*tile), False)),
-        [VMEM(deep, F32), VMEM(deep, F32), VMEM((TALL, 2 * COLS), F32), VMEM((2, 2 * TALL, COLS), F32),
-         VMEM((2, 2 * ROWS, COLS), F32), VMEM((2, 2 * ROWS, COLS), F32), VMEM((SPAN_LEVELS, 2, TALL, COLS), F32),
-         VMEM((SPAN_LEVELS * 4 * ROWS, 3 * COLS), BF16), VMEM((SPAN_LEVELS * 4 * ROWS, COLS), F32),
-         VMEM((3 * COLS, COLS), BF16), pltpu.SemaphoreType.DMA((len(SPANS), 2))],
-        (gram, vec, lev, side, lat1, h2, mixed, vel, tr),
+        [VMEM(deep, F32), VMEM(deep, F32), VMEM(deep, F32), VMEM(deep, F32), VMEM((TALL, 2 * COLS), F32),
+         VMEM((2, TALL, COLS), F32), VMEM((2,) + tile, F32), VMEM((2, 2) + tile, F32), VMEM((SPAN_LEVELS,) + tile, F32),
+         VMEM((rows, 3 * COLS), BF16), VMEM((rows, COLS), F32), VMEM((3 * COLS, COLS), BF16),
+         pltpu.SemaphoreType.DMA((len(SPANS), 2)), pltpu.SemaphoreType.DMA((len(SPANS), 2))],
+        (gram, vec, lev, side, lat1, h2, lat2, swept, velocity, tracer),
     )
 
 

time: 60.2 us -> 52.5 us (0.87)
  waiting for transfers between devices: 15.6 us -> 8.65 us
  local copies, waits for them, and re-layouts: 5.92 us -> 0 us
  Pallas kernels: 15.1 us -> 19.2 us
  starting transfers between devices: 22.6 us -> 23.6 us
    unnamed x14 -> x0, local copies, waits for them, and re-layouts: 5.92 us -> none
    all_to_all x1, waiting for transfers between devices: 9.34 us -> 4.11 us  [per_device(): gram = lax.all_to_all(gram, ('lon', 'lat'), 0, 0, tiled=True)]
    pallas_call x5, Pallas kernels: 15.1 us -> 19.2 us  [call(): pl.pallas_call(kernel, name=name, out_shape=tuple((o for o, _ in outs)),...]
    ppermute x2, starting transfers between devices: 5.55 us -> 9.31 us  [the longest x1 4.94 us: per_device(): h2 = lax.ppermute(g2, 'lat', swaps(lat, 1, False))]
    ppermute x1, starting transfers between devices: 2.1 us -> 0.09 us  [per_device(): lat1 = lax.ppermute(lat1, 'lat', swaps(lat, 0, False))]
    ppermute x2, waiting for transfers between devices: 3.38 us -> 1.67 us  [the longest x1 1.67 us: per_device(): lat2 = lax.ppermute(lat2, 'lat', swaps(lat, 1, False))]
    ppermute x1, starting transfers between devices: 2.13 us -> 1.38 us  [per_device(): o1 = lax.ppermute(lon1, 'lon', swaps(lon, 0, True))]
  transfers between devices with their start and end apart: 6 -> 6, of which waited for: 3 -> 3; matrix products, arithmetic and copies ran while one was open for 0% -> 0% of each run, Pallas kernels for 2% -> 10%
where the time goes in v4:
time: 52.5 us; the launch traced here: 52.3 us
  starting transfers between devices  23.6 us (45%)
  Pallas kernels  19.2 us (37%)
  waiting for transfers between devices  8.65 us (16%)
  between operations  0.85 us (2%)
    pallas_call x5, Pallas kernels, call(): pl.pallas_call(kernel, name=name, out_shape=tuple((o for o, _ in outs)),...  19.2 us
    all_to_all x1, starting transfers between devices, per_device(): gram = lax.all_to_all(gram, ('lon', 'lat'), 0, 0, tiled=True)  8.77 us
    ppermute x1, starting transfers between devices, per_device(): h2 = lax.ppermute(g2, 'lat', swaps(lat, 1, False))  4.94 us
    ppermute x1, starting transfers between devices, per_device(): lat2 = lax.ppermute(lat2, 'lat', swaps(lat, 1, False))  4.37 us
    all_to_all x1, waiting for transfers between devices, per_device(): gram = lax.all_to_all(gram, ('lon', 'lat'), 0, 0, tiled=True)  4.11 us
    ppermute x1, starting transfers between devices, per_device(): o2 = lax.ppermute(lon2, 'lon', swaps(lon, 1, True))  4.1 us
    ppermute x1, waiting for transfers between devices, per_device(): o2 = lax.ppermute(lon2, 'lon', swaps(lon, 1, True))  2.86 us
    ppermute x1, waiting for transfers between devices, per_device(): lat2 = lax.ppermute(lat2, 'lat', swaps(lat, 1, False))  1.67 us
  transfers between devices with their start and end apart: 6, of which 3 were waited for; matrix products, arithmetic and copies ran while one was open for 0% of the time, Pallas kernels for 10%

profile of v4, /device:TPU:1, one launch (start us, length us, event | category | flops | bytes accessed | tf_op | source)
XLA Modules:
  0.0 52.3 jit_solution(1731609325375504032)
XLA Ops:
  0.6 4.6 %column_solve.1 = (f32[2,50,32,128]{3,2,1,0:T(8,128)S(1)}, f32[3,32,128]{2,1,0:T(8,128)S(1)}, f32[7,32,128]{2,1,0:T(8,128)S(1)}, f32[7,32,128]{2,1,0:T(8,128)S(1...) custom-call(f32[2,50,32,128]{3,2,1,0:T(8,128)} %lam_h.1, ...), custom_call_target="tpu_custom_call" | custom-call | tf_op jit(solution)/shard_map/column_solve/pallas_call | solution.py:602
  5.3 4.9 %collective-permute-start.2 = (f32[78,8,128]{2,1,0:T(8,128)S(1)}, f32[78,8,128]{2,1,0:T(8,128)S(1)}, u32[]{:S(2)}, u32[]{:S(2)}) collective-permute-start(f32[78,8,128]{2,1,0:T(8,128)S(1)} %get-tuple-element.23), channel_id=1, source_target_pairs={{1,2},{2,1},{3,4},{4,3},{5,6},{6,5},{9,10},{10,9},{11,12},{12,11},... | collective-permute-start | bytes 958472 | tf_op jit(solution)/shard_map/ppermute | solution.py:631
  10.2 1.4 %collective-permute-start = (f32[7,32,128]{2,1,0:T(8,128)S(1)}, f32[7,32,128]{2,1,0:T(8,128)S(1)}, u32[]{:S(2)}, u32[]{:S(2)}) collective-permute-start(f32[7,32,128]{2,1,0:T(8,128)S(1)} %get-tuple-element.21), channel_id=1, source_target_pairs={{0,8},{8,0},{16,24},{24,16},{32,40},{40,32},{48,56},{56,48},{64,72... | collective-permute-start | bytes 344072 | tf_op jit(solution)/shard_map/ppermute | solution.py:632
  11.6 4.1 %collective-permute-start.1 = (f32[7,32,128]{2,1,0:T(8,128)S(1)}, f32[7,32,128]{2,1,0:T(8,128)S(1)}, u32[]{:S(2)}, u32[]{:S(2)}) collective-permute-start(f32[7,32,128]{2,1,0:T(8,128)S(1)} %get-tuple-element.22), channel_id=1, source_target_pairs={{8,16},{16,8},{24,32},{32,24},{40,48},{48,40},{56,64},{64,56},{72,... | collective-permute-start | bytes 344072 | tf_op jit(solution)/shard_map/ppermute | solution.py:633
  15.7 0.0 collective-permute-done.o1_ref
  15.7 2.9 %collective-permute-done.1.o2_ref = f32[7,32,128]{2,1,0:T(8,128)S(1)} collective-permute-done((f32[7,32,128]{2,1,0:T(8,128)S(1)}, f32[7,32,128]{2,1,0:T(8,128)S(1)}, u32[]{:S(2)}, u32[]{:S(2)}) %collective-permute-start.1) | collective-permute-done | bytes 114720 | tf_op jit(solution)/shard_map/ppermute | solution.py:633
  18.6 0.0 collective-permute-done.2.h2_ref
  18.6 0.2 after_lon.1
  18.7 0.1 collective-permute-start.3
  18.8 4.4 %collective-permute-start.4 = (f32[10,8,128]{2,1,0:T(8,128)S(1)}, f32[10,8,128]{2,1,0:T(8,128)S(1)}, u32[]{:S(2)}, u32[]{:S(2)}) collective-permute-start(f32[10,8,128]{2,1,0:T(8,128)S(1)} %get-tuple-element.30), channel_id=1, source_target_pairs={{1,2},{2,1},{3,4},{4,3},{5,6},{6,5},{9,10},{10,9},{11,12},{12,11},... | collective-permute-start | bytes 122888 | tf_op jit(solution)/shard_map/ppermute | solution.py:642
  23.2 1.7 %collective-permute-done.4.lat2_ref.c2_ref = f32[10,8,128]{2,1,0:T(8,128)S(1)} collective-permute-done((f32[10,8,128]{2,1,0:T(8,128)S(1)}, f32[10,8,128]{2,1,0:T(8,128)S(1)}, u32[]{:S(2)}, u32[]{:S(2)}) %collective-permute-start.4) | collective-permute-done | bytes 40992 | tf_op jit(solution)/shard_map/ppermute | solution.py:642
  24.9 0.0 collective-permute-done.3.lat1_ref.h1_ref
  24.9 1.9 %krylov.1 = (f32[4,40,256]{2,1,0:T(8,128)S(1)}, f32[40,256]{1,0:T(8,128)S(1)}, f32[128,128]{1,0:T(8,128)}) custom-call(f32[3,32,256]{2,1,0:T(8,128)S(1)} %get-tuple-element.28.ext_ref, f32[88,8,128]{2,1,0:T(8,128)S(1)} %collective-permute-done.3.lat1_ref.h1_ref, f32[10,8,128]{2,1,0:T(8,128)S(1)} %collective-permute-done.4.lat2_ref.c2_ref), custom_call_target="tpu_custom_call" | custom-call | tf_op jit(solution)/shard_map/krylov/pallas_call | solution.py:602
  26.8 8.8 %all-to-all-start = ((f32[128,1,128]{2,1,0:T(1,128)}), f32[128,1,128]{2,1,0:T(1,128)S(1)}, u32[]{:S(2)}, u32[]{:S(2)}) async-start(f32[128,1,128]{2,1,0:T(1,128)} %bitcast.1), calls=%async_computation | async-start | bytes 131072 | tf_op jit(solution)/shard_map/all_to_all | solution.py:649
  35.5 5.2 %mixed_sweeps.1.swept = f32[2,50,32,128]{3,2,1,0:T(8,128)S(1)} custom-call(f32[40,256]{1,0:T(8,128)S(1)} %get-tuple-element.33.lev_ref, f32[2,6,2,32,128]{4,3,2,1,0:T(8,128)S(1)} %get-tuple-element.34.side_ref, f32[88,8,128]{2,1,0:T(8,128)S(1)} %collective-permute-done.3.lat1_ref.h1_ref, ...), custom_call_target="tpu_custom_call", output_to_operand_aliasing={{}: (5, {})} | custom-call | tf_op jit(solution)/shard_map/mixed_sweeps/pallas_call | solution.py:602
  40.7 4.1 %all-to-all-done = f32[128,1,128]{2,1,0:T(1,128)S(1)} async-done(((f32[128,1,128]{2,1,0:T(1,128)}), f32[128,1,128]{2,1,0:T(1,128)S(1)}, u32[]{:S(2)}, u32[]{:S(2)}) %all-to-all-start) | async-done | bytes 65568 | tf_op jit(solution)/shard_map/all_to_all | solution.py:649
  44.8 7.4 %sweeps.1 = (f32[2,50,32,128]{3,2,1,0:T(8,128)}, f32[2,50,32,128]{3,2,1,0:T(8,128)}, f32[32,128]{1,0:T(8,128)}) custom-call(f32[128,128]{1,0:T(8,128)S(1)} %bitcast.4, f32[4,40,256]{2,1,0:T(8,128)S(1)} %get-tuple-element.32.vec_ref, f32[40,256]{1,0:T(8,128)S(1)} %get-tuple-element.33.lev_ref, f32[2,6,2,32,128]{4,3,2,1,0:T(8,128)S(1)} %get-tuple-element.34.side_ref, ...), custom_call_target="tpu_custom_call" | custom-call | tf_op jit(solution)/shard_map/sweeps/pallas_call | solution.py:602
Async XLA Ops:
  5.3 13.3 %collective-permute-start.2 = (f32[78,8,128]{2,1,0:T(8,128)S(1)}, f32[78,8,128]{2,1,0:T(8,128)S(1)}, u32[]{:S(2)}, u32[]{:S(2)}) collective-permute-start(f32[78,8,128]{2,1,0:T(8,128)S(1)} %get-tuple-element.23), channel_id=1, source_target_pairs={{1,2},{2,1},{3,4},{4,3},{5,6},{6,5},{9,10},{10,9},{11,12},{12,11},... | collective-permute-start | bytes 958472 | tf_op jit(solution)/shard_map/ppermute | solution.py:631
  10.2 5.5 %collective-permute-start = (f32[7,32,128]{2,1,0:T(8,128)S(1)}, f32[7,32,128]{2,1,0:T(8,128)S(1)}, u32[]{:S(2)}, u32[]{:S(2)}) collective-permute-start(f32[7,32,128]{2,1,0:T(8,128)S(1)} %get-tuple-element.21), channel_id=1, source_target_pairs={{0,8},{8,0},{16,24},{24,16},{32,40},{40,32},{48,56},{56,48},{64,72... | collective-permute-start | bytes 344072 | tf_op jit(solution)/shard_map/ppermute | solution.py:632
  11.6 7.0 %collective-permute-start.1 = (f32[7,32,128]{2,1,0:T(8,128)S(1)}, f32[7,32,128]{2,1,0:T(8,128)S(1)}, u32[]{:S(2)}, u32[]{:S(2)}) collective-permute-start(f32[7,32,128]{2,1,0:T(8,128)S(1)} %get-tuple-element.22), channel_id=1, source_target_pairs={{8,16},{16,8},{24,32},{32,24},{40,48},{48,40},{56,64},{64,56},{72,... | collective-permute-start | bytes 344072 | tf_op jit(solution)/shard_map/ppermute | solution.py:633
  18.7 6.1 %collective-permute-start.3 = (f32[88,8,128]{2,1,0:T(8,128)S(1)}, f32[88,8,128]{2,1,0:T(8,128)S(1)}, u32[]{:S(2)}, u32[]{:S(2)}) collective-permute-start(f32[88,8,128]{2,1,0:T(8,128)S(1)} %get-tuple-element.29), channel_id=1, source_target_pairs={{0,1},{1,0},{2,3},{3,2},{4,5},{5,4},{6,7},{7,6},{8,9},{9,8},{10,11... | collective-permute-start | bytes 1081352 | tf_op jit(solution)/shard_map/ppermute | solution.py:641
  18.8 6.1 %collective-permute-start.4 = (f32[10,8,128]{2,1,0:T(8,128)S(1)}, f32[10,8,128]{2,1,0:T(8,128)S(1)}, u32[]{:S(2)}, u32[]{:S(2)}) collective-permute-start(f32[10,8,128]{2,1,0:T(8,128)S(1)} %get-tuple-element.30), channel_id=1, source_target_pairs={{1,2},{2,1},{3,4},{4,3},{5,6},{6,5},{9,10},{10,9},{11,12},{12,11},... | collective-permute-start | bytes 122888 | tf_op jit(solution)/shard_map/ppermute | solution.py:642
  26.8 18.1 %all-to-all-start = ((f32[128,1,128]{2,1,0:T(1,128)}), f32[128,1,128]{2,1,0:T(1,128)S(1)}, u32[]{:S(2)}, u32[]{:S(2)}) async-start(f32[128,1,128]{2,1,0:T(1,128)} %bitcast.1), calls=%async_computation | async-start | bytes 131072 | tf_op jit(solution)/shard_map/all_to_all | solution.py:649

commit v5 on v4

--- a/solution.py
+++ b/solution.py
@@ -79,6 +79,22 @@
     p, e = two_prod(a[0], r)
     rest = ((1.0 - p) - e) - a[1] * r
     return quick_sum(r, r * rest)
+
+
+PAIRED = (0, 1, 2, 5)
+LON_TILES = 2 + len(PAIRED)
+
+
+def put_tile(ref, i, x):
+    ref[4 * i : 4 * i + 4] = x.reshape(4, 8, COLS)
+
+
+def get_tile(ref, i):
+    return ref[4 * i : 4 * i + 4].reshape(ROWS, COLS)
+
+
+def quarter(at, *x):
+    return jnp.where(at < 2, jnp.where(at == 0, x[0], x[1]), jnp.where(at == 2, x[2], x[3]))
 
 
 def solve_kernel(
@@ -193,15 +209,24 @@
     base_ref[0] = f
     base_ref[2] = levels
     small = jnp.where(lane < 16, roll(f, 8, 1), jnp.where(lane < 32, roll(base_ref[1], 24, 1), roll(levels, 40, 1)))
-    lon1_ref[FIELDS] = small
-    lon2_ref[FIELDS] = small
-    near = lane % 4 < 2
-    for i in range(FIELDS):
+    put_tile(lon1_ref, 0, small)
+    put_tile(lon2_ref, 0, small)
+    at = lane % 4
+
+    def send(place, east_edge, west_edge):
+        put_tile(lon1_ref, place, pick(lon_par, east_edge, west_edge))
+        put_tile(lon2_ref, place, pick(lon_par, west_edge, east_edge))
+
+    for place, i in enumerate(PAIRED):
         a, b = slots_ref[i, 0], slots_ref[i, 1]
-        east_edge = jnp.where(near, a, roll(b, 2, 1))
-        west_edge = jnp.where(near, roll(a, COLS - 2, 1), b)
-        lon1_ref[i] = pick(lon_par, east_edge, west_edge)
-        lon2_ref[i] = pick(lon_par, west_edge, east_edge)
+        send(1 + place, jnp.where(at < 2, a, roll(b, 2, 1)), jnp.where(at < 2, roll(a, COLS - 2, 1), b))
+    va, vb, ta, tb = slots_ref[3, 0], slots_ref[3, 1], slots_ref[4, 0], slots_ref[4, 1]
+    send(
+        1 + len(PAIRED),
+        quarter(at, roll(ta, COLS - 1, 1), va, roll(tb, 1, 1), roll(vb, 2, 1)),
+        quarter(at, roll(vb, COLS - 2, 1), roll(tb, COLS - 1, 1), va, roll(ta, 1, 1)),
+    )
+    lon2_ref[4 * LON_TILES] = jnp.zeros((8, COLS), F32)
 
     pair = iota((8, COLS), 0) // 2
     for i, src in enumerate((mixed_ref, mixed_ref, vel, vel, tr, tr)):
@@ -228,7 +253,7 @@
     lon_par = lax.rem(lax.axis_index("lon"), 2)
     lat_par = lax.rem(lax.axis_index("lat"), 2)
     lane = iota((ROWS, COLS), 1)
-    o1, o2 = o1_ref[FIELDS], o2_ref[FIELDS]
+    o1, o2 = get_tile(o1_ref, 0), get_tile(o2_ref, 0)
     from_east, from_west = pick(lon_par, o1, o2), pick(lon_par, o2, o1)
     for i in range(3):
         own = base_ref[i]
@@ -242,14 +267,24 @@
             lat1_ref[EDGES + CORNERS + 2 * i + half] = pick(lat_par, last, first)
             lat2_ref[CORNERS + 2 * i + half] = pick(lat_par, first, last)
     near = lane % 4 < 2
-    for i in range(FIELDS):
-        b1, b2 = o1_ref[i], o2_ref[i]
-        east, west = pick(lon_par, b1, b2), pick(lon_par, b2, b1)
+
+    def receive(place):
+        b1, b2 = get_tile(o1_ref, place), get_tile(o2_ref, place)
+        return pick(lon_par, b1, b2), pick(lon_par, b2, b1)
+
+    def side_of(i, west_a, west_b, east_a, east_b):
         own_a, own_b = slots_ref[i, 0], slots_ref[i, 1]
-        side_ref[0, i, 0] = jnp.where(near, west, own_a)
-        side_ref[0, i, 1] = jnp.where(near, roll(west, COLS - 2, 1), own_b)
-        side_ref[1, i, 0] = jnp.where(near, own_a, roll(east, 2, 1))
-        side_ref[1, i, 1] = jnp.where(near, own_b, east)
+        side_ref[0, i, 0] = jnp.where(near, west_a, own_a)
+        side_ref[0, i, 1] = jnp.where(near, west_b, own_b)
+        side_ref[1, i, 0] = jnp.where(near, own_a, east_a)
+        side_ref[1, i, 1] = jnp.where(near, own_b, east_b)
+
+    for place, i in enumerate(PAIRED):
+        east, west = receive(1 + place)
+        side_of(i, west, roll(west, COLS - 2, 1), roll(east, 2, 1), east)
+    east, west = receive(1 + len(PAIRED))
+    side_of(3, west, roll(west, COLS - 2, 1), east, roll(east, 2, 1))
+    side_of(4, roll(west, 1, 1), roll(west, COLS - 1, 1), roll(east, COLS - 1, 1), roll(east, 1, 1))
     lat1_ref[:EDGES] = g1_ref[...]
     pair = iota((8, COLS), 0) // 2
     for c in range(CORNERS):
@@ -364,13 +399,14 @@
 
 SPANS = ((0, 12), (12, 26), (26, 38), (38, LEVELS))
 SPAN_LEVELS = 14
+PART_LEVELS = 8
 TALL = ROWS + 8
 BF16 = jnp.bfloat16
 
 
 class Sweeps:
-    def __init__(self, lev_ref, side_ref, h1_ref, h2_ref, c2_ref, lhs, weights):
-        self.lev_ref, self.side_ref, self.lhs = lev_ref, side_ref, lhs
+    def __init__(self, lev_ref, side_ref, h1_ref, h2_ref, c2_ref, weights):
+        self.lev_ref, self.side_ref = lev_ref, side_ref
         self.h1_ref, self.h2_ref, self.c2_ref = h1_ref, h2_ref, c2_ref
         shape = (COLS, COLS)
         source, target = iota(shape, 0), iota(shape, 1)
@@ -447,16 +483,22 @@
         hi, mid = (t.astype(F32) for t in self.parts(both))
         return jnp.where(at >= 2, hi, roll(mid, COLS - 2, 1))
 
-    def put(self, at, fields):
+    def put(self, lhs, at, fields):
         x = jnp.concatenate([f for f, _, _ in fields], axis=0)
         edge = [
             jnp.where(iota(e.shape, 1) // 4 == k % SLOTS, e, 0.0) for _, e, k in fields
         ]
         here = pl.ds(at, x.shape[0])
         hi, mid = self.parts(x)
-        self.lhs[here, :COLS] = hi
-        self.lhs[here, COLS : 2 * COLS] = mid
-        self.lhs[here, 2 * COLS :] = jnp.concatenate(edge, axis=0).astype(BF16)
+        lhs[here, :COLS] = hi
+        lhs[here, COLS : 2 * COLS] = mid
+        lhs[here, 2 * COLS :] = jnp.concatenate(edge, axis=0).astype(BF16)
+
+
+def halves(span, lhs, diff):
+    first, last = span
+    middle = first + (last - first) // 4 * 2
+    return [(a, b, l, d) for (a, b), l, d in zip(((first, middle), (middle, last)), lhs, diff)]
 
 
 def fetch(pairs, sem):
@@ -468,59 +510,77 @@
 
 
 def mixed_kernel(
-    lev_ref, side_ref, h1_ref, h2_ref, c2_ref, mixed, vel_h,
-    swept,
-    vel, edge1, edge2, lhs, diff, weights, in_sem,
+    lev_ref, side_ref, h1_ref, h2_ref, c2_ref, mixed, vel_h, tr_h,
+    swept, ties_h,
+    vel, tr, ties, edge1, edge2, edge3, lhs0, lhs1, diff0, diff1, weights, in_sem, out_sem,
 ):
-    reads = fetch(((vel_h, vel),), in_sem)
+    reads = fetch(((vel_h, vel), (tr_h, tr)), in_sem)
     for r in sum(reads, []):
         r.start()
-    sw = Sweeps(lev_ref, side_ref, h1_ref, h2_ref, c2_ref, lhs, weights)
+    sw = Sweeps(lev_ref, side_ref, h1_ref, h2_ref, c2_ref, weights)
     flux1, flux2 = sw.columns(lambda side, tile, column, wet: (column(0), column(1)))
     for tile in range(2):
         for n in range(2):
             edge1[n, tile] = sw.pack(flux1[0][tile][n], flux1[1][tile][n])
             edge2[n, tile] = sw.pack(flux2[0][tile][n], flux2[1][tile][n])
-    for (first, last), part in zip(SPANS, reads):
+            edge3[n, tile] = sw.pack(side_ref[0, 4 + n, tile], side_ref[1, 4 + n, tile])
+    writes = []
+    for span, part in zip(SPANS, reads):
         for r in part:
             r.wait()
-        rows = 0
-        for k in range(first, last):
-            u, tile = sw.tall(vel, 0, 2, k), k // SLOTS
-            sw.put(rows, [(u * sw.tall(mixed, n, n, k), edge1[n, tile], k) for n in range(2)])
-            rows += 2 * TALL
-        diff[:rows] = jnp.dot(lhs[:rows], weights[...], preferred_element_type=F32)
-        rows = 0
-        for k in range(first, last):
-            move, tile = COURANT * sw.wet(k, TALL), k // SLOTS
-            u, v = vel[0, k], sw.tall(vel, 1, 3, k)
-            fields = []
-            for n in range(2):
-                at = (2 * (k - first) + n) * TALL
-                x = sw.tall(mixed, n, n, k) + move * diff[at : at + TALL]
-                x = x + move * sw.meridional(v * x)
-                x = (x + move * sw.meridional(v * x))[:ROWS]
-                swept[n, k] = x
-                fields.append((u * x, edge2[n, tile], k))
-            sw.put(rows, fields)
-            rows += 2 * ROWS
-        diff[:rows] = jnp.dot(lhs[:rows], weights[...], preferred_element_type=F32)
-        for k in range(first, last):
-            move = COURANT * sw.wet(k, ROWS)
-            for n in range(2):
-                at = (2 * (k - first) + n) * ROWS
-                swept[n, k] = swept[n, k] + move * diff[at : at + ROWS]
+        parts = halves(span, (lhs0, lhs1), (diff0, diff1))
+        for first, last, lhs, diff in parts:
+            rows = 0
+            for k in range(first, last):
+                u, tile = sw.tall(vel, 0, 2, k), k // SLOTS
+                sw.put(lhs, rows, [(u * sw.tall(mixed, n, n, k), edge1[n, tile], k) for n in range(2)])
+                rows += 2 * TALL
+            diff[:rows] = jnp.dot(lhs[:rows], weights[...], preferred_element_type=F32)
+        for first, last, lhs, diff in parts:
+            rows = 0
+            for k in range(first, last):
+                move, tile = COURANT * sw.wet(k, TALL), k // SLOTS
+                u, v = vel[0, k], sw.tall(vel, 1, 3, k)
+                fields = []
+                for n in range(2):
+                    at = (2 * (k - first) + n) * TALL
+                    x = sw.tall(mixed, n, n, k) + move * diff[at : at + TALL]
+                    x = x + move * sw.meridional(v * x)
+                    x = (x + move * sw.meridional(v * x))[:ROWS]
+                    swept[n, k] = x
+                    fields.append((u * x, edge2[n, tile], k))
+                sw.put(lhs, rows, fields + [(tr[n, k], edge3[n, tile], k) for n in range(2)])
+                rows += 4 * ROWS
+            diff[:rows] = jnp.dot(lhs[:rows], weights[...], preferred_element_type=F32)
+        for first, last, lhs, diff in parts:
+            for k in range(first, last):
+                move, at = COURANT * sw.wet(k, ROWS), 4 * (k - first) * ROWS
+                x, east, north = [], [], []
+                for n in range(2):
+                    x.append(swept[n, k] + move * diff[at + n * ROWS : at + (n + 1) * ROWS])
+                    swept[n, k] = x[n]
+                    east.append(diff[at + (2 + n) * ROWS : at + (3 + n) * ROWS])
+                    north.append(sw.meridional(sw.tall(tr, n, 4 + n, k))[:ROWS])
+                for i, d in enumerate((east, north)):
+                    ties[2 * i, k] = -move * (x[0] * d[0] + x[1] * d[1])
+                    ties[2 * i + 1, k] = -move * (GAINS[0] * d[0] + GAINS[1] * d[1])
+        here = pl.ds(span[0], span[1] - span[0])
+        copy = pltpu.make_async_copy(ties.at[:, here], ties_h.at[:, here], out_sem.at[len(writes)])
+        copy.start()
+        writes.append(copy)
+    for copy in writes:
+        copy.wait()
 
 
 def final_kernel(
-    gram_ref, vec_ref, lev_ref, side_ref, h1_ref, h2_ref, c2_ref, swept, vel_h, tr_h,
+    gram_ref, vec_ref, lev_ref, side_ref, h1_ref, h2_ref, c2_ref, swept, vel_h, ties_h,
     adj_h, avel_h, sol_ref,
-    vel, tr, adj, avel, sol_s, edge1, edge2, edge3, late, lhs, diff, weights, in_sem, out_sem,
+    vel, ties, adj, avel, sol_s, edge1, edge2, late, lhs0, lhs1, diff0, diff1, weights, in_sem, out_sem,
 ):
-    reads = fetch(((vel_h, vel), (tr_h, tr)), in_sem)
+    reads = fetch(((vel_h, vel), (ties_h, ties)), in_sem)
     for r in sum(reads, []):
         r.start()
-    sw = Sweeps(lev_ref, side_ref, h1_ref, h2_ref, c2_ref, lhs, weights)
+    sw = Sweeps(lev_ref, side_ref, h1_ref, h2_ref, c2_ref, weights)
     coefs = galerkin(gram_ref[...])
     for half in range(2):
         at = half * COLS
@@ -534,47 +594,42 @@
     for tile in range(2):
         edge1[tile] = sw.pack(flux1[0][tile][0], flux1[1][tile][0])
         edge2[tile] = sw.pack(flux2[0][tile][0], flux2[1][tile][0])
-        for n in range(2):
-            edge3[n, tile] = sw.pack(side_ref[0, 4 + n, tile], side_ref[1, 4 + n, tile])
     writes = []
-    for (first, last), part in zip(SPANS, reads):
+    for span, part in zip(SPANS, reads):
         for r in part:
             r.wait()
-        rows = 0
-        for k in range(first, last, 2):
-            fields = []
-            for m in (k, k + 1):
-                x = sw.wet(m, TALL) * sol_s[:, :COLS]
-                fields.append((sw.tall(vel, 0, 2, m) * x, edge1[m // SLOTS], m))
-            sw.put(rows, fields)
-            rows += 2 * TALL
-        diff[:rows] = jnp.dot(lhs[:rows], weights[...], preferred_element_type=F32)
-        rows = 0
-        for k in range(first, last):
-            wet = sw.wet(k, TALL)
-            move, at = COURANT * wet, (k - first) * TALL
-            v = sw.tall(vel, 1, 3, k)
-            x = wet * sol_s[:, :COLS] + move * diff[at : at + TALL]
-            x = x + move * sw.meridional(v * x)
-            x = (x + move * sw.meridional(v * x))[:ROWS]
-            late[k - first] = x
-            tile = k // SLOTS
-            sw.put(rows, [(vel[0, k] * x, edge2[tile], k)] + [(tr[n, k], edge3[n, tile], k) for n in range(2)])
-            rows += 3 * ROWS
-        diff[:rows] = jnp.dot(lhs[:rows], weights[...], preferred_element_type=F32)
-        for k in range(first, last):
-            at = 3 * (k - first) * ROWS
-            move = COURANT * sw.wet(k, ROWS)
-            x = late[k - first] + move * diff[at : at + ROWS]
-            east_sum, north_sum = 0.0, 0.0
-            for n in range(2):
-                total = swept[n, k] + GAINS[n] * x
-                adj[n, k] = total
-                at += ROWS
-                east_sum = east_sum + total * diff[at : at + ROWS]
-                north_sum = north_sum + total * sw.meridional(sw.tall(tr, n, 4 + n, k))[:ROWS]
-            avel[0, k] = -move * east_sum
-            avel[1, k] = -move * north_sum
+        parts = halves(span, (lhs0, lhs1), (diff0, diff1))
+        for first, last, lhs, diff in parts:
+            rows = 0
+            for k in range(first, last, 2):
+                fields = []
+                for m in (k, k + 1):
+                    x = sw.wet(m, TALL) * sol_s[:, :COLS]
+                    fields.append((sw.tall(vel, 0, 2, m) * x, edge1[m // SLOTS], m))
+                sw.put(lhs, rows, fields)
+                rows += 2 * TALL
+            diff[:rows] = jnp.dot(lhs[:rows], weights[...], preferred_element_type=F32)
+        for first, last, lhs, diff in parts:
+            rows = 0
+            for k in range(first, last):
+                wet = sw.wet(k, TALL)
+                move, at = COURANT * wet, (k - first) * TALL
+                v = sw.tall(vel, 1, 3, k)
+                x = wet * sol_s[:, :COLS] + move * diff[at : at + TALL]
+                x = x + move * sw.meridional(v * x)
+                x = (x + move * sw.meridional(v * x))[:ROWS]
+                late[k - span[0]] = x
+                sw.put(lhs, rows, [(vel[0, k] * x, edge2[k // SLOTS], k)])
+                rows += ROWS
+            diff[:rows] = jnp.dot(lhs[:rows], weights[...], preferred_element_type=F32)
+        for first, last, lhs, diff in parts:
+            for k in range(first, last):
+                at = (k - first) * ROWS
+                x = late[k - span[0]] + COURANT * sw.wet(k, ROWS) * diff[at : at + ROWS]
+                for n in range(2):
+                    adj[n, k] = swept[n, k] + GAINS[n] * x
+                    avel[n, k] = ties[2 * n, k] + ties[2 * n + 1, k] * x
+        first, last = span
         here = pl.ds(first, last - first)
         for i, (src, dst) in enumerate(((adj, adj_h), (avel, avel_h))):
             copy = pltpu.make_async_copy(src.at[:, here], dst.at[:, here], out_sem.at[len(writes) // 2, i])
@@ -621,7 +676,7 @@
     deep = (2, LEVELS) + tile
     mixed, base, lon1, lon2, slots, g1, g2 = call(
         solve_kernel, "column_solve", (True,) * 7,
-        (kept(*deep), kept(3, *tile), kept(FIELDS + 1, *tile), kept(FIELDS + 1, *tile),
+        (kept(*deep), kept(3, *tile), kept(4 * LON_TILES, 8, COLS), kept(4 * LON_TILES + 1, 8, COLS),
          kept(FIELDS, 2, *tile), kept(FIELDS * GROUPS, 8, COLS), kept(FIELDS * GROUPS, 8, COLS)),
         [VMEM(deep, F32), VMEM(deep, F32), VMEM(deep, F32), VMEM((LEVELS,) + tile, F32), VMEM(tile, F32), VMEM(tile, jnp.int32),
          VMEM((LEVELS,) + tile, F32), VMEM(deep, F32),
@@ -647,24 +702,24 @@
         (ext, lat1, lat2),
     )
     gram = lax.all_to_all(gram, ("lon", "lat"), 0, 0, tiled=True)
-    rows = SPAN_LEVELS * 2 * TALL
-    (swept,) = call(
-        mixed_kernel, "mixed_sweeps", (False,) * 6 + (True,),
-        (kept(*deep),),
-        [VMEM(deep, F32), VMEM((2, 2, TALL, COLS), F32), VMEM((2, 2) + tile, F32),
-         VMEM((rows, 3 * COLS), BF16), VMEM((rows, COLS), F32), VMEM((3 * COLS, COLS), BF16),
-         pltpu.SemaphoreType.DMA((len(SPANS), 1))],
-        (lev, side, lat1, h2, lat2, mixed, velocity), {5: 0},
+    rows, many = PART_LEVELS * 4 * ROWS, (4, LEVELS) + tile
+    swept, ties = call(
+        mixed_kernel, "mixed_sweeps", (False,) * 6 + (True,) * 2,
+        (kept(*deep), (pltpu.HBM(many, F32), True)),
+        [VMEM(deep, F32), VMEM(deep, F32), VMEM(many, F32), VMEM((2, 2, TALL, COLS), F32), VMEM((2, 2) + tile, F32), VMEM((2, 2) + tile, F32),
+         VMEM((rows, 3 * COLS), BF16), VMEM((rows, 3 * COLS), BF16), VMEM((rows, COLS), F32), VMEM((rows, COLS), F32), VMEM((3 * COLS, COLS), BF16),
+         pltpu.SemaphoreType.DMA((len(SPANS), 2)), pltpu.SemaphoreType.DMA((len(SPANS),))],
+        (lev, side, lat1, h2, lat2, mixed, velocity, tracer), {5: 0},
     )
-    rows = SPAN_LEVELS * 3 * ROWS
+    rows = PART_LEVELS * TALL
     return call(
         final_kernel, "sweeps", (False,) * 8 + (True,) * 2,
         ((shape(*deep), True), (shape(*deep), True), (shape(*tile), False)),
-        [VMEM(deep, F32), VMEM(deep, F32), VMEM(deep, F32), VMEM(deep, F32), VMEM((TALL, 2 * COLS), F32),
-         VMEM((2, TALL, COLS), F32), VMEM((2,) + tile, F32), VMEM((2, 2) + tile, F32), VMEM((SPAN_LEVELS,) + tile, F32),
-         VMEM((rows, 3 * COLS), BF16), VMEM((rows, COLS), F32), VMEM((3 * COLS, COLS), BF16),
+        [VMEM(deep, F32), VMEM(many, F32), VMEM(deep, F32), VMEM(deep, F32), VMEM((TALL, 2 * COLS), F32),
+         VMEM((2, TALL, COLS), F32), VMEM((2,) + tile, F32), VMEM((SPAN_LEVELS,) + tile, F32),
+         VMEM((rows, 3 * COLS), BF16), VMEM((rows, 3 * COLS), BF16), VMEM((rows, COLS), F32), VMEM((rows, COLS), F32), VMEM((3 * COLS, COLS), BF16),
          pltpu.SemaphoreType.DMA((len(SPANS), 2)), pltpu.SemaphoreType.DMA((len(SPANS), 2))],
-        (gram, vec, lev, side, lat1, h2, lat2, swept, velocity, tracer),
+        (gram, vec, lev, side, lat1, h2, lat2, swept, velocity, ties),
     )
 
 

time: 52.5 us -> 50.4 us (0.960)
  waiting for transfers between devices: 8.65 us -> 6.74 us
  starting transfers between devices: 23.6 us -> 22 us
  Pallas kernels: 19.2 us -> 20.6 us
    ppermute x1, waiting for transfers between devices: 0.01 us -> 3.46 us  [per_device(): o1 = lax.ppermute(lon1, 'lon', swaps(lon, 0, True))]
    ppermute x1, waiting for transfers between devices: 2.86 us -> 0.01 us  [per_device(): o2 = lax.ppermute(lon2, 'lon', swaps(lon, 1, True))]
    all_to_all x1, waiting for transfers between devices: 4.11 us -> 1.6 us  [per_device(): gram = lax.all_to_all(gram, ('lon', 'lat'), 0, 0, tiled=True)]
    pallas_call x5, Pallas kernels: 19.2 us -> 20.6 us  [call(): pl.pallas_call(kernel, name=name, out_shape=tuple((o for o, _ in outs)),...]
    ppermute x1, starting transfers between devices: 1.38 us -> 0.01 us  [per_device(): o1 = lax.ppermute(lon1, 'lon', swaps(lon, 0, True))]
    all_to_all x1, starting transfers between devices: 8.77 us -> 7.8 us  [per_device(): gram = lax.all_to_all(gram, ('lon', 'lat'), 0, 0, tiled=True)]
    ppermute x1, starting transfers between devices: 4.1 us -> 5.01 us  [per_device(): o2 = lax.ppermute(lon2, 'lon', swaps(lon, 1, True))]
  transfers between devices with their start and end apart: 6 -> 6, of which waited for: 3 -> 3; matrix products, arithmetic and copies ran while one was open for 0% -> 0% of each run, Pallas kernels for 10% -> 15%
where the time goes in v5:
time: 50.4 us; the launch traced here: 50.2 us
  starting transfers between devices  22 us (44%)
  Pallas kernels  20.6 us (41%)
  waiting for transfers between devices  6.74 us (13%)
  between operations  0.85 us (2%)
    pallas_call x5, Pallas kernels, call(): pl.pallas_call(kernel, name=name, out_shape=tuple((o for o, _ in outs)),...  20.6 us
    all_to_all x1, starting transfers between devices, per_device(): gram = lax.all_to_all(gram, ('lon', 'lat'), 0, 0, tiled=True)  7.8 us
    ppermute x1, starting transfers between devices, per_device(): o2 = lax.ppermute(lon2, 'lon', swaps(lon, 1, True))  5.01 us
    ppermute x1, starting transfers between devices, per_device(): h2 = lax.ppermute(g2, 'lat', swaps(lat, 1, False))  4.94 us
    ppermute x1, starting transfers between devices, per_device(): lat2 = lax.ppermute(lat2, 'lat', swaps(lat, 1, False))  4.2 us
    ppermute x1, waiting for transfers between devices, per_device(): o1 = lax.ppermute(lon1, 'lon', swaps(lon, 0, True))  3.46 us
    ppermute x1, waiting for transfers between devices, per_device(): lat2 = lax.ppermute(lat2, 'lat', swaps(lat, 1, False))  1.67 us
    all_to_all x1, waiting for transfers between devices, per_device(): gram = lax.all_to_all(gram, ('lon', 'lat'), 0, 0, tiled=True)  1.6 us
  transfers between devices with their start and end apart: 6, of which 3 were waited for; matrix products, arithmetic and copies ran while one was open for 0% of the time, Pallas kernels for 15%

profile of v5, /device:TPU:1, one launch (start us, length us, event | category | flops | bytes accessed | tf_op | source)
XLA Modules:
  0.0 50.2 jit_solution(2542036954090503266)
XLA Ops:
  0.6 4.7 %column_solve.1 = (f32[2,50,32,128]{3,2,1,0:T(8,128)S(1)}, f32[3,32,128]{2,1,0:T(8,128)S(1)}, f32[24,8,128]{2,1,0:T(8,128)S(1)}, f32[25,8,128]{2,1,0:T(8,128)S(1...) custom-call(f32[2,50,32,128]{3,2,1,0:T(8,128)} %lam_h.1, ...), custom_call_target="tpu_custom_call" | custom-call | tf_op jit(solution)/shard_map/column_solve/pallas_call | solution.py:657
  5.3 4.9 %collective-permute-start.2 = (f32[78,8,128]{2,1,0:T(8,128)S(1)}, f32[78,8,128]{2,1,0:T(8,128)S(1)}, u32[]{:S(2)}, u32[]{:S(2)}) collective-permute-start(f32[78,8,128]{2,1,0:T(8,128)S(1)} %get-tuple-element.25), channel_id=1, source_target_pairs={{1,2},{2,1},{3,4},{4,3},{5,6},{6,5},{9,10},{10,9},{11,12},{12,11},... | collective-permute-start | bytes 958472 | tf_op jit(solution)/shard_map/ppermute | solution.py:686
  10.2 5.0 %collective-permute-start.1 = (f32[25,8,128]{2,1,0:T(8,128)S(1)}, f32[25,8,128]{2,1,0:T(8,128)S(1)}, u32[]{:S(2)}, u32[]{:S(2)}) collective-permute-start(f32[25,8,128]{2,1,0:T(8,128)S(1)} %get-tuple-element.24), channel_id=1, source_target_pairs={{8,16},{16,8},{24,32},{32,24},{40,48},{48,40},{56,64},{64,56},{72,... | collective-permute-start | bytes 307208 | tf_op jit(solution)/shard_map/ppermute | solution.py:688
  15.3 0.0 collective-permute-start
  15.3 3.5 %collective-permute-done.o1_ref = f32[24,8,128]{2,1,0:T(8,128)S(1)} collective-permute-done((f32[24,8,128]{2,1,0:T(8,128)S(1)}, f32[24,8,128]{2,1,0:T(8,128)S(1)}, u32[]{:S(2)}, u32[]{:S(2)}) %collective-permute-start) | collective-permute-done | bytes 98336 | tf_op jit(solution)/shard_map/ppermute | solution.py:687
  18.7 0.0 collective-permute-done.1.o2_ref
  18.7 0.0 collective-permute-done.2.h2_ref
  18.7 0.2 after_lon.1
  18.9 0.1 collective-permute-start.3
  19.0 4.2 %collective-permute-start.4 = (f32[10,8,128]{2,1,0:T(8,128)S(1)}, f32[10,8,128]{2,1,0:T(8,128)S(1)}, u32[]{:S(2)}, u32[]{:S(2)}) collective-permute-start(f32[10,8,128]{2,1,0:T(8,128)S(1)} %get-tuple-element.32), channel_id=1, source_target_pairs={{1,2},{2,1},{3,4},{4,3},{5,6},{6,5},{9,10},{10,9},{11,12},{12,11},... | collective-permute-start | bytes 122888 | tf_op jit(solution)/shard_map/ppermute | solution.py:697
  23.2 1.7 %collective-permute-done.4.lat2_ref.c2_ref = f32[10,8,128]{2,1,0:T(8,128)S(1)} collective-permute-done((f32[10,8,128]{2,1,0:T(8,128)S(1)}, f32[10,8,128]{2,1,0:T(8,128)S(1)}, u32[]{:S(2)}, u32[]{:S(2)}) %collective-permute-start.4) | collective-permute-done | bytes 40992 | tf_op jit(solution)/shard_map/ppermute | solution.py:697
  24.9 0.0 collective-permute-done.3.lat1_ref.h1_ref
  24.9 1.9 %krylov.1 = (f32[4,40,256]{2,1,0:T(8,128)S(1)}, f32[40,256]{1,0:T(8,128)S(1)}, f32[128,128]{1,0:T(8,128)}) custom-call(f32[3,32,256]{2,1,0:T(8,128)S(1)} %get-tuple-element.30.ext_ref, f32[88,8,128]{2,1,0:T(8,128)S(1)} %collective-permute-done.3.lat1_ref.h1_ref, f32[10,8,128]{2,1,0:T(8,128)S(1)} %collective-permute-done.4.lat2_ref.c2_ref), custom_call_target="tpu_custom_call" | custom-call | tf_op jit(solution)/shard_map/krylov/pallas_call | solution.py:657
  26.7 7.8 %all-to-all-start = ((f32[128,1,128]{2,1,0:T(1,128)}), f32[128,1,128]{2,1,0:T(1,128)S(1)}, u32[]{:S(2)}, u32[]{:S(2)}) async-start(f32[128,1,128]{2,1,0:T(1,128)} %bitcast.1), calls=%async_computation | async-start | bytes 131072 | tf_op jit(solution)/shard_map/all_to_all | solution.py:704
  34.5 7.7 %mixed_sweeps.1 = (f32[2,50,32,128]{3,2,1,0:T(8,128)S(1)}, f32[4,50,32,128]{3,2,1,0:T(8,128)}) custom-call(f32[40,256]{1,0:T(8,128)S(1)} %get-tuple-element.35.lev_ref, f32[2,6,2,32,128]{4,3,2,1,0:T(8,128)S(1)} %get-tuple-element.36.side_ref, f32[88,8,128]{2,1,0:T(8,128)S(1)} %collective-permute-done.3.lat1_ref.h1_ref, ...), custom_call_target="tpu_custom_call", output_to_operand_aliasing={{0}: (5, {})} | custom-call | tf_op jit(solution)/shard_map/mixed_sweeps/pallas_call | solution.py:657
  42.2 1.6 %all-to-all-done = f32[128,1,128]{2,1,0:T(1,128)S(1)} async-done(((f32[128,1,128]{2,1,0:T(1,128)}), f32[128,1,128]{2,1,0:T(1,128)S(1)}, u32[]{:S(2)}, u32[]{:S(2)}) %all-to-all-start) | async-done | bytes 65568 | tf_op jit(solution)/shard_map/all_to_all | solution.py:704
  43.8 6.2 %sweeps.1 = (f32[2,50,32,128]{3,2,1,0:T(8,128)}, f32[2,50,32,128]{3,2,1,0:T(8,128)}, f32[32,128]{1,0:T(8,128)}) custom-call(f32[128,128]{1,0:T(8,128)S(1)} %bitcast.4, f32[4,40,256]{2,1,0:T(8,128)S(1)} %get-tuple-element.34.vec_ref, f32[40,256]{1,0:T(8,128)S(1)} %get-tuple-element.35.lev_ref, f32[2,6,2,32,128]{4,3,2,1,0:T(8,128)S(1)} %get-tuple-element.36.side_ref, ...), custom_call_target="tpu_custom_call" | custom-call | tf_op jit(solution)/shard_map/sweeps/pallas_call | solution.py:657
Async XLA Ops:
  5.3 13.4 %collective-permute-start.2 = (f32[78,8,128]{2,1,0:T(8,128)S(1)}, f32[78,8,128]{2,1,0:T(8,128)S(1)}, u32[]{:S(2)}, u32[]{:S(2)}) collective-permute-start(f32[78,8,128]{2,1,0:T(8,128)S(1)} %get-tuple-element.25), channel_id=1, source_target_pairs={{1,2},{2,1},{3,4},{4,3},{5,6},{6,5},{9,10},{10,9},{11,12},{12,11},... | collective-permute-start | bytes 958472 | tf_op jit(solution)/shard_map/ppermute | solution.py:686
  10.2 8.5 %collective-permute-start.1 = (f32[25,8,128]{2,1,0:T(8,128)S(1)}, f32[25,8,128]{2,1,0:T(8,128)S(1)}, u32[]{:S(2)}, u32[]{:S(2)}) collective-permute-start(f32[25,8,128]{2,1,0:T(8,128)S(1)} %get-tuple-element.24), channel_id=1, source_target_pairs={{8,16},{16,8},{24,32},{32,24},{40,48},{48,40},{56,64},{64,56},{72,... | collective-permute-start | bytes 307208 | tf_op jit(solution)/shard_map/ppermute | solution.py:688
  15.3 3.5 %collective-permute-start = (f32[24,8,128]{2,1,0:T(8,128)S(1)}, f32[24,8,128]{2,1,0:T(8,128)S(1)}, u32[]{:S(2)}, u32[]{:S(2)}) collective-permute-start(f32[24,8,128]{2,1,0:T(8,128)S(1)} %get-tuple-element.23), channel_id=1, source_target_pairs={{0,8},{8,0},{16,24},{24,16},{32,40},{40,32},{48,56},{56,48},{64,72... | collective-permute-start | bytes 294920 | tf_op jit(solution)/shard_map/ppermute | solution.py:687
  18.9 6.0 %collective-permute-start.3 = (f32[88,8,128]{2,1,0:T(8,128)S(1)}, f32[88,8,128]{2,1,0:T(8,128)S(1)}, u32[]{:S(2)}, u32[]{:S(2)}) collective-permute-start(f32[88,8,128]{2,1,0:T(8,128)S(1)} %get-tuple-element.31), channel_id=1, source_target_pairs={{0,1},{1,0},{2,3},{3,2},{4,5},{5,4},{6,7},{7,6},{8,9},{9,8},{10,11... | collective-permute-start | bytes 1081352 | tf_op jit(solution)/shard_map/ppermute | solution.py:696
  19.0 5.9 %collective-permute-start.4 = (f32[10,8,128]{2,1,0:T(8,128)S(1)}, f32[10,8,128]{2,1,0:T(8,128)S(1)}, u32[]{:S(2)}, u32[]{:S(2)}) collective-permute-start(f32[10,8,128]{2,1,0:T(8,128)S(1)} %get-tuple-element.32), channel_id=1, source_target_pairs={{1,2},{2,1},{3,4},{4,3},{5,6},{6,5},{9,10},{10,9},{11,12},{12,11},... | collective-permute-start | bytes 122888 | tf_op jit(solution)/shard_map/ppermute | solution.py:697
  26.7 17.1 %all-to-all-start = ((f32[128,1,128]{2,1,0:T(1,128)}), f32[128,1,128]{2,1,0:T(1,128)S(1)}, u32[]{:S(2)}, u32[]{:S(2)}) async-start(f32[128,1,128]{2,1,0:T(1,128)} %bitcast.1), calls=%async_computation | async-start | bytes 131072 | tf_op jit(solution)/shard_map/all_to_all | solution.py:704

commit v6 on v5

--- a/solution.py
+++ b/solution.py
@@ -249,7 +249,7 @@
     return index // 8, index // 2 % 4, index % 2
 
 
-def lon_kernel(base_ref, o1_ref, o2_ref, slots_ref, g1_ref, ext_ref, lat1_ref, lat2_ref, side_ref):
+def lon_kernel(base_ref, o1_ref, o2_ref, slots_ref, ext_ref, lat1_ref, lat2_ref, side_ref):
     lon_par = lax.rem(lax.axis_index("lon"), 2)
     lat_par = lax.rem(lax.axis_index("lat"), 2)
     lane = iota((ROWS, COLS), 1)
@@ -264,8 +264,9 @@
         ext_ref[i, :, COLS:] = edge
         for half, here in enumerate((own, edge)):
             first, last = here[:8], here[ROWS - 8 :]
-            lat1_ref[EDGES + CORNERS + 2 * i + half] = pick(lat_par, last, first)
+            lat1_ref[CORNERS + 2 * i + half] = pick(lat_par, last, first)
             lat2_ref[CORNERS + 2 * i + half] = pick(lat_par, first, last)
+    lat2_ref[CORNERS + 6] = jnp.zeros((8, COLS), F32)
     near = lane % 4 < 2
 
     def receive(place):
@@ -285,7 +286,6 @@
     east, west = receive(1 + len(PAIRED))
     side_of(3, west, roll(west, COLS - 2, 1), east, roll(east, 2, 1))
     side_of(4, roll(west, 1, 1), roll(west, COLS - 1, 1), roll(east, COLS - 1, 1), roll(east, 1, 1))
-    lat1_ref[:EDGES] = g1_ref[...]
     pair = iota((8, COLS), 0) // 2
     for c in range(CORNERS):
         first = jnp.zeros((8, COLS), F32)
@@ -295,7 +295,7 @@
             x = side_ref[side, field, tile]
             first = jnp.where(pair == q, roll(x[:8], 2 * q, 0) if q else x[:8], first)
             last = jnp.where(pair == (q + 3) % 4, roll(x[ROWS - 8 :], 2 * q, 0) if q else x[ROWS - 8 :], last)
-        lat1_ref[EDGES + c] = pick(lat_par, last, first)
+        lat1_ref[c] = pick(lat_par, last, first)
         lat2_ref[c] = pick(lat_par, first, last)
 
 
@@ -304,7 +304,7 @@
     rows, cols = ROWS + 16, 2 * COLS
     whole = []
     for i in range(3):
-        s1 = jnp.concatenate([lat1_ref[EDGES + CORNERS + 2 * i + half] for half in range(2)], axis=1)
+        s1 = jnp.concatenate([lat1_ref[CORNERS + 2 * i + half] for half in range(2)], axis=1)
         s2 = jnp.concatenate([lat2_ref[CORNERS + 2 * i + half] for half in range(2)], axis=1)
         whole.append(jnp.concatenate([ext_ref[i], pick(lat_par, s1, s2), pick(lat_par, s2, s1)], axis=0))
     f, depth, lev = whole
@@ -397,7 +397,7 @@
     return [r[0] for r in rhs]
 
 
-SPANS = ((0, 12), (12, 26), (26, 38), (38, LEVELS))
+SPANS = ((0, 8), (8, 20), (20, 32), (32, 44), (44, LEVELS))
 SPAN_LEVELS = 14
 PART_LEVELS = 8
 TALL = ROWS + 8
@@ -405,9 +405,9 @@
 
 
 class Sweeps:
-    def __init__(self, lev_ref, side_ref, h1_ref, h2_ref, c2_ref, weights):
+    def __init__(self, lev_ref, side_ref, h1_ref, h2_ref, c1_ref, c2_ref, weights):
         self.lev_ref, self.side_ref = lev_ref, side_ref
-        self.h1_ref, self.h2_ref, self.c2_ref = h1_ref, h2_ref, c2_ref
+        self.deep, self.corners = (h1_ref, h2_ref), (c1_ref, c2_ref)
         shape = (COLS, COLS)
         source, target = iota(shape, 0), iota(shape, 1)
         shift = jnp.where(source == target + 1, 1.0, jnp.where(source == target - 1, -1.0, 0.0)).astype(BF16)
@@ -423,8 +423,8 @@
         self.masks = [(pair == q) == even for q in range(4)]
 
     def edge_rows(self, index, q):
-        other = self.h2_ref[index] if index < EDGES else self.c2_ref[index - EDGES]
-        x = jnp.where(self.masks[q], self.h1_ref[index], other)
+        one, two = (r[index] for r in self.deep) if index < EDGES else (r[index - EDGES] for r in self.corners)
+        x = jnp.where(self.masks[q], one, two)
         return roll(x, 8 - 2 * q, 0) if q else x
 
     def tall(self, ref, n, field, k):
@@ -510,14 +510,14 @@
 
 
 def mixed_kernel(
-    lev_ref, side_ref, h1_ref, h2_ref, c2_ref, mixed, vel_h, tr_h,
+    lev_ref, side_ref, h1_ref, h2_ref, c1_ref, c2_ref, mixed, vel_h, tr_h,
     swept, ties_h,
     vel, tr, ties, edge1, edge2, edge3, lhs0, lhs1, diff0, diff1, weights, in_sem, out_sem,
 ):
     reads = fetch(((vel_h, vel), (tr_h, tr)), in_sem)
     for r in sum(reads, []):
         r.start()
-    sw = Sweeps(lev_ref, side_ref, h1_ref, h2_ref, c2_ref, weights)
+    sw = Sweeps(lev_ref, side_ref, h1_ref, h2_ref, c1_ref, c2_ref, weights)
     flux1, flux2 = sw.columns(lambda side, tile, column, wet: (column(0), column(1)))
     for tile in range(2):
         for n in range(2):
@@ -573,14 +573,14 @@
 
 
 def final_kernel(
-    gram_ref, vec_ref, lev_ref, side_ref, h1_ref, h2_ref, c2_ref, swept, vel_h, ties_h,
+    gram_ref, vec_ref, lev_ref, side_ref, h1_ref, h2_ref, c1_ref, c2_ref, swept, vel_h, ties_h,
     adj_h, avel_h, sol_ref,
     vel, ties, adj, avel, sol_s, edge1, edge2, late, lhs0, lhs1, diff0, diff1, weights, in_sem, out_sem,
 ):
     reads = fetch(((vel_h, vel), (ties_h, ties)), in_sem)
     for r in sum(reads, []):
         r.start()
-    sw = Sweeps(lev_ref, side_ref, h1_ref, h2_ref, c2_ref, weights)
+    sw = Sweeps(lev_ref, side_ref, h1_ref, h2_ref, c1_ref, c2_ref, weights)
     coefs = galerkin(gram_ref[...])
     for half in range(2):
         at = half * COLS
@@ -683,15 +683,16 @@
          pltpu.SemaphoreType.DMA((HALF // 5, 4)), pltpu.SemaphoreType.DMA((5,))],
         (lam_tracer, velocity, tracer, diffusivity, lam_surface, sea_depth, levels),
     )
+    h1 = lax.ppermute(g1, "lat", swaps(lat, 0, False))
     h2 = lax.ppermute(g2, "lat", swaps(lat, 1, False))
     o1 = lax.ppermute(lon1, "lon", swaps(lon, 0, True))
     o2 = lax.ppermute(lon2, "lon", swaps(lon, 1, True))
-    o1, o2, h2 = lax.optimization_barrier((o1, o2, h2))
+    o1, o2, h1, h2 = lax.optimization_barrier((o1, o2, h1, h2))
     ext, lat1, lat2, side = call(
-        lon_kernel, "after_lon", (False,) * 5,
-        (kept(3, ROWS, 2 * COLS), kept(EDGES + CORNERS + 6, 8, COLS), kept(CORNERS + 6, 8, COLS), kept(2, FIELDS, 2, *tile)),
+        lon_kernel, "after_lon", (False,) * 4,
+        (kept(3, ROWS, 2 * COLS), kept(CORNERS + 6, 8, COLS), kept(CORNERS + 7, 8, COLS), kept(2, FIELDS, 2, *tile)),
         [],
-        (base, o1, o2, slots, g1),
+        (base, o1, o2, slots),
     )
     lat1 = lax.ppermute(lat1, "lat", swaps(lat, 0, False))
     lat2 = lax.ppermute(lat2, "lat", swaps(lat, 1, False))
@@ -704,22 +705,22 @@
     gram = lax.all_to_all(gram, ("lon", "lat"), 0, 0, tiled=True)
     rows, many = PART_LEVELS * 4 * ROWS, (4, LEVELS) + tile
     swept, ties = call(
-        mixed_kernel, "mixed_sweeps", (False,) * 6 + (True,) * 2,
+        mixed_kernel, "mixed_sweeps", (False,) * 7 + (True,) * 2,
         (kept(*deep), (pltpu.HBM(many, F32), True)),
         [VMEM(deep, F32), VMEM(deep, F32), VMEM(many, F32), VMEM((2, 2, TALL, COLS), F32), VMEM((2, 2) + tile, F32), VMEM((2, 2) + tile, F32),
          VMEM((rows, 3 * COLS), BF16), VMEM((rows, 3 * COLS), BF16), VMEM((rows, COLS), F32), VMEM((rows, COLS), F32), VMEM((3 * COLS, COLS), BF16),
          pltpu.SemaphoreType.DMA((len(SPANS), 2)), pltpu.SemaphoreType.DMA((len(SPANS),))],
-        (lev, side, lat1, h2, lat2, mixed, velocity, tracer), {5: 0},
+        (lev, side, h1, h2, lat1, lat2, mixed, velocity, tracer), {6: 0},
     )
     rows = PART_LEVELS * TALL
     return call(
-        final_kernel, "sweeps", (False,) * 8 + (True,) * 2,
+        final_kernel, "sweeps", (False,) * 9 + (True,) * 2,
         ((shape(*deep), True), (shape(*deep), True), (shape(*tile), False)),
         [VMEM(deep, F32), VMEM(many, F32), VMEM(deep, F32), VMEM(deep, F32), VMEM((TALL, 2 * COLS), F32),
          VMEM((2, TALL, COLS), F32), VMEM((2,) + tile, F32), VMEM((SPAN_LEVELS,) + tile, F32),
          VMEM((rows, 3 * COLS), BF16), VMEM((rows, 3 * COLS), BF16), VMEM((rows, COLS), F32), VMEM((rows, COLS), F32), VMEM((3 * COLS, COLS), BF16),
          pltpu.SemaphoreType.DMA((len(SPANS), 2)), pltpu.SemaphoreType.DMA((len(SPANS), 2))],
-        (gram, vec, lev, side, lat1, h2, lat2, swept, velocity, ties),
+        (gram, vec, lev, side, h1, h2, lat1, lat2, swept, velocity, ties),
     )
 
 

time: 50.4 us -> 50.2 us (level)
    ppermute x0 -> x1, starting transfers between devices: none -> 1.5 us  [per_device(): h1 = lax.ppermute(g1, 'lat', swaps(lat, 0, False))]
    ppermute x1, starting transfers between devices: 4.94 us -> 3.53 us  [per_device(): h2 = lax.ppermute(g2, 'lat', swaps(lat, 1, False))]
    ppermute x1, waiting for transfers between devices: 1.67 us -> 0.42 us  [per_device(): lat2 = lax.ppermute(lat2, 'lat', swaps(lat, 1, False))]
    ppermute x1, waiting for transfers between devices: 0.01 us -> 1.21 us  [per_device(): lat1 = lax.ppermute(lat1, 'lat', swaps(lat, 0, False))]
  transfers between devices with their start and end apart: 6 -> 7, of which waited for: 3 -> 4; matrix products, arithmetic and copies ran while one was open for 0% -> 0% of each run, Pallas kernels for 15% -> 15%
where the time goes in v6:
time: 50.2 us; the launch traced here: 50.1 us
  starting transfers between devices  22 us (44%)
  Pallas kernels  20.5 us (41%)
  waiting for transfers between devices  6.77 us (13%)
  between operations  0.86 us (2%)
    pallas_call x5, Pallas kernels, call(): pl.pallas_call(kernel, name=name, out_shape=tuple((o for o, _ in outs)),...  20.5 us
    all_to_all x1, starting transfers between devices, per_device(): gram = lax.all_to_all(gram, ('lon', 'lat'), 0, 0, tiled=True)  7.81 us
    ppermute x1, starting transfers between devices, per_device(): o2 = lax.ppermute(lon2, 'lon', swaps(lon, 1, True))  5.01 us
    ppermute x1, starting transfers between devices, per_device(): lat2 = lax.ppermute(lat2, 'lat', swaps(lat, 1, False))  4.06 us
    ppermute x1, starting transfers between devices, per_device(): h2 = lax.ppermute(g2, 'lat', swaps(lat, 1, False))  3.53 us
    ppermute x1, waiting for transfers between devices, per_device(): o1 = lax.ppermute(lon1, 'lon', swaps(lon, 0, True))  3.46 us
    all_to_all x1, waiting for transfers between devices, per_device(): gram = lax.all_to_all(gram, ('lon', 'lat'), 0, 0, tiled=True)  1.67 us
    ppermute x1, starting transfers between devices, per_device(): h1 = lax.ppermute(g1, 'lat', swaps(lat, 0, False))  1.5 us
  transfers between devices with their start and end apart: 7, of which 4 were waited for; matrix products, arithmetic and copies ran while one was open for 0% of the time, Pallas kernels for 15%

profile of v6, /device:TPU:1, one launch (start us, length us, event | category | flops | bytes accessed | tf_op | source)
XLA Modules:
  0.0 50.1 jit_solution(15848983192196894869)
XLA Ops:
  0.6 4.7 %column_solve.1 = (f32[2,50,32,128]{3,2,1,0:T(8,128)S(1)}, f32[3,32,128]{2,1,0:T(8,128)S(1)}, f32[24,8,128]{2,1,0:T(8,128)S(1)}, f32[25,8,128]{2,1,0:T(8,128)S(1...) custom-call(f32[2,50,32,128]{3,2,1,0:T(8,128)} %lam_h.1, ...), custom_call_target="tpu_custom_call" | custom-call | tf_op jit(solution)/shard_map/column_solve/pallas_call | solution.py:657
  5.3 1.5 %collective-permute-start.2 = (f32[78,8,128]{2,1,0:T(8,128)S(1)}, f32[78,8,128]{2,1,0:T(8,128)S(1)}, u32[]{:S(2)}, u32[]{:S(2)}) collective-permute-start(f32[78,8,128]{2,1,0:T(8,128)S(1)} %get-tuple-element.26), channel_id=1, source_target_pairs={{0,1},{1,0},{2,3},{3,2},{4,5},{5,4},{6,7},{7,6},{8,9},{9,8},{10,11... | collective-permute-start | bytes 958472 | tf_op jit(solution)/shard_map/ppermute | solution.py:686
  6.8 3.5 %collective-permute-start.3 = (f32[78,8,128]{2,1,0:T(8,128)S(1)}, f32[78,8,128]{2,1,0:T(8,128)S(1)}, u32[]{:S(2)}, u32[]{:S(2)}) collective-permute-start(f32[78,8,128]{2,1,0:T(8,128)S(1)} %get-tuple-element.27), channel_id=1, source_target_pairs={{1,2},{2,1},{3,4},{4,3},{5,6},{6,5},{9,10},{10,9},{11,12},{12,11},... | collective-permute-start | bytes 958472 | tf_op jit(solution)/shard_map/ppermute | solution.py:687
  10.3 5.0 %collective-permute-start.1 = (f32[25,8,128]{2,1,0:T(8,128)S(1)}, f32[25,8,128]{2,1,0:T(8,128)S(1)}, u32[]{:S(2)}, u32[]{:S(2)}) collective-permute-start(f32[25,8,128]{2,1,0:T(8,128)S(1)} %get-tuple-element.25), channel_id=1, source_target_pairs={{8,16},{16,8},{24,32},{32,24},{40,48},{48,40},{56,64},{64,56},{72,... | collective-permute-start | bytes 307208 | tf_op jit(solution)/shard_map/ppermute | solution.py:689
  15.3 0.0 collective-permute-start
  15.4 3.5 %collective-permute-done.o1_ref = f32[24,8,128]{2,1,0:T(8,128)S(1)} collective-permute-done((f32[24,8,128]{2,1,0:T(8,128)S(1)}, f32[24,8,128]{2,1,0:T(8,128)S(1)}, u32[]{:S(2)}, u32[]{:S(2)}) %collective-permute-start) | collective-permute-done | bytes 98336 | tf_op jit(solution)/shard_map/ppermute | solution.py:688
  18.8 0.0 collective-permute-done.1.o2_ref
  18.8 0.0 collective-permute-done.2.h1_ref
  18.8 0.0 collective-permute-done.3.h2_ref
  18.8 0.2 after_lon.1
  19.0 4.1 %collective-permute-start.5 = (f32[11,8,128]{2,1,0:T(8,128)S(1)}, f32[11,8,128]{2,1,0:T(8,128)S(1)}, u32[]{:S(2)}, u32[]{:S(2)}) collective-permute-start(f32[11,8,128]{2,1,0:T(8,128)S(1)} %get-tuple-element.33), channel_id=1, source_target_pairs={{1,2},{2,1},{3,4},{4,3},{5,6},{6,5},{9,10},{10,9},{11,12},{12,11},... | collective-permute-start | bytes 135176 | tf_op jit(solution)/shard_map/ppermute | solution.py:698
  23.1 0.1 collective-permute-start.4
  23.2 1.2 %collective-permute-done.4.lat1_ref.c1_ref = f32[10,8,128]{2,1,0:T(8,128)S(1)} collective-permute-done((f32[10,8,128]{2,1,0:T(8,128)S(1)}, f32[10,8,128]{2,1,0:T(8,128)S(1)}, u32[]{:S(2)}, u32[]{:S(2)}) %collective-permute-start.4) | collective-permute-done | bytes 40992 | tf_op jit(solution)/shard_map/ppermute | solution.py:697
  24.4 0.4 collective-permute-done.5.lat2_ref.c2_ref
  24.8 1.9 %krylov.1 = (f32[4,40,256]{2,1,0:T(8,128)S(1)}, f32[40,256]{1,0:T(8,128)S(1)}, f32[128,128]{1,0:T(8,128)}) custom-call(f32[3,32,256]{2,1,0:T(8,128)S(1)} %get-tuple-element.31.ext_ref, f32[10,8,128]{2,1,0:T(8,128)S(1)} %collective-permute-done.4.lat1_ref.c1_ref, f32[11,8,128]{2,1,0:T(8,128)S(1)} %collective-permute-done.5.lat2_ref.c2_ref), custom_call_target="tpu_custom_call" | custom-call | tf_op jit(solution)/shard_map/krylov/pallas_call | solution.py:657
  26.6 7.8 %all-to-all-start = ((f32[128,1,128]{2,1,0:T(1,128)}), f32[128,1,128]{2,1,0:T(1,128)S(1)}, u32[]{:S(2)}, u32[]{:S(2)}) async-start(f32[128,1,128]{2,1,0:T(1,128)} %bitcast.1), calls=%async_computation | async-start | bytes 131072 | tf_op jit(solution)/shard_map/all_to_all | solution.py:705
  34.5 7.6 %mixed_sweeps.1 = (f32[2,50,32,128]{3,2,1,0:T(8,128)S(1)}, f32[4,50,32,128]{3,2,1,0:T(8,128)}) custom-call(f32[40,256]{1,0:T(8,128)S(1)} %get-tuple-element.36.lev_ref, f32[2,6,2,32,128]{4,3,2,1,0:T(8,128)S(1)} %get-tuple-element.37.side_ref, f32[78,8,128]{2,1,0:T(8,128)S(1)} %collective-permute-done.2.h1_ref, ...), custom_call_target="tpu_custom_call", output_to_operand_aliasing={{0}: (6, {})} | custom-call | tf_op jit(solution)/shard_map/mixed_sweeps/pallas_call | solution.py:657
  42.1 1.7 %all-to-all-done = f32[128,1,128]{2,1,0:T(1,128)S(1)} async-done(((f32[128,1,128]{2,1,0:T(1,128)}), f32[128,1,128]{2,1,0:T(1,128)S(1)}, u32[]{:S(2)}, u32[]{:S(2)}) %all-to-all-start) | async-done | bytes 65568 | tf_op jit(solution)/shard_map/all_to_all | solution.py:705
  43.7 6.2 %sweeps.1 = (f32[2,50,32,128]{3,2,1,0:T(8,128)}, f32[2,50,32,128]{3,2,1,0:T(8,128)}, f32[32,128]{1,0:T(8,128)}) custom-call(f32[128,128]{1,0:T(8,128)S(1)} %bitcast.4, f32[4,40,256]{2,1,0:T(8,128)S(1)} %get-tuple-element.35.vec_ref, f32[40,256]{1,0:T(8,128)S(1)} %get-tuple-element.36.lev_ref, f32[2,6,2,32,128]{4,3,2,1,0:T(8,128)S(1)} %get-tuple-element.37.side_ref, ...), custom_call_target="tpu_custom_call" | custom-call | tf_op jit(solution)/shard_map/sweeps/pallas_call | solution.py:657
Async XLA Ops:
  5.3 13.5 %collective-permute-start.2 = (f32[78,8,128]{2,1,0:T(8,128)S(1)}, f32[78,8,128]{2,1,0:T(8,128)S(1)}, u32[]{:S(2)}, u32[]{:S(2)}) collective-permute-start(f32[78,8,128]{2,1,0:T(8,128)S(1)} %get-tuple-element.26), channel_id=1, source_target_pairs={{0,1},{1,0},{2,3},{3,2},{4,5},{5,4},{6,7},{7,6},{8,9},{9,8},{10,11... | collective-permute-start | bytes 958472 | tf_op jit(solution)/shard_map/ppermute | solution.py:686
  6.8 12.0 %collective-permute-start.3 = (f32[78,8,128]{2,1,0:T(8,128)S(1)}, f32[78,8,128]{2,1,0:T(8,128)S(1)}, u32[]{:S(2)}, u32[]{:S(2)}) collective-permute-start(f32[78,8,128]{2,1,0:T(8,128)S(1)} %get-tuple-element.27), channel_id=1, source_target_pairs={{1,2},{2,1},{3,4},{4,3},{5,6},{6,5},{9,10},{10,9},{11,12},{12,11},... | collective-permute-start | bytes 958472 | tf_op jit(solution)/shard_map/ppermute | solution.py:687
  10.3 8.5 %collective-permute-start.1 = (f32[25,8,128]{2,1,0:T(8,128)S(1)}, f32[25,8,128]{2,1,0:T(8,128)S(1)}, u32[]{:S(2)}, u32[]{:S(2)}) collective-permute-start(f32[25,8,128]{2,1,0:T(8,128)S(1)} %get-tuple-element.25), channel_id=1, source_target_pairs={{8,16},{16,8},{24,32},{32,24},{40,48},{48,40},{56,64},{64,56},{72,... | collective-permute-start | bytes 307208 | tf_op jit(solution)/shard_map/ppermute | solution.py:689
  15.3 3.5 %collective-permute-start = (f32[24,8,128]{2,1,0:T(8,128)S(1)}, f32[24,8,128]{2,1,0:T(8,128)S(1)}, u32[]{:S(2)}, u32[]{:S(2)}) collective-permute-start(f32[24,8,128]{2,1,0:T(8,128)S(1)} %get-tuple-element.24), channel_id=1, source_target_pairs={{0,8},{8,0},{16,24},{24,16},{32,40},{40,32},{48,56},{56,48},{64,72... | collective-permute-start | bytes 294920 | tf_op jit(solution)/shard_map/ppermute | solution.py:688
  19.0 5.8 %collective-permute-start.5 = (f32[11,8,128]{2,1,0:T(8,128)S(1)}, f32[11,8,128]{2,1,0:T(8,128)S(1)}, u32[]{:S(2)}, u32[]{:S(2)}) collective-permute-start(f32[11,8,128]{2,1,0:T(8,128)S(1)} %get-tuple-element.33), channel_id=1, source_target_pairs={{1,2},{2,1},{3,4},{4,3},{5,6},{6,5},{9,10},{10,9},{11,12},{12,11},... | collective-permute-start | bytes 135176 | tf_op jit(solution)/shard_map/ppermute | solution.py:698
  23.1 1.3 %collective-permute-start.4 = (f32[10,8,128]{2,1,0:T(8,128)S(1)}, f32[10,8,128]{2,1,0:T(8,128)S(1)}, u32[]{:S(2)}, u32[]{:S(2)}) collective-permute-start(f32[10,8,128]{2,1,0:T(8,128)S(1)} %get-tuple-element.32), channel_id=1, source_target_pairs={{0,1},{1,0},{2,3},{3,2},{4,5},{5,4},{6,7},{7,6},{8,9},{9,8},{10,11... | collective-permute-start | bytes 122888 | tf_op jit(solution)/shard_map/ppermute | solution.py:697
  26.6 17.1 %all-to-all-start = ((f32[128,1,128]{2,1,0:T(1,128)}), f32[128,1,128]{2,1,0:T(1,128)S(1)}, u32[]{:S(2)}, u32[]{:S(2)}) async-start(f32[128,1,128]{2,1,0:T(1,128)} %bitcast.1), calls=%async_computation | async-start | bytes 131072 | tf_op jit(solution)/shard_map/all_to_all | solution.py:705

commit v7 on v6

--- a/solution.py
+++ b/solution.py
@@ -170,6 +170,24 @@
     for c in rest:
         c.wait()
 
+    pair = iota((8, COLS), 0) // 2
+    sources = (mixed_ref, mixed_ref, vel, vel, tr, tr)
+
+    def edge_rows(i):
+        src = sources[i]
+        for g in range(GROUPS):
+            first = jnp.zeros((8, COLS), F32)
+            last = first
+            for q in range(min(4, LEVELS - 4 * g)):
+                top, end = src[i % 2, 4 * g + q, :8], src[i % 2, 4 * g + q, ROWS - 8 :]
+                first = jnp.where(pair == q, roll(top, 2 * q, 0) if q else top, first)
+                last = jnp.where(pair == (q + 3) % 4, roll(end, 2 * q, 0) if q else end, last)
+            g1_ref[i * GROUPS + g] = pick(lat_par, last, first)
+            g2_ref[i * GROUPS + g] = pick(lat_par, first, last)
+
+    for i in range(2, FIELDS):
+        edge_rows(i)
+
     lane = iota((ROWS, COLS), 1)
     slot = lane // 4
     begun = set()
@@ -228,17 +246,8 @@
     )
     lon2_ref[4 * LON_TILES] = jnp.zeros((8, COLS), F32)
 
-    pair = iota((8, COLS), 0) // 2
-    for i, src in enumerate((mixed_ref, mixed_ref, vel, vel, tr, tr)):
-        for g in range(GROUPS):
-            first = jnp.zeros((8, COLS), F32)
-            last = first
-            for q in range(min(4, LEVELS - 4 * g)):
-                top, end = src[i % 2, 4 * g + q, :8], src[i % 2, 4 * g + q, ROWS - 8 :]
-                first = jnp.where(pair == q, roll(top, 2 * q, 0) if q else top, first)
-                last = jnp.where(pair == (q + 3) % 4, roll(end, 2 * q, 0) if q else end, last)
-            g1_ref[i * GROUPS + g] = pick(lat_par, last, first)
-            g2_ref[i * GROUPS + g] = pick(lat_par, first, last)
+    for i in range(2):
+        edge_rows(i)
 
 
 CORNERS = 4

time: 50.2 us -> 50.2 us (level)
  no operation moved by 1% of the time
where the time goes in v7:
time: 50.2 us; the launch traced here: 50.1 us
  starting transfers between devices  22 us (44%)
  Pallas kernels  20.5 us (41%)
  waiting for transfers between devices  6.77 us (13%)
  between operations  0.86 us (2%)
    pallas_call x5, Pallas kernels, call(): pl.pallas_call(kernel, name=name, out_shape=tuple((o for o, _ in outs)),...  20.5 us
    all_to_all x1, starting transfers between devices, per_device(): gram = lax.all_to_all(gram, ('lon', 'lat'), 0, 0, tiled=True)  7.81 us
    ppermute x1, starting transfers between devices, per_device(): o2 = lax.ppermute(lon2, 'lon', swaps(lon, 1, True))  5.01 us
    ppermute x1, starting transfers between devices, per_device(): lat2 = lax.ppermute(lat2, 'lat', swaps(lat, 1, False))  4.06 us
    ppermute x1, starting transfers between devices, per_device(): h2 = lax.ppermute(g2, 'lat', swaps(lat, 1, False))  3.53 us
    ppermute x1, waiting for transfers between devices, per_device(): o1 = lax.ppermute(lon1, 'lon', swaps(lon, 0, True))  3.46 us
    all_to_all x1, waiting for transfers between devices, per_device(): gram = lax.all_to_all(gram, ('lon', 'lat'), 0, 0, tiled=True)  1.67 us
    ppermute x1, starting transfers between devices, per_device(): h1 = lax.ppermute(g1, 'lat', swaps(lat, 0, False))  1.5 us
  transfers between devices with their start and end apart: 7, of which 4 were waited for; matrix products, arithmetic and copies ran while one was open for 0% of the time, Pallas kernels for 15%

profile of v7, /device:TPU:1, one launch (start us, length us, event | category | flops | bytes accessed | tf_op | source)
XLA Modules:
  0.0 50.1 jit_solution(13829632540683729328)
XLA Ops:
  0.6 4.7 %column_solve.1 = (f32[2,50,32,128]{3,2,1,0:T(8,128)S(1)}, f32[3,32,128]{2,1,0:T(8,128)S(1)}, f32[24,8,128]{2,1,0:T(8,128)S(1)}, f32[25,8,128]{2,1,0:T(8,128)S(1...) custom-call(f32[2,50,32,128]{3,2,1,0:T(8,128)} %lam_h.1, ...), custom_call_target="tpu_custom_call" | custom-call | tf_op jit(solution)/shard_map/column_solve/pallas_call | solution.py:666
  5.3 1.5 %collective-permute-start.2 = (f32[78,8,128]{2,1,0:T(8,128)S(1)}, f32[78,8,128]{2,1,0:T(8,128)S(1)}, u32[]{:S(2)}, u32[]{:S(2)}) collective-permute-start(f32[78,8,128]{2,1,0:T(8,128)S(1)} %get-tuple-element.26), channel_id=1, source_target_pairs={{0,1},{1,0},{2,3},{3,2},{4,5},{5,4},{6,7},{7,6},{8,9},{9,8},{10,11... | collective-permute-start | bytes 958472 | tf_op jit(solution)/shard_map/ppermute | solution.py:695
  6.8 3.5 %collective-permute-start.3 = (f32[78,8,128]{2,1,0:T(8,128)S(1)}, f32[78,8,128]{2,1,0:T(8,128)S(1)}, u32[]{:S(2)}, u32[]{:S(2)}) collective-permute-start(f32[78,8,128]{2,1,0:T(8,128)S(1)} %get-tuple-element.27), channel_id=1, source_target_pairs={{1,2},{2,1},{3,4},{4,3},{5,6},{6,5},{9,10},{10,9},{11,12},{12,11},... | collective-permute-start | bytes 958472 | tf_op jit(solution)/shard_map/ppermute | solution.py:696
  10.3 5.0 %collective-permute-start.1 = (f32[25,8,128]{2,1,0:T(8,128)S(1)}, f32[25,8,128]{2,1,0:T(8,128)S(1)}, u32[]{:S(2)}, u32[]{:S(2)}) collective-permute-start(f32[25,8,128]{2,1,0:T(8,128)S(1)} %get-tuple-element.25), channel_id=1, source_target_pairs={{8,16},{16,8},{24,32},{32,24},{40,48},{48,40},{56,64},{64,56},{72,... | collective-permute-start | bytes 307208 | tf_op jit(solution)/shard_map/ppermute | solution.py:698
  15.3 0.0 collective-permute-start
  15.4 3.5 %collective-permute-done.o1_ref = f32[24,8,128]{2,1,0:T(8,128)S(1)} collective-permute-done((f32[24,8,128]{2,1,0:T(8,128)S(1)}, f32[24,8,128]{2,1,0:T(8,128)S(1)}, u32[]{:S(2)}, u32[]{:S(2)}) %collective-permute-start) | collective-permute-done | bytes 98336 | tf_op jit(solution)/shard_map/ppermute | solution.py:697
  18.8 0.0 collective-permute-done.1.o2_ref
  18.8 0.0 collective-permute-done.2.h1_ref
  18.8 0.0 collective-permute-done.3.h2_ref
  18.8 0.2 after_lon.1
  19.0 4.1 %collective-permute-start.5 = (f32[11,8,128]{2,1,0:T(8,128)S(1)}, f32[11,8,128]{2,1,0:T(8,128)S(1)}, u32[]{:S(2)}, u32[]{:S(2)}) collective-permute-start(f32[11,8,128]{2,1,0:T(8,128)S(1)} %get-tuple-element.33), channel_id=1, source_target_pairs={{1,2},{2,1},{3,4},{4,3},{5,6},{6,5},{9,10},{10,9},{11,12},{12,11},... | collective-permute-start | bytes 135176 | tf_op jit(solution)/shard_map/ppermute | solution.py:707
  23.1 0.1 collective-permute-start.4
  23.2 1.2 %collective-permute-done.4.lat1_ref.c1_ref = f32[10,8,128]{2,1,0:T(8,128)S(1)} collective-permute-done((f32[10,8,128]{2,1,0:T(8,128)S(1)}, f32[10,8,128]{2,1,0:T(8,128)S(1)}, u32[]{:S(2)}, u32[]{:S(2)}) %collective-permute-start.4) | collective-permute-done | bytes 40992 | tf_op jit(solution)/shard_map/ppermute | solution.py:706
  24.4 0.4 collective-permute-done.5.lat2_ref.c2_ref
  24.8 1.9 %krylov.1 = (f32[4,40,256]{2,1,0:T(8,128)S(1)}, f32[40,256]{1,0:T(8,128)S(1)}, f32[128,128]{1,0:T(8,128)}) custom-call(f32[3,32,256]{2,1,0:T(8,128)S(1)} %get-tuple-element.31.ext_ref, f32[10,8,128]{2,1,0:T(8,128)S(1)} %collective-permute-done.4.lat1_ref.c1_ref, f32[11,8,128]{2,1,0:T(8,128)S(1)} %collective-permute-done.5.lat2_ref.c2_ref), custom_call_target="tpu_custom_call" | custom-call | tf_op jit(solution)/shard_map/krylov/pallas_call | solution.py:666
  26.6 7.8 %all-to-all-start = ((f32[128,1,128]{2,1,0:T(1,128)}), f32[128,1,128]{2,1,0:T(1,128)S(1)}, u32[]{:S(2)}, u32[]{:S(2)}) async-start(f32[128,1,128]{2,1,0:T(1,128)} %bitcast.1), calls=%async_computation | async-start | bytes 131072 | tf_op jit(solution)/shard_map/all_to_all | solution.py:714
  34.5 7.6 %mixed_sweeps.1 = (f32[2,50,32,128]{3,2,1,0:T(8,128)S(1)}, f32[4,50,32,128]{3,2,1,0:T(8,128)}) custom-call(f32[40,256]{1,0:T(8,128)S(1)} %get-tuple-element.36.lev_ref, f32[2,6,2,32,128]{4,3,2,1,0:T(8,128)S(1)} %get-tuple-element.37.side_ref, f32[78,8,128]{2,1,0:T(8,128)S(1)} %collective-permute-done.2.h1_ref, ...), custom_call_target="tpu_custom_call", output_to_operand_aliasing={{0}: (6, {})} | custom-call | tf_op jit(solution)/shard_map/mixed_sweeps/pallas_call | solution.py:666
  42.1 1.7 %all-to-all-done = f32[128,1,128]{2,1,0:T(1,128)S(1)} async-done(((f32[128,1,128]{2,1,0:T(1,128)}), f32[128,1,128]{2,1,0:T(1,128)S(1)}, u32[]{:S(2)}, u32[]{:S(2)}) %all-to-all-start) | async-done | bytes 65568 | tf_op jit(solution)/shard_map/all_to_all | solution.py:714
  43.7 6.2 %sweeps.1 = (f32[2,50,32,128]{3,2,1,0:T(8,128)}, f32[2,50,32,128]{3,2,1,0:T(8,128)}, f32[32,128]{1,0:T(8,128)}) custom-call(f32[128,128]{1,0:T(8,128)S(1)} %bitcast.4, f32[4,40,256]{2,1,0:T(8,128)S(1)} %get-tuple-element.35.vec_ref, f32[40,256]{1,0:T(8,128)S(1)} %get-tuple-element.36.lev_ref, f32[2,6,2,32,128]{4,3,2,1,0:T(8,128)S(1)} %get-tuple-element.37.side_ref, ...), custom_call_target="tpu_custom_call" | custom-call | tf_op jit(solution)/shard_map/sweeps/pallas_call | solution.py:666
Async XLA Ops:
  5.3 13.5 %collective-permute-start.2 = (f32[78,8,128]{2,1,0:T(8,128)S(1)}, f32[78,8,128]{2,1,0:T(8,128)S(1)}, u32[]{:S(2)}, u32[]{:S(2)}) collective-permute-start(f32[78,8,128]{2,1,0:T(8,128)S(1)} %get-tuple-element.26), channel_id=1, source_target_pairs={{0,1},{1,0},{2,3},{3,2},{4,5},{5,4},{6,7},{7,6},{8,9},{9,8},{10,11... | collective-permute-start | bytes 958472 | tf_op jit(solution)/shard_map/ppermute | solution.py:695
  6.8 12.0 %collective-permute-start.3 = (f32[78,8,128]{2,1,0:T(8,128)S(1)}, f32[78,8,128]{2,1,0:T(8,128)S(1)}, u32[]{:S(2)}, u32[]{:S(2)}) collective-permute-start(f32[78,8,128]{2,1,0:T(8,128)S(1)} %get-tuple-element.27), channel_id=1, source_target_pairs={{1,2},{2,1},{3,4},{4,3},{5,6},{6,5},{9,10},{10,9},{11,12},{12,11},... | collective-permute-start | bytes 958472 | tf_op jit(solution)/shard_map/ppermute | solution.py:696
  10.3 8.5 %collective-permute-start.1 = (f32[25,8,128]{2,1,0:T(8,128)S(1)}, f32[25,8,128]{2,1,0:T(8,128)S(1)}, u32[]{:S(2)}, u32[]{:S(2)}) collective-permute-start(f32[25,8,128]{2,1,0:T(8,128)S(1)} %get-tuple-element.25), channel_id=1, source_target_pairs={{8,16},{16,8},{24,32},{32,24},{40,48},{48,40},{56,64},{64,56},{72,... | collective-permute-start | bytes 307208 | tf_op jit(solution)/shard_map/ppermute | solution.py:698
  15.3 3.5 %collective-permute-start = (f32[24,8,128]{2,1,0:T(8,128)S(1)}, f32[24,8,128]{2,1,0:T(8,128)S(1)}, u32[]{:S(2)}, u32[]{:S(2)}) collective-permute-start(f32[24,8,128]{2,1,0:T(8,128)S(1)} %get-tuple-element.24), channel_id=1, source_target_pairs={{0,8},{8,0},{16,24},{24,16},{32,40},{40,32},{48,56},{56,48},{64,72... | collective-permute-start | bytes 294920 | tf_op jit(solution)/shard_map/ppermute | solution.py:697
  19.0 5.8 %collective-permute-start.5 = (f32[11,8,128]{2,1,0:T(8,128)S(1)}, f32[11,8,128]{2,1,0:T(8,128)S(1)}, u32[]{:S(2)}, u32[]{:S(2)}) collective-permute-start(f32[11,8,128]{2,1,0:T(8,128)S(1)} %get-tuple-element.33), channel_id=1, source_target_pairs={{1,2},{2,1},{3,4},{4,3},{5,6},{6,5},{9,10},{10,9},{11,12},{12,11},... | collective-permute-start | bytes 135176 | tf_op jit(solution)/shard_map/ppermute | solution.py:707
  23.1 1.3 %collective-permute-start.4 = (f32[10,8,128]{2,1,0:T(8,128)S(1)}, f32[10,8,128]{2,1,0:T(8,128)S(1)}, u32[]{:S(2)}, u32[]{:S(2)}) collective-permute-start(f32[10,8,128]{2,1,0:T(8,128)S(1)} %get-tuple-element.32), channel_id=1, source_target_pairs={{0,1},{1,0},{2,3},{3,2},{4,5},{5,4},{6,7},{7,6},{8,9},{9,8},{10,11... | collective-permute-start | bytes 122888 | tf_op jit(solution)/shard_map/ppermute | solution.py:706
  26.6 17.1 %all-to-all-start = ((f32[128,1,128]{2,1,0:T(1,128)}), f32[128,1,128]{2,1,0:T(1,128)S(1)}, u32[]{:S(2)}, u32[]{:S(2)}) async-start(f32[128,1,128]{2,1,0:T(1,128)} %bitcast.1), calls=%async_computation | async-start | bytes 131072 | tf_op jit(solution)/shard_map/all_to_all | solution.py:714
